TPU v7x, 32 devices: a whole 2x2x4 slice. The times are simulated.
32 devices in a mesh: gx: 4 (over z), gy: 8 (over y, x, core).
Axes of the slice: x: 2, y: 2, z: 4, core: 2. Of those that a mesh axis runs over, the one named last changes fastest.
Arguments:
- media_features: bfloat16 [64, 256, 1536], P(('gx', 'gy')), may hold values from -6 to 6
- latents: bfloat16 [64, 64, 1536], P(('gx', 'gy')), may hold values from -6 to 6
- cotangent: bfloat16 [64, 64, 1536], P(('gx', 'gy')), may hold values from -6 to 6
- image_counts: int32 [32], P(('gx', 'gy')), may hold values from 1 to 2, 48 in all
- w_query: bfloat16 [1536, 1536], P(('gx', 'gy')), may hold values from -0.15625 to 0.15625
- w_key: bfloat16 [1536, 1536], P(('gx', 'gy')), may hold values from -0.15625 to 0.15625
- w_value: bfloat16 [1536, 1536], P(('gx', 'gy')), may hold values from -0.15625 to 0.15625
- w_out: bfloat16 [1536, 1536], P(None, ('gx', 'gy')), may hold values from -0.625 to 0.625
- w_up: bfloat16 [1536, 6144], P(('gx', 'gy')), may hold values from -0.15625 to 0.15625
- w_down: bfloat16 [6144, 1536], P(None, ('gx', 'gy')), may hold values from -0.078125 to 0.078125
- norm_gains: float32 [3, 1536], P(None, ('gx', 'gy')), may hold values from 0.1 to 1.9
- norm_biases: float32 [3, 1536], P(None, ('gx', 'gy')), may hold values from -2 to 2
Outputs:
- latents_out: bfloat16 [64, 64, 1536], P(('gx', 'gy'))
- grad_media: float32 [64, 256, 1536], P(('gx', 'gy'))
- grad_latents: float32 [64, 64, 1536], P(('gx', 'gy'))
- grad_w_query: float32 [1536, 1536], P(('gx', 'gy'))
- grad_w_key: float32 [1536, 1536], P(('gx', 'gy'))
- grad_w_value: float32 [1536, 1536], P(('gx', 'gy'))
- grad_w_out: float32 [1536, 1536], P(None, ('gx', 'gy'))
- grad_w_up: float32 [1536, 6144], P(('gx', 'gy'))
- grad_w_down: float32 [6144, 1536], P(None, ('gx', 'gy'))
- grad_norm_gains: float32 [3, 1536], P(None, ('gx', 'gy'))
- grad_norm_biases: float32 [3, 1536], P(None, ('gx', 'gy'))
Inputs may be any that keep to these rules, and one draw needn't show every extreme that they name: image_counts[d] is the number of images of the sequence held by device d (index d of gx+gy); they fill the first image_counts[d] slots of that device, the other slots hold unused data. The counts sum to 48 and some device is full.
All inputs are finite; a program needn't handle non-finite values.
Results may differ from a plain program's by a relative error of at most 0.033.
Values may be sent and summed in bfloat16 or wider, within the bound.
No kernel may reach another device: no remote copies, remote signals or barrier semaphores. Data moves between devices by JAX's collectives and lax.ppermute only.
A program may use at most 320 MiB of HBM per device.

v0:
```python
import jax
import jax.numpy as jnp
from jax import lax
from jax.sharding import PartitionSpec as P

HEAD = 96


EPSILON = 1e-05


def product(left, right):
    return jnp.dot(left, right, preferred_element_type=jnp.float32)


def product_left(left, right):
    return lax.dot_general(
        left, right, (((0,), (0,)), ((), ())), preferred_element_type=jnp.float32
    )


def product_right(left, right):
    return lax.dot_general(
        left, right, (((1,), (1,)), ((), ())), preferred_element_type=jnp.float32
    )


def layer_norm(rows, gain_row, bias_row):
    average = jnp.mean(rows, axis=-1, keepdims=True)
    centred = rows - average
    spread = jnp.mean(centred * centred, axis=-1, keepdims=True)
    return centred * lax.rsqrt(spread + EPSILON) * gain_row + bias_row


def gelu_exact(values):
    return jax.nn.gelu(values, approximate=False)


def head_plan(
    media_features,
    latents,
    cotangent,
    image_counts,
    w_query,
    w_key,
    w_value,
    w_out,
    w_up,
    w_down,
    norm_gains,
    norm_biases,
):
    query_scale = HEAD ** (-0.5)
    img_count = latents.shape[0]
    lat_count = latents.shape[1]
    patch_count = media_features.shape[1]
    width = latents.shape[2]
    total_rows = patch_count + lat_count
    weight_parts = (
        lax.all_to_all(w_query, "gy", split_axis=1, concat_axis=0, tiled=True),
        lax.all_to_all(w_key, "gy", split_axis=1, concat_axis=0, tiled=True),
        lax.all_to_all(w_value, "gy", split_axis=1, concat_axis=0, tiled=True),
        lax.all_to_all(w_out.T, "gy", split_axis=1, concat_axis=0, tiled=True),
        lax.all_to_all(w_up, "gy", split_axis=1, concat_axis=0, tiled=True),
        lax.all_to_all(w_down.T, "gy", split_axis=1, concat_axis=0, tiled=True),
    )
    query_cols, key_cols, value_cols, out_cols, up_cols, down_cols = (
        lax.all_gather(weight_parts[0], "gx", axis=0, tiled=True),
        lax.all_gather(weight_parts[1], "gx", axis=0, tiled=True),
        lax.all_gather(weight_parts[2], "gx", axis=0, tiled=True),
        lax.all_gather(weight_parts[3], "gx", axis=0, tiled=True),
        lax.all_gather(weight_parts[4], "gx", axis=0, tiled=True),
        lax.all_gather(weight_parts[5], "gx", axis=0, tiled=True),
    )
    gains, biases = (
        lax.all_gather(norm_gains, ("gx", "gy"), axis=1, tiled=True),
        lax.all_gather(norm_biases, ("gx", "gy"), axis=1, tiled=True),
    )
    live_mask = (jnp.arange(img_count, dtype=jnp.int32) < image_counts[0]).astype(jnp.float32)
    media_float = media_features.astype(jnp.float32)
    latent_float = latents.astype(jnp.float32)
    media_norm = layer_norm(media_float, gains[0], biases[0]).astype(jnp.bfloat16)
    latent_norm = layer_norm(latent_float, gains[1], biases[1]).astype(jnp.bfloat16)
    joined_own = jnp.concatenate([media_norm, latent_norm], axis=1)
    cot_own = (cotangent.astype(jnp.float32) * live_mask[:, None, None]).astype(jnp.bfloat16)
    joined_all, cot_all = (
        lax.all_gather(joined_own, "gy", axis=0, tiled=True),
        lax.all_gather(cot_own, "gy", axis=0, tiled=True),
    )
    group_count = joined_all.shape[0]
    head_width = query_cols.shape[1]
    head_count = head_width // HEAD
    ff_width = up_cols.shape[1]
    joined_flat = joined_all.reshape(group_count * total_rows, width)
    latent_flat = joined_all[:, patch_count:].reshape(group_count * lat_count, width)
    query = (product(latent_flat, query_cols) * query_scale).astype(jnp.bfloat16)
    query = query.reshape(group_count, lat_count, head_count, HEAD)
    key_heads = (
        product(joined_flat, key_cols)
        .astype(jnp.bfloat16)
        .reshape(group_count, total_rows, head_count, HEAD)
    )
    value_heads = (
        product(joined_flat, value_cols)
        .astype(jnp.bfloat16)
        .reshape(group_count, total_rows, head_count, HEAD)
    )
    scores = jnp.einsum("gqhd,gkhd->ghqk", query, key_heads, preferred_element_type=jnp.float32)
    probs = jax.nn.softmax(scores, axis=-1)
    probs_low = probs.astype(jnp.bfloat16)
    mixed = jnp.einsum(
        "ghqk,gkhd->gqhd", probs_low, value_heads, preferred_element_type=jnp.float32
    )
    mixed = mixed.reshape(group_count * lat_count, head_width).astype(jnp.bfloat16)
    mixed_rows = mixed.reshape(group_count, lat_count, head_width)
    piece = mixed_rows
    piece = piece.reshape(img_count * lax.axis_size("gy") * lat_count, head_width)
    attended_own = (
        lax.psum_scatter(
            product_right(piece, out_cols)
            .reshape(img_count * lax.axis_size("gy"), lat_count, width)
            .astype(jnp.bfloat16),
            "gy",
            scatter_dimension=0,
            tiled=True,
        ).astype(jnp.float32)
        + latent_float
    )
    attended_all = lax.all_gather(
        attended_own.astype(jnp.bfloat16), "gy", axis=0, tiled=True
    ).astype(attended_own.dtype)
    hidden_all = layer_norm(attended_all, gains[2], biases[2]).astype(jnp.bfloat16)
    hidden_flat = hidden_all.reshape(group_count * lat_count, width)
    upper = product(hidden_flat, up_cols)
    active = gelu_exact(upper).astype(jnp.bfloat16)
    active_rows = active.reshape(group_count, lat_count, ff_width)
    piece = active_rows
    piece = piece.reshape(img_count * lax.axis_size("gy") * lat_count, ff_width)
    ffn_own = lax.psum_scatter(
        product_right(piece, down_cols)
        .reshape(img_count * lax.axis_size("gy"), lat_count, width)
        .astype(jnp.bfloat16),
        "gy",
        scatter_dimension=0,
        tiled=True,
    ).astype(jnp.float32)
    result = attended_own + ffn_own
    outputs = (result * live_mask[:, None, None]).astype(jnp.bfloat16)
    cot_flat = cot_all.reshape(group_count * lat_count, width)
    grad_down = product_left(cot_flat, active)
    grad_active = product(cot_flat, down_cols)
    unused, gelu_back = jax.vjp(gelu_exact, upper)
    grad_upper = gelu_back(grad_active)[0].astype(jnp.bfloat16)
    grad_up = product_left(hidden_flat, grad_upper)
    upper_rows = grad_upper.reshape(group_count, lat_count, ff_width)
    piece = upper_rows
    piece = piece.reshape(img_count * lax.axis_size("gy") * lat_count, ff_width)
    grad_hidden = lax.psum_scatter(
        product_right(piece, up_cols)
        .reshape(img_count * lax.axis_size("gy"), lat_count, width)
        .astype(jnp.bfloat16),
        "gy",
        scatter_dimension=0,
        tiled=True,
    ).astype(jnp.float32)
    unused, ffn_norm_back = jax.vjp(layer_norm, attended_own, gains[2], biases[2])
    grad_norm_input, gain_two, bias_two = ffn_norm_back(grad_hidden)
    grad_attended = cot_own.astype(jnp.float32) + grad_norm_input
    grad_branch = grad_attended.astype(jnp.bfloat16)
    branch_all = lax.all_gather(grad_branch, "gy", axis=0, tiled=True)
    branch_flat = branch_all.reshape(group_count * lat_count, width)
    grad_out = product_left(branch_flat, mixed)
    grad_mixed = product(branch_flat, out_cols).astype(jnp.bfloat16)
    grad_mixed = grad_mixed.reshape(group_count, lat_count, head_count, HEAD)
    grad_values = jnp.einsum(
        "ghqk,gqhd->gkhd", probs_low, grad_mixed, preferred_element_type=jnp.float32
    )
    grad_values = grad_values.astype(jnp.bfloat16).reshape(group_count, total_rows, head_width)
    grad_probs = jnp.einsum(
        "gqhd,gkhd->ghqk", grad_mixed, value_heads, preferred_element_type=jnp.float32
    )
    inner_sums = jnp.sum(grad_probs * probs, axis=-1, keepdims=True)
    grad_scores = (probs * (grad_probs - inner_sums)).astype(jnp.bfloat16)
    grad_query = jnp.einsum(
        "ghqk,gkhd->gqhd", grad_scores, key_heads, preferred_element_type=jnp.float32
    )
    grad_query = grad_query.astype(jnp.bfloat16).reshape(group_count, lat_count, head_width)
    grad_keys = jnp.einsum(
        "ghqk,gqhd->gkhd", grad_scores, query, preferred_element_type=jnp.float32
    )
    grad_keys = grad_keys.astype(jnp.bfloat16).reshape(group_count, total_rows, head_width)
    grad_query_cols = (
        product_left(latent_flat, grad_query.reshape(group_count * lat_count, head_width))
        * query_scale
    )
    grad_key_cols = product_left(
        joined_flat, grad_keys.reshape(group_count * total_rows, head_width)
    )
    grad_value_cols = product_left(
        joined_flat, grad_values.reshape(group_count * total_rows, head_width)
    )
    row_count = img_count * lax.axis_size("gy")
    keys_piece = grad_keys.reshape(row_count * total_rows, head_width)
    values_piece = grad_values.reshape(row_count * total_rows, head_width)
    query_piece = grad_query.reshape(row_count * lat_count, head_width)
    both = product_right(keys_piece, key_cols) + product_right(values_piece, value_cols)
    both = both.reshape(row_count, total_rows, width)
    extra = (product_right(query_piece, query_cols) * query_scale).reshape(
        row_count, lat_count, width
    )
    grad_joined = lax.psum_scatter(
        jnp.concatenate([both[:, :patch_count], both[:, patch_count:] + extra], axis=1).astype(
            jnp.bfloat16
        ),
        "gy",
        scatter_dimension=0,
        tiled=True,
    ).astype(jnp.float32)
    unused, media_norm_back = jax.vjp(layer_norm, media_float, gains[0], biases[0])
    grad_media, gain_zero, bias_zero = media_norm_back(grad_joined[:, :patch_count])
    unused, latent_norm_back = jax.vjp(layer_norm, latent_float, gains[1], biases[1])
    grad_latent_input, gain_one, bias_one = latent_norm_back(grad_joined[:, patch_count:])
    grad_latents = grad_attended + grad_latent_input
    grad_gains = jnp.stack([gain_zero, gain_one, gain_two], axis=0)
    grad_biases = jnp.stack([bias_zero, bias_one, bias_two], axis=0)
    norm_sums = (
        lax.psum_scatter(grad_gains, ("gx", "gy"), scatter_dimension=1, tiled=True),
        lax.psum_scatter(grad_biases, ("gx", "gy"), scatter_dimension=1, tiled=True),
    )
    column_sums = (
        lax.psum_scatter(
            grad_query_cols.astype(jnp.bfloat16), "gx", scatter_dimension=0, tiled=True
        ).astype(jnp.float32),
        lax.psum_scatter(
            grad_key_cols.astype(jnp.bfloat16), "gx", scatter_dimension=0, tiled=True
        ).astype(jnp.float32),
        lax.psum_scatter(
            grad_value_cols.astype(jnp.bfloat16), "gx", scatter_dimension=0, tiled=True
        ).astype(jnp.float32),
        lax.psum_scatter(
            grad_out.astype(jnp.bfloat16), "gx", scatter_dimension=0, tiled=True
        ).astype(jnp.float32),
        lax.psum_scatter(
            grad_up.astype(jnp.bfloat16), "gx", scatter_dimension=0, tiled=True
        ).astype(jnp.float32),
        lax.psum_scatter(
            grad_down.astype(jnp.bfloat16), "gx", scatter_dimension=0, tiled=True
        ).astype(jnp.float32),
    )
    shares = (
        lax.all_to_all(
            column_sums[0].astype(jnp.bfloat16), "gy", split_axis=0, concat_axis=1, tiled=True
        ).astype(jnp.float32),
        lax.all_to_all(
            column_sums[1].astype(jnp.bfloat16), "gy", split_axis=0, concat_axis=1, tiled=True
        ).astype(jnp.float32),
        lax.all_to_all(
            column_sums[2].astype(jnp.bfloat16), "gy", split_axis=0, concat_axis=1, tiled=True
        ).astype(jnp.float32),
        lax.all_to_all(
            column_sums[3].astype(jnp.bfloat16), "gy", split_axis=0, concat_axis=1, tiled=True
        ).astype(jnp.float32),
        lax.all_to_all(
            column_sums[4].astype(jnp.bfloat16), "gy", split_axis=0, concat_axis=1, tiled=True
        ).astype(jnp.float32),
        lax.all_to_all(
            column_sums[5].astype(jnp.bfloat16), "gy", split_axis=0, concat_axis=1, tiled=True
        ).astype(jnp.float32),
    )
    return (
        outputs,
        grad_media,
        grad_latents,
        shares[0],
        shares[1],
        shares[2],
        shares[3].T,
        shares[4],
        shares[5].T,
        norm_sums[0],
        norm_sums[1],
    )


def local(
    media_features,
    latents,
    cotangent,
    image_counts,
    w_query,
    w_key,
    w_value,
    w_out,
    w_up,
    w_down,
    norm_gains,
    norm_biases,
):
    return head_plan(
        media_features,
        latents,
        cotangent,
        image_counts,
        w_query,
        w_key,
        w_value,
        w_out,
        w_up,
        w_down,
        norm_gains,
        norm_biases,
    )


def solution(mesh):
    return jax.shard_map(
        local,
        mesh=mesh,
        in_specs=(
            P(("gx", "gy"), None, None),
            P(("gx", "gy"), None, None),
            P(("gx", "gy"), None, None),
            P(("gx", "gy")),
            P(("gx", "gy"), None),
            P(("gx", "gy"), None),
            P(("gx", "gy"), None),
            P(None, ("gx", "gy")),
            P(("gx", "gy"), None),
            P(None, ("gx", "gy")),
            P(None, ("gx", "gy")),
            P(None, ("gx", "gy")),
        ),
        out_specs=(
            P(("gx", "gy"), None, None),
            P(("gx", "gy"), None, None),
            P(("gx", "gy"), None, None),
            P(("gx", "gy"), None),
            P(("gx", "gy"), None),
            P(("gx", "gy"), None),
            P(None, ("gx", "gy")),
            P(("gx", "gy"), None),
            P(None, ("gx", "gy")),
            P(None, ("gx", "gy")),
            P(None, ("gx", "gy")),
        ),
        check_vma=False,
    )
```

profile of v0, /device:TPU:0, one launch (start us, length us, event | category | flops | bytes accessed | tf_op | source)
XLA Modules:
  0.0 1144.2 jit_solution(5422500293734798480)
XLA Ops:
  12.7 43.4 %all-gather = f32[32,48,3]{1,2,0:T(4,128)S(1)} all-gather(f32[1,48,3]{1,2,0:T(4,128)S(1)} %bitcast.191), channel_id=1, replica_groups=mesh['gx'=4,'gy'=8] {'gx','gy'}, dimensions={0}, use_global_device_ids=true | all-gather | bytes 19008 | tf_op jit(solution)/shard_map/all_gather | solution.py:76
  56.2 36.8 %all-gather.1 = f32[32,48,3]{1,2,0:T(4,128)S(1)} all-gather(f32[1,48,3]{1,2,0:T(4,128)S(1)} %bitcast.192), channel_id=1, replica_groups=mesh['gx'=4,'gy'=8] {'gx','gy'}, dimensions={0}, use_global_device_ids=true | all-gather | bytes 19008 | tf_op jit(solution)/shard_map/all_gather | solution.py:77
  96.6 3.4 all-to-all-start.3
  102.8 4.1 all-to-all-done.3
  106.9 3.4 all-to-all-start
  110.4 16.9 %all_gather.42 = bf16[1536,192]{0,1:T(8,128)(2,1)S(1)} all-gather(bf16[384,192]{0,1:T(8,128)(2,1)S(1)} %copy.111), channel_id=1, replica_groups=mesh['gx'=4,'gy'=8] {'gx'}, dimensions={0}, use_global_device_ids=true | all-gather | bytes 737280 | tf_op jit(solution)/shard_map/all_gather | solution.py:71
  127.3 3.9 all-to-all-start.2
  131.3 17.9 %all_gather.39 = bf16[1536,192]{1,0:T(8,128)(2,1)S(1)} all-gather(bf16[384,192]{1,0:T(8,128)(2,1)S(1)} %bitcast.170), channel_id=1, replica_groups=mesh['gx'=4,'gy'=8] {'gx'}, dimensions={0}, use_global_device_ids=true | all-gather | bytes 737280 | tf_op jit(solution)/shard_map/all_gather | solution.py:70
  149.2 3.8 all-to-all-start.1
  153.1 18.4 %all_gather.41 = bf16[1536,192]{1,0:T(8,128)(2,1)S(1)} all-gather(bf16[384,192]{1,0:T(8,128)(2,1)S(1)} %bitcast.171), channel_id=1, replica_groups=mesh['gx'=4,'gy'=8] {'gx'}, dimensions={0}, use_global_device_ids=true | all-gather | bytes 737280 | tf_op jit(solution)/shard_map/all_gather | solution.py:69
  172.4 18.5 %all_gather.40 = bf16[1536,192]{1,0:T(8,128)(2,1)S(1)} all-gather(bf16[384,192]{1,0:T(8,128)(2,1)} %bitcast.172), channel_id=1, replica_groups=mesh['gx'=4,'gy'=8] {'gx'}, dimensions={0}, use_global_device_ids=true | all-gather | bytes 737280 | tf_op jit(solution)/shard_map/all_gather | solution.py:68
  190.9 12.0 %convolution_convert_fusion = bf16[5120,192]{0,1:T(8,128)(2,1)} fusion(bf16[5120,1536]{1,0:T(8,128)(2,1)} %bitcast.173, bf16[1536,192]{1,0:T(8,128)(2,1)S(1)} %all_gather.41), kind=kOutput, calls=%fused_computation.14 | convolution fusion | flops 3020881920 | bytes 18284544 | tf_op jit(solution)/shard_map/dot_general | solution.py:13
  202.9 4.9 reshape.239
  207.8 12.0 %convolution_convert_fusion.1 = bf16[5120,192]{0,1:T(8,128)(2,1)} fusion(bf16[5120,1536]{1,0:T(8,128)(2,1)} %bitcast.174, bf16[1536,192]{1,0:T(8,128)(2,1)S(1)} %all_gather.39), kind=kOutput, calls=%fused_computation.15 | convolution fusion | flops 3020881920 | bytes 18284544 | tf_op jit(solution)/shard_map/dot_general | solution.py:13
  219.8 4.8 reshape.236
  230.8 4.8 fusion.78
  235.6 3.9 fusion.41
  241.1 3.7 convolution_convert_fusion.2
  244.9 46.2 %reduce-scatter.25.cloned.1.call-done = bf16[2,64,1536]{2,1,0:T(8,128)(2,1)} async-done(((bf16[16,64,1536]{2,1,0:T(8,128)(2,1)}), bf16[2,64,1536]{2,1,0:T(8,128)(2,1)}) %reduce-scatter.25.cloned.1.call-update) | async-done | bytes 393232 | tf_op jit(solution)/shard_map/reduce_scatter | solution.py:119
  294.2 16.7 %all_to_all.192 = bf16[48,8,768]{2,0,1:T(8,128)(2,1)} all-to-all(bf16[48,8,768]{2,0,1:T(8,128)(2,1)S(1)} %bitcast.165), channel_id=1, replica_groups=mesh['gx'=4,'gy'=8] {'gy'}, dimensions={1} | all-to-all | bytes 1179648 | tf_op jit(solution)/shard_map/all_to_all | solution.py:64
  312.1 19.9 %all_to_all.193 = bf16[48,8,768]{2,0,1:T(8,128)(2,1)} all-to-all(bf16[48,8,768]{2,0,1:T(8,128)(2,1)S(1)} %bitcast.166), channel_id=1, replica_groups=mesh['gx'=4,'gy'=8] {'gy'}, dimensions={1} | all-to-all | bytes 1179648 | tf_op jit(solution)/shard_map/all_to_all | solution.py:65
  341.1 45.7 %all-gather.13.cloned.1.call-done = bf16[1536,768]{1,0:T(8,128)(2,1)} async-done(((bf16[384,768]{1,0:T(8,128)(2,1)}), bf16[1536,768]{1,0:T(8,128)(2,1)}) %all-gather.13.cloned.1.call-update) | async-done | bytes 2359312 | tf_op jit(solution)/shard_map/all_gather | solution.py:72
  386.7 6.9 fusion.81
  393.6 44.0 %all-gather.15.cloned.1.call-done = bf16[1536,768]{1,0:T(8,128)(2,1)} async-done(((bf16[384,768]{1,0:T(8,128)(2,1)}), bf16[1536,768]{1,0:T(8,128)(2,1)}) %all-gather.15.cloned.1.call-update) | async-done | bytes 2359312 | tf_op jit(solution)/shard_map/all_gather | solution.py:73
  437.6 33.1 %all-gather.17.cloned.1.call-done = bf16[16,64,1536]{2,1,0:T(8,128)(2,1)} async-done(((bf16[2,64,1536]{2,1,0:T(8,128)(2,1)}), bf16[16,64,1536]{2,1,0:T(8,128)(2,1)}) %all-gather.17.cloned.1.call-update) | async-done | bytes 3145744 | tf_op jit(solution)/shard_map/all_gather | solution.py:88
  470.6 13.2 %add_convert_fusion = (bf16[1024,768]{1,0:T(8,128)(2,1)S(1)}, f32[1024,768]{1,0:T(8,128)}) fusion(f32[1024,768]{1,0:T(8,128)} %fusion.81, bf16[1024,1536]{1,0:T(8,128)(2,1)} %bitcast.193, bf16[1536,768]{1,0:T(8,128)(2,1)} %all-gather.15.cloned.1.call-done), kind=kOutput, calls=%fused_computation.40 | convolution fusion | flops 2472542208 | bytes 13369344 | tf_op jit(solution)/shard_map/dot_general | solution.py:13
  483.8 4.1 convolution_convert_fusion.3
  488.0 46.4 %reduce-scatter.29.cloned.1.call-done = bf16[2,64,1536]{2,1,0:T(8,128)(2,1)} async-done(((bf16[16,64,1536]{2,1,0:T(8,128)(2,1)}), bf16[2,64,1536]{2,1,0:T(8,128)(2,1)}) %reduce-scatter.29.cloned.1.call-update) | async-done | bytes 393232 | tf_op jit(solution)/shard_map/reduce_scatter | solution.py:158
  539.9 3.4 multiply_convert_fusion.1
  544.4 3.9 convolution_convert_fusion.5
  548.5 6.4 convolution_convert_fusion.6
  556.1 15.8 %all-gather.19.cloned.1.call-done = bf16[16,64,1536]{2,1,0:T(8,128)(2,1)} async-done(((bf16[2,64,1536]{2,1,0:T(8,128)(2,1)}), bf16[16,64,1536]{2,1,0:T(8,128)(2,1)}) %all-gather.19.cloned.1.call-update) | async-done | bytes 3145744 | tf_op jit(solution)/shard_map/all_gather | solution.py:170
  571.8 3.6 convolution_convert_fusion.7
  577.7 3.2 convolution_convert_fusion.10
  589.7 4.9 reshape_reshape.13
  594.6 4.4 multiply_reduce_fusion
  604.6 3.5 fusion.25
  615.4 4.8 reshape_reshape.12
  620.4 17.0 %fusion.82 = f32[5120,1536]{1,0:T(8,128)} fusion(bf16[5120,192]{0,1:T(8,128)(2,1)} %reshape_reshape.12, bf16[1536,192]{1,0:T(8,128)(2,1)} %copy-done.15), kind=kOutput, calls=%fused_computation.157 | convolution fusion | flops 3019898880 | bytes 34013184 | tf_op jit(solution)/shard_map/dot_general | solution.py:23
  637.5 24.3 %convolution_add_fusion = f32[5120,1536]{1,0:T(8,128)} fusion(f32[5120,1536]{1,0:T(8,128)} %fusion.82, bf16[5120,192]{0,1:T(8,128)(2,1)} %reshape_reshape.13, bf16[1536,192]{1,0:T(8,128)(2,1)S(1)} %copy-done.14), kind=kOutput, calls=%fused_computation.2 | convolution fusion | flops 3027763200 | bytes 65470464 | tf_op jit(solution)/shard_map/dot_general | solution.py:23
  661.8 7.4 convolution_convert_fusion.8
  670.5 9.3 convolution_convert_fusion.9
  681.0 3.8 convolution_multiply_fusion
  685.0 5.7 fusion.7
  690.8 9.4 slice.85
  700.2 6.4 pad_maximum_fusion
  706.7 3.5 all-to-all-start.11
  710.3 6.5 convolution_convert_fusion.4
  716.8 3.8 all-to-all-done.11
  720.6 4.2 all-to-all-start.10
  726.0 9.3 all-to-all-done.10
  735.3 3.4 all-to-all-start.9
  744.8 3.4 all-to-all-start.6
  749.4 5.0 all-to-all-done.6
  754.4 3.4 all-to-all-start.8
  758.9 13.7 %reduce-scatter.39.cloned.1.call-done = bf16[384,192]{1,0:T(8,128)(2,1)} async-done(((bf16[1536,192]{1,0:T(8,128)(2,1)}), bf16[384,192]{1,0:T(8,128)(2,1)}) %reduce-scatter.39.cloned.1.call-update) | async-done | bytes 147472 | tf_op jit(solution)/shard_map/reduce_scatter | solution.py:234
  772.6 3.7 all-to-all-start.7
  777.4 5.1 all-to-all-done.7
  783.7 100.7 %reduce-scatter.31.cloned.1.call-done = bf16[2,320,1536]{2,1,0:T(8,128)(2,1)} async-done(((bf16[16,320,1536]{2,1,0:T(8,128)(2,1)}), bf16[2,320,1536]{2,1,0:T(8,128)(2,1)}) %reduce-scatter.31.cloned.1.call-update) | async-done | bytes 1966096 | tf_op jit(solution)/shard_map/reduce_scatter | solution.py:211
  891.2 4.6 broadcast_add_fusion
  897.2 36.7 %reduce-scatter.27.cloned.1.call-done = bf16[2,64,1536]{2,1,0:T(8,128)(2,1)} async-done(((bf16[16,64,1536]{2,1,0:T(8,128)(2,1)}), bf16[2,64,1536]{2,1,0:T(8,128)(2,1)}) %reduce-scatter.27.cloned.1.call-update) | async-done | bytes 393232 | tf_op jit(solution)/shard_map/reduce_scatter | solution.py:139
  933.9 2.9 add_add_fusion.3
  936.8 98.5 %reduce-scatter.47.cloned.1.call-done = f32[48,3]{1,0:T(8,128)} async-done(((f32[1536,3]{1,0:T(8,128)}), f32[48,3]{1,0:T(8,128)}) %reduce-scatter.47.cloned.1.call-update) | async-done | bytes 592
  1036.6 98.9 %reduce-scatter.45.cloned.1.call-done = f32[48,3]{1,0:T(8,128)} async-done(((f32[1536,3]{1,0:T(8,128)}), f32[48,3]{1,0:T(8,128)}) %reduce-scatter.45.cloned.1.call-update) | async-done | bytes 592
  (238 shorter events, 90.9 us)
Async XLA Ops:
  7.2 86.0 %copy-start.3 = (bf16[2,64,1536]{2,1,0:T(8,128)(2,1)S(1)}, bf16[2,64,1536]{2,1,0:T(8,128)(2,1)}, u32[]{:S(2)}) copy-start(bf16[2,64,1536]{2,1,0:T(8,128)(2,1)} %param.13) | copy-start | bytes 1179652
  7.2 4.3 copy-start.1
  7.2 5.5 copy-start.40
  7.2 49.0 %copy-start.41 = (f32[3,48]{1,0:T(4,128)S(1)}, f32[3,48]{1,0:T(4,128)}, u32[]{:S(2)}) copy-start(f32[3,48]{1,0:T(4,128)} %param.23) | copy-start | bytes 1732
  7.2 183.7 %all-gather.9.cloned.1.call-start = ((), (), s32[]{:S(2)}) async-start(), calls=%async_computation.24 | async-start | bytes 17694720 | tf_op jit(solution)/shard_map/all_gather | solution.py:87
  8.5 85.7 %copy-start.30 = (f32[2,64]{1,0:T(2,128)}, f32[2,64]{1,0:T(2,128)S(1)}, u32[]{:S(2)}) copy-start(f32[2,64]{1,0:T(2,128)S(1)} %broadcast_multiply_fusion.3) | copy-start | bytes 1540
  9.8 1.7 copy-start.38
  9.8 84.4 %copy-start.36 = (f32[2,64]{1,0:T(2,128)}, f32[2,64]{1,0:T(2,128)S(1)}, u32[]{:S(2)}) copy-start(f32[2,64]{1,0:T(2,128)S(1)} %fusion.74) | copy-start | bytes 1540
  11.5 84.1 %copy-start.28 = (f32[2,256]{1,0:T(2,128)}, f32[2,256]{1,0:T(2,128)S(1)}, u32[]{:S(2)}) copy-start(f32[2,256]{1,0:T(2,128)S(1)} %broadcast_multiply_fusion.1) | copy-start | bytes 6148
  12.1 83.6 %copy-start.32 = (f32[2,256]{1,0:T(2,128)}, f32[2,256]{1,0:T(2,128)S(1)}, u32[]{:S(2)}) copy-start(f32[2,256]{1,0:T(2,128)S(1)} %fusion.73) | copy-start | bytes 6148
  56.2 39.5 %copy-start.20 = (f32[1536]{0:T(1024)}, f32[1536]{0:T(1024)S(1)}, u32[]{:S(2)}) copy-start(f32[1536]{0:T(1024)S(1)} %get-tuple-element.23) | copy-start | bytes 18436
  56.2 39.4 %copy-start.22 = (f32[1536]{0:T(1024)}, f32[1536]{0:T(1024)S(1)}, u32[]{:S(2)}) copy-start(f32[1536]{0:T(1024)S(1)} %get-tuple-element.24) | copy-start | bytes 18436
  94.2 5.8 copy-start.25
  94.2 6.7 copy-start.26
  95.7 6.2 copy-start.27
  96.6 10.3 all-to-all-start.3
  106.9 20.4 %all-to-all-start = ((bf16[48,8,192]{2,0,1:T(8,128)(2,1)}), bf16[48,8,192]{2,0,1:T(8,128)(2,1)S(1)}, u32[]{:S(2)}, u32[]{:S(2)}) async-start(bf16[48,8,192]{2,0,1:T(8,128)(2,1)} %copy.102), calls=%async_computation | async-start | bytes 393216 | tf_op jit(solution)/shard_map/all_to_all | solution.py:62
  127.3 113.8 %copy-start.17 = (bf16[1536,192]{0,1:T(8,128)(2,1)}, bf16[1536,192]{0,1:T(8,128)(2,1)S(1)}, u32[]{:S(2)}) copy-start(bf16[1536,192]{0,1:T(8,128)(2,1)S(1)} %all_gather.42) | copy-start | bytes 1769476
  127.3 21.9 %all-to-all-start.2 = ((bf16[48,8,192]{2,0,1:T(8,128)(2,1)}), bf16[48,8,192]{2,0,1:T(8,128)(2,1)S(1)}, u32[]{:S(2)}, u32[]{:S(2)}) async-start(bf16[48,8,192]{2,0,1:T(8,128)(2,1)} %copy.105), calls=%async_computation.2 | async-start | bytes 393216 | tf_op jit(solution)/shard_map/all_to_all | solution.py:61
  149.2 58.6 %copy-start.13 = (bf16[1536,192]{1,0:T(8,128)(2,1)}, bf16[1536,192]{1,0:T(8,128)(2,1)S(1)}, u32[]{:S(2)}) copy-start(bf16[1536,192]{1,0:T(8,128)(2,1)S(1)} %all_gather.39) | copy-start | bytes 1769476
  149.2 22.3 %all-to-all-start.1 = ((bf16[48,8,192]{2,0,1:T(8,128)(2,1)}), bf16[48,8,192]{2,0,1:T(8,128)(2,1)S(1)}, u32[]{:S(2)}, u32[]{:S(2)}) async-start(bf16[48,8,192]{2,0,1:T(8,128)(2,1)} %copy.103), calls=%async_computation.1 | async-start | bytes 393216 | tf_op jit(solution)/shard_map/all_to_all | solution.py:60
  153.0 138.1 %reduce-scatter.25.cloned.1.call-start = ((), (), s32[]{:S(2)}) async-start(), calls=%async_computation.25 | async-start | bytes 3538944 | tf_op jit(solution)/shard_map/reduce_scatter | solution.py:119
  171.5 31.4 %copy-start.15 = (bf16[1536,192]{1,0:T(8,128)(2,1)}, bf16[1536,192]{1,0:T(8,128)(2,1)S(1)}, u32[]{:S(2)}) copy-start(bf16[1536,192]{1,0:T(8,128)(2,1)S(1)} %all_gather.41) | copy-start | bytes 1769476
  244.9 89.9 %all-gather.11.cloned.1.call-start = ((), (), s32[]{:S(2)}) async-start(), calls=%async_computation.26 | async-start | bytes 3538944 | tf_op jit(solution)/shard_map/all_gather | solution.py:129
  293.0 39.7 %copy-start.12 = (bf16[2,64,1536]{2,1,0:T(8,128)(2,1)S(1)}, bf16[2,64,1536]{2,1,0:T(8,128)(2,1)}, u32[]{:S(2)}) copy-start(bf16[2,64,1536]{2,1,0:T(8,128)(2,1)} %param.14) | copy-start | bytes 1179652
  293.0 93.7 %all-gather.13.cloned.1.call-start = ((), (), s32[]{:S(2)}) async-start(), calls=%async_computation.27 | async-start | bytes 2949120 | tf_op jit(solution)/shard_map/all_gather | solution.py:72
  311.0 126.6 %all-gather.15.cloned.1.call-start = ((), (), s32[]{:S(2)}) async-start(), calls=%async_computation.28 | async-start | bytes 2949120 | tf_op jit(solution)/shard_map/all_gather | solution.py:73
  332.0 138.6 %all-gather.17.cloned.1.call-start = ((), (), s32[]{:S(2)}) async-start(), calls=%async_computation.30 | async-start | bytes 3538944 | tf_op jit(solution)/shard_map/all_gather | solution.py:88
  333.6 200.7 %reduce-scatter.29.cloned.1.call-start = ((), (), s32[]{:S(2)}) async-start(), calls=%async_computation.31 | async-start | bytes 3538944 | tf_op jit(solution)/shard_map/reduce_scatter | solution.py:158
  334.8 2.8 copy-start.4
  470.6 13.2 %copy-start.43 = (bf16[1536,768]{1,0:T(8,128)(2,1)S(1)}, bf16[1536,768]{1,0:T(8,128)(2,1)}, u32[]{:S(2)}) copy-start(bf16[1536,768]{1,0:T(8,128)(2,1)} %all-gather.13.cloned.1.call-done) | copy-start | bytes 7077892
  483.8 4.1 copy-start.44
  487.9 46.5 %copy-start.7 = (bf16[2,64,1536]{2,1,0:T(8,128)(2,1)S(1)}, bf16[2,64,1536]{2,1,0:T(8,128)(2,1)}, u32[]{:S(2)}) copy-start(bf16[2,64,1536]{2,1,0:T(8,128)(2,1)} %reduce-scatter.25.cloned.1.call-done) | copy-start | bytes 1179652
  487.9 83.9 %all-gather.19.cloned.1.call-start = ((), (), s32[]{:S(2)}) async-start(), calls=%async_computation.32 | async-start | bytes 3538944 | tf_op jit(solution)/shard_map/all_gather | solution.py:170
  539.4 167.3 %reduce-scatter.35.cloned.1.call-start = ((), (), s32[]{:S(2)}) async-start(), calls=%async_computation.35 | async-start | bytes 2949120 | tf_op jit(solution)/shard_map/reduce_scatter | solution.py:246
  539.8 4.6 copy-start.42
  548.4 168.4 %reduce-scatter.33.cloned.1.call-start = ((), (), s32[]{:S(2)}) async-start(), calls=%async_computation.34 | async-start | bytes 2949120 | tf_op jit(solution)/shard_map/reduce_scatter | solution.py:243
  554.9 180.4 %reduce-scatter.43.cloned.1.call-start = ((), (), s32[]{:S(2)}) async-start(), calls=%async_computation.39 | async-start | bytes 983040 | tf_op jit(solution)/shard_map/reduce_scatter | solution.py:240
  594.6 4.4 copy-start.6
  620.2 17.3 %copy-start.14 = (bf16[1536,192]{1,0:T(8,128)(2,1)S(1)}, bf16[1536,192]{1,0:T(8,128)(2,1)}, u32[]{:S(2)}) copy-start(bf16[1536,192]{1,0:T(8,128)(2,1)} %copy-done.13) | copy-start | bytes 1769476
  620.2 121.9 %reduce-scatter.37.cloned.1.call-start = ((), (), s32[]{:S(2)}) async-start(), calls=%async_computation.36 | async-start | bytes 983040 | tf_op jit(solution)/shard_map/reduce_scatter | solution.py:231
  637.4 111.9 %reduce-scatter.41.cloned.1.call-start = ((), (), s32[]{:S(2)}) async-start(), calls=%async_computation.38 | async-start | bytes 983040 | tf_op jit(solution)/shard_map/reduce_scatter | solution.py:237
  637.5 24.3 %copy-start.9 = (bf16[5120,192]{0,1:T(8,128)(2,1)S(1)}, bf16[5120,192]{0,1:T(8,128)(2,1)}, u32[]{:S(2)}) copy-start(bf16[5120,192]{0,1:T(8,128)(2,1)} %reshape_reshape.13) | copy-start | bytes 5898244
  670.4 102.2 %reduce-scatter.39.cloned.1.call-start = ((), (), s32[]{:S(2)}) async-start(), calls=%async_computation.37 | async-start | bytes 983040 | tf_op jit(solution)/shard_map/reduce_scatter | solution.py:234
  684.7 199.7 %reduce-scatter.31.cloned.1.call-start = ((), (), s32[]{:S(2)}) async-start(), calls=%async_computation.33 | async-start | bytes 17694720 | tf_op jit(solution)/shard_map/reduce_scatter | solution.py:211
  706.7 13.9 %all-to-all-start.11 = ((bf16[8,48,768]{2,1,0:T(8,128)(2,1)}), bf16[8,48,768]{2,1,0:T(8,128)(2,1)S(1)}, u32[]{:S(2)}, u32[]{:S(2)}) async-start(bf16[8,48,768]{2,1,0:T(8,128)(2,1)} %bitcast.180), calls=%async_computation.17 | async-start | bytes 1179648 | tf_op jit(solution)/shard_map/all_to_all | solution.py:266
  710.2 223.7 %reduce-scatter.27.cloned.1.call-start = ((), (), s32[]{:S(2)}) async-start(), calls=%async_computation.29 | async-start | bytes 3538944 | tf_op jit(solution)/shard_map/reduce_scatter | solution.py:139
  720.6 4.2 copy-start.16
  720.6 14.7 %all-to-all-start.10 = ((bf16[8,48,768]{2,1,0:T(8,128)(2,1)}), bf16[8,48,768]{2,1,0:T(8,128)(2,1)}, u32[]{:S(2)}, u32[]{:S(2)}) async-start(bf16[8,48,768]{2,1,0:T(8,128)(2,1)} %bitcast.179), calls=%async_computation.15 | async-start | bytes 1179648 | tf_op jit(solution)/shard_map/all_to_all | solution.py:263
  735.3 9.6 all-to-all-start.9
  744.8 9.6 all-to-all-start.6
  754.4 18.2 %all-to-all-start.8 = ((bf16[8,48,192]{2,1,0:T(8,128)(2,1)}), bf16[8,48,192]{2,1,0:T(8,128)(2,1)S(1)}, u32[]{:S(2)}, u32[]{:S(2)}) async-start(bf16[8,48,192]{2,1,0:T(8,128)(2,1)} %bitcast.182), calls=%async_computation.12 | async-start | bytes 393216 | tf_op jit(solution)/shard_map/all_to_all | solution.py:257
  772.6 9.9 all-to-all-start.7
  776.3 259.0 %reduce-scatter.47.cloned.1.call-start = ((), (), s32[]{:S(2)}) async-start(), calls=%async_computation.41 | async-start | bytes 811008
  782.8 103.7 %copy-start.21 = (f32[1536]{0:T(1024)S(1)}, f32[1536]{0:T(1024)}, u32[]{:S(2)}) copy-start(f32[1536]{0:T(1024)} %copy-done.20) | copy-start | bytes 18436
  782.8 103.7 %copy-start.31 = (f32[2,64]{1,0:T(2,128)S(1)}, f32[2,64]{1,0:T(2,128)}, u32[]{:S(2)}) copy-start(f32[2,64]{1,0:T(2,128)} %copy-done.30) | copy-start | bytes 1540
  783.6 103.1 %copy-start.39 = (f32[2,64]{1,0:T(2,128)S(1)}, f32[2,64]{1,0:T(2,128)}, u32[]{:S(2)}) copy-start(f32[2,64]{1,0:T(2,128)} %copy-done.38) | copy-start | bytes 1540
  783.6 103.2 %copy-start.37 = (f32[2,64]{1,0:T(2,128)S(1)}, f32[2,64]{1,0:T(2,128)}, u32[]{:S(2)}) copy-start(f32[2,64]{1,0:T(2,128)} %copy-done.36) | copy-start | bytes 1540
  783.7 103.6 %copy-start.2 = (bf16[2,256,1536]{2,1,0:T(8,128)(2,1)S(1)}, bf16[2,256,1536]{2,1,0:T(8,128)(2,1)}, u32[]{:S(2)}) copy-start(bf16[2,256,1536]{2,1,0:T(8,128)(2,1)} %param.12) | copy-start | bytes 4718596
  783.7 103.7 %copy-start.23 = (f32[1536]{0:T(1024)S(1)}, f32[1536]{0:T(1024)}, u32[]{:S(2)}) copy-start(f32[1536]{0:T(1024)} %copy-done.22) | copy-start | bytes 18436
  783.7 103.7 %copy-start.29 = (f32[2,256]{1,0:T(2,128)S(1)}, f32[2,256]{1,0:T(2,128)}, u32[]{:S(2)}) copy-start(f32[2,256]{1,0:T(2,128)} %copy-done.28) | copy-start | bytes 6148
  886.5 1.9 copy-start
  891.2 42.7 %copy-start.10 = (bf16[2,64,1536]{2,1,0:T(8,128)(2,1)S(1)}, bf16[2,64,1536]{2,1,0:T(8,128)(2,1)}, u32[]{:S(2)}) copy-start(bf16[2,64,1536]{2,1,0:T(8,128)(2,1)} %reduce-scatter.29.cloned.1.call-done) | copy-start | bytes 1179652
  895.9 239.7 %reduce-scatter.45.cloned.1.call-start = ((), (), s32[]{:S(2)}) async-start(), calls=%async_computation.40 | async-start | bytes 811008
  (9 other events, 11.5 us)
Sparse Core Ops, SparseCore 0:
  95.8 87.8 all-gather.8
  245.0 46.1 reduce-scatter.24
  293.8 40.9 all-gather.10
  336.3 50.4 all-gather.12
  388.2 49.2 all-gather.14
  439.5 31.1 all-gather.16
  488.0 46.2 reduce-scatter.28
  539.5 32.2 all-gather.18
  574.2 48.0 reduce-scatter.34
  624.4 47.5 reduce-scatter.32
  674.3 22.7 reduce-scatter.42
  699.8 22.5 reduce-scatter.36
  724.7 22.5 reduce-scatter.40
  750.0 22.5 reduce-scatter.38
  775.9 108.4 reduce-scatter.30
  887.6 46.2 reduce-scatter.26
  939.7 95.5 reduce-scatter.46
  1041.0 94.4 reduce-scatter.44
where the time goes:
time: 1150 us; the launch traced here: 1140 us
  waiting for transfers between devices  611 us (53%)
  blocking collectives  188 us (16%)
  matrix products  161 us (14%)
  local copies, waits for them, and re-layouts  77.4 us (7%)
  other arithmetic  52.3 us (5%)
  starting transfers between devices  38 us (3%)
  between operations  16.3 us (1%)
    unnamed x20, waiting for transfers between devices  198 us
    reduce_scatter x1, waiting for transfers between devices, head_plan(): lax.psum_scatter(jnp.concatenate([both[:, :patch_count], both[:, patch_co...  101 us
    dot_general x6, matrix products, product_right(): lax.dot_general(left, right, (((1,), (1,)), ((), ())), preferred_element_...  59.3 us
    dot_general x6, matrix products, product(): return jnp.dot(left, right, preferred_element_type=jnp.float32)  48.4 us
    reduce_scatter x1, waiting for transfers between devices, head_plan(): lax.psum_scatter(product_right(piece, up_cols).reshape(img_count * lax.ax...  46.4 us
    reduce_scatter x1, waiting for transfers between devices, head_plan(): lax.psum_scatter(product_right(piece, out_cols).reshape(img_count * lax.a...  46.2 us
    all_gather x1, waiting for transfers between devices, head_plan(): lax.all_gather(weight_parts[4], 'gx', axis=0, tiled=True)  45.7 us
    all_gather x1, waiting for transfers between devices, head_plan(): lax.all_gather(weight_parts[5], 'gx', axis=0, tiled=True)  44 us
  transfers between devices with their start and end apart: 28, of which 18 were waited for; matrix products, arithmetic and copies ran while one was open for 17% of the time, Pallas kernels for 0%

commit v1 on v0

v1 whole, which is shorter than its diff:
```python
import functools

import jax
import jax.numpy as jnp
from jax import lax
from jax.experimental import pallas as pl
from jax.experimental.pallas import tpu as pltpu
from jax.sharding import PartitionSpec as P

HEAD = 96
LANES = 128
EPSILON = 1e-05
BF16 = jnp.bfloat16
F32 = jnp.float32


def product(left, right):
    return jnp.dot(left, right, preferred_element_type=F32)


def product_left(left, right):
    return lax.dot_general(left, right, (((0,), (0,)), ((), ())), preferred_element_type=F32)


def product_right(left, right):
    return lax.dot_general(left, right, (((1,), (1,)), ((), ())), preferred_element_type=F32)


def swap(block, mask, axis="gy"):
    count = lax.axis_size(axis)
    return lax.ppermute(block, axis, [(i, i ^ mask) for i in range(count)])


def far_masks():
    return [mask for mask in range(lax.axis_size("gy")) if mask % 2 == 0]


def spread(block):
    far = jnp.stack([block] + [swap(block, mask) for mask in far_masks()[1:]])
    return jnp.concatenate([far, swap(far, 1)])


def collect(parts):
    count = parts.shape[0] // 2
    own = (parts[:count].astype(F32) + swap(parts[count:], 1).astype(F32)).astype(BF16)
    total = own[0].astype(F32)
    for index, mask in enumerate(far_masks()[1:]):
        total = total + swap(own[1 + index], mask).astype(F32)
    return total


def far_bits():
    bits, bit = [], 2
    while bit < lax.axis_size("gy"):
        bits.append(bit)
        bit *= 2
    return bits


def route(turn):
    bits = far_bits()
    turn = turn % len(bits)
    return bits[turn:] + bits[:turn]


def spread_big(block, turn):
    held = {0: block}
    for bit in route(turn):
        held.update({mask ^ bit: swap(part, bit) for mask, part in list(held.items())})
    return held


def collect_big(parts, turn):
    held = dict(parts)
    for bit in reversed(route(turn)):
        for mask in [m for m in held if not m & bit]:
            arrived = swap(held.pop(mask ^ bit), bit)
            held[mask] = (held[mask].astype(F32) + arrived.astype(F32)).astype(BF16)
    return held[0]


def bits_of(count):
    bits, bit = [], 1
    while bit < count:
        bits.append(bit)
        bit *= 2
    return bits


def gather_small(rows):
    for axis in ("gy", "gx"):
        place = lax.axis_index(axis)
        for bit in bits_of(lax.axis_size(axis)):
            other = swap(rows, bit, axis)
            upper = (place & bit) != 0
            rows = jnp.concatenate([jnp.where(upper, other, rows), jnp.where(upper, rows, other)])
    return rows


def sum_small(rows):
    for axis in ("gy", "gx"):
        for bit in bits_of(lax.axis_size(axis)):
            rows = rows + swap(rows, bit, axis)
    return rows


def normed(rows, gain, bias):
    average = jnp.mean(rows, axis=-1, keepdims=True)
    centred = rows - average
    spread_of = jnp.mean(centred * centred, axis=-1, keepdims=True)
    return centred * lax.rsqrt(spread_of + EPSILON) * gain + bias


def head_mask(rows, lanes, head):
    lane = lax.broadcasted_iota(jnp.int32, (rows, lanes), 1)
    return (lane >= head * HEAD) & (lane < (head + 1) * HEAD)


def stacked(rows, heads):
    count, lanes = rows.shape
    return jnp.concatenate(
        [jnp.where(head_mask(count, lanes, h), rows, jnp.zeros_like(rows)) for h in range(heads)]
    )


def unstacked(rows, heads):
    count, lanes = rows.shape[0] // heads, rows.shape[1]
    total = jnp.zeros((count, lanes), rows.dtype)
    for h in range(heads):
        total = jnp.where(head_mask(count, lanes, h), rows[h * count : (h + 1) * count], total)
    return total


def softmax_rows(scores):
    top = jnp.max(scores, axis=-1, keepdims=True)
    raised = jnp.exp(scores - top)
    return raised / jnp.sum(raised, axis=-1, keepdims=True)


def attend_kernel(heads, patch, scale, media_ref, latent_ref, gains_ref, biases_ref, weights_ref,
                  joined_ref, kv_ref, query_ref, mixed_ref, out_ref):
    lanes = weights_ref.shape[1] // 4
    media = normed(media_ref[0].astype(F32), gains_ref[0:1], biases_ref[0:1]).astype(BF16)
    latent = normed(latent_ref[0].astype(F32), gains_ref[1:2], biases_ref[1:2]).astype(BF16)
    joined_ref[0, :patch] = media
    joined_ref[0, patch:] = latent
    kv_ref[0, :patch] = product(media, weights_ref[:, : 2 * lanes]).astype(BF16)
    kv_ref[0, patch:] = product(latent, weights_ref[:, : 2 * lanes]).astype(BF16)
    query = (product(latent, weights_ref[:, 2 * lanes : 3 * lanes]) * scale).astype(BF16)
    query_ref[0] = query
    keys, values = kv_ref[0, :, :lanes], kv_ref[0, :, lanes:]
    probs = softmax_rows(product_right(stacked(query, heads), keys))
    mixed = unstacked(product(probs.astype(BF16), values), heads).astype(BF16)
    mixed_ref[0] = mixed
    out_ref[0] = product_right(mixed, weights_ref[:, 3 * lanes :]).astype(BF16)


def attend(media, latent, gains, biases, weights, heads):
    count, patch, width = media.shape
    lat = latent.shape[1]
    lanes = weights.shape[1] // 4
    rows = patch + lat
    whole = lambda shape: pl.BlockSpec(shape, lambda i: (0,) * len(shape))
    one = lambda *shape: pl.BlockSpec((1,) + shape, lambda i: (i, 0, 0))
    return pl.pallas_call(
        functools.partial(attend_kernel, heads, patch, HEAD ** (-0.5)),
        grid=(count,),
        in_specs=[one(patch, width), one(lat, width), whole(gains.shape), whole(biases.shape), whole(weights.shape)],
        out_specs=[one(rows, width), one(rows, 2 * lanes), one(lat, lanes), one(lat, lanes), one(lat, width)],
        out_shape=[
            jax.ShapeDtypeStruct((count, rows, width), BF16),
            jax.ShapeDtypeStruct((count, rows, 2 * lanes), BF16),
            jax.ShapeDtypeStruct((count, lat, lanes), BF16),
            jax.ShapeDtypeStruct((count, lat, lanes), BF16),
            jax.ShapeDtypeStruct((count, lat, width), BF16),
        ],
        compiler_params=pltpu.CompilerParams(vmem_limit_bytes=48 * 2**20),
        cost_estimate=pl.CostEstimate(
            flops=2 * count * rows * width * 3 * lanes, bytes_accessed=4 * count * rows * width, transcendentals=0
        ),
    )(media, latent, gains, biases, weights)


def attend_back_kernel(heads, patch, scale, branch_ref, kv_ref, query_ref, weights_ref, joined_ref, dkv_ref, dquery_ref):
    lanes = weights_ref.shape[1] // 4
    query = stacked(query_ref[0], heads)
    keys, values = kv_ref[0, :, :lanes], kv_ref[0, :, lanes:]
    probs = softmax_rows(product_right(query, keys))
    grad_mixed = product(branch_ref[0], weights_ref[:, 3 * lanes :]).astype(BF16)
    grad_mixed = stacked(grad_mixed, heads)
    grad_values = product_left(probs.astype(BF16), grad_mixed).astype(BF16)
    grad_probs = product_right(grad_mixed, values)
    inner = jnp.sum(grad_probs * probs, axis=-1, keepdims=True)
    grad_scores = (probs * (grad_probs - inner)).astype(BF16)
    grad_query = unstacked(product(grad_scores, keys), heads).astype(BF16)
    grad_keys = product_left(grad_scores, query).astype(BF16)
    dkv_ref[0, :, :lanes] = grad_keys
    dkv_ref[0, :, lanes:] = grad_values
    dquery_ref[0] = grad_query
    back = product_right(grad_keys, weights_ref[:, :lanes]) + product_right(grad_values, weights_ref[:, lanes : 2 * lanes])
    extra = product_right(grad_query, weights_ref[:, 2 * lanes : 3 * lanes]) * scale
    joined_ref[0, :patch] = back[:patch].astype(BF16)
    joined_ref[0, patch:] = (back[patch:] + extra).astype(BF16)


def attend_back(branch, kv, query, weights, heads):
    count, lat, width = branch.shape
    rows, lanes = kv.shape[1], weights.shape[1] // 4
    whole = lambda shape: pl.BlockSpec(shape, lambda i: (0,) * len(shape))
    one = lambda *shape: pl.BlockSpec((1,) + shape, lambda i: (i, 0, 0))
    return pl.pallas_call(
        functools.partial(attend_back_kernel, heads, rows - lat, HEAD ** (-0.5)),
        grid=(count,),
        in_specs=[one(lat, width), one(rows, 2 * lanes), one(lat, lanes), whole(weights.shape)],
        out_specs=[one(rows, width), one(rows, 2 * lanes), one(lat, lanes)],
        out_shape=[
            jax.ShapeDtypeStruct((count, rows, width), BF16),
            jax.ShapeDtypeStruct((count, rows, 2 * lanes), BF16),
            jax.ShapeDtypeStruct((count, lat, lanes), BF16),
        ],
        compiler_params=pltpu.CompilerParams(vmem_limit_bytes=48 * 2**20),
        cost_estimate=pl.CostEstimate(
            flops=2 * count * rows * width * 3 * lanes, bytes_accessed=3 * count * rows * width, transcendentals=0
        ),
    )(branch, kv, query, weights)


def norm_back(rows, gain, grad):
    average = jnp.mean(rows, axis=-1, keepdims=True)
    centred = rows - average
    inverse = lax.rsqrt(jnp.mean(centred * centred, axis=-1, keepdims=True) + EPSILON)
    unit = centred * inverse
    scaled = grad * gain
    first = jnp.mean(scaled, axis=-1, keepdims=True)
    second = jnp.mean(scaled * unit, axis=-1, keepdims=True)
    back = inverse * (scaled - first - unit * second)
    axes = tuple(range(rows.ndim - 1))
    return back, jnp.sum(grad * unit, axis=axes), jnp.sum(grad, axis=axes)


def local(media_features, latents, cotangent, image_counts, w_query, w_key, w_value, w_out, w_up, w_down,
          norm_gains, norm_biases):
    devices_x, devices_y = lax.axis_size("gx"), lax.axis_size("gy")
    img_count, lat, width = latents.shape
    patch = media_features.shape[1]
    rows = patch + lat
    shard = w_query.shape[0]
    head_width = width // devices_y
    heads = head_width // HEAD
    ff_width = w_up.shape[1] // devices_y
    lanes = -(-head_width // LANES) * LANES

    four = jnp.stack([w_key, w_value, w_query, w_out.T])
    four = four.reshape(4, shard, devices_y, head_width).transpose(2, 1, 0, 3).reshape(devices_y, shard, 4 * head_width)
    four = lax.all_to_all(four, "gy", split_axis=0, concat_axis=0, tiled=True)
    four = lax.all_gather(four.reshape(devices_y * shard, 4 * head_width), "gx", axis=0, tiled=True)
    weights = jnp.pad(four.reshape(width, 4, head_width), ((0, 0), (0, 0), (0, lanes - head_width)))
    weights = weights.reshape(width, 4 * lanes)

    two = jnp.stack([w_up, w_down.T]).reshape(2, shard, devices_y, ff_width).transpose(2, 0, 1, 3)
    two = lax.all_to_all(two, "gy", split_axis=0, concat_axis=0, tiled=True)
    up_cols = lax.all_gather(two[:, 0].reshape(devices_y * shard, ff_width), "gx", axis=0, tiled=True)
    down_cols = lax.all_gather(two[:, 1].reshape(devices_y * shard, ff_width), "gx", axis=0, tiled=True)

    small = jnp.stack([norm_gains, norm_biases]).reshape(1, 6 * shard)
    small = gather_small(small).reshape(devices_x * devices_y, 2, 3, shard).transpose(1, 2, 0, 3).reshape(2, 3, width)
    gains, biases = small[0], small[1]

    own = jnp.concatenate([media_features, latents], axis=1)
    pieces = []
    for image in range(img_count):
        held = spread_big(own[image], image)
        for mask in far_masks():
            pieces.append((image, mask, jnp.stack([held[mask], swap(held[mask], 1)])))

    live = (jnp.arange(img_count, dtype=jnp.int32) < image_counts[0]).astype(BF16)
    cot_own = cotangent * live[:, None, None]
    cot_all = spread(cot_own)

    done = {}
    for image, mask, piece in pieces:
        done[image, mask] = attend(piece[:, :patch], piece[:, patch:], gains, biases, weights, heads)

    def in_order(position):
        near = [jnp.stack([done[image, mask][position][0] for image in range(img_count)]) for mask in far_masks()]
        far = [jnp.stack([done[image, mask][position][1] for image in range(img_count)]) for mask in far_masks()]
        return jnp.stack(near + far)

    latent_float = latents.astype(F32)
    attended = collect(in_order(4)) + latent_float
    hidden_own = normed(attended, gains[2], biases[2]).astype(BF16)
    hidden = spread(hidden_own).reshape(-1, width)
    group = devices_y * img_count

    upper = product(hidden, up_cols)
    cdf = 0.5 * (1.0 + lax.erf(upper * (0.5**0.5)))
    active = (upper * cdf).astype(BF16)
    slope = cdf + upper * jnp.exp(-0.5 * upper * upper) * (0.5 / jnp.pi) ** 0.5
    cot_flat = cot_all.reshape(-1, width)
    grad_upper = (slope * product(cot_flat, down_cols)).astype(BF16)
    hidden_parts = product_right(grad_upper, up_cols).astype(BF16)
    grad_hidden = collect(hidden_parts.reshape(devices_y, img_count, lat, width))
    ffn_parts = product_right(active, down_cols).astype(BF16)
    result = attended + collect(ffn_parts.reshape(devices_y, img_count, lat, width))
    outputs = (result * live.astype(F32)[:, None, None]).astype(BF16)

    def home(grads, count):
        part = lax.psum_scatter(grads.astype(BF16), "gx", scatter_dimension=0, tiled=True)
        part = part.reshape(devices_y, shard, -1)
        part = lax.all_to_all(part, "gy", split_axis=0, concat_axis=0, tiled=True)
        part = part.reshape(devices_y, shard, count, -1).transpose(2, 1, 0, 3).reshape(count, shard, -1)
        return part.astype(F32)

    grad_down = home(product_left(cot_flat, active), 1)[0]
    grad_up = home(product_left(hidden, grad_upper), 1)[0]

    grad_norm_input, gain_two, bias_two = norm_back(attended, gains[2], grad_hidden)
    grad_attended = cot_own.astype(F32) + grad_norm_input
    branch = spread(grad_attended.astype(BF16))

    grads = {}
    count = len(far_masks())
    for image, mask, piece in pieces:
        index = far_masks().index(mask)
        pair = jnp.stack([branch[index, image], branch[count + index, image]])
        grads[image, mask] = attend_back(pair, done[image, mask][1], done[image, mask][2], weights, heads)

    back = []
    for image in range(img_count):
        parts = {}
        for mask in far_masks():
            both = grads[image, mask][0]
            parts[mask] = (both[0].astype(F32) + swap(both[1], 1).astype(F32)).astype(BF16)
        back.append(collect_big(parts, image))
    grad_joined = jnp.stack(back).astype(F32)

    keys = [(image, mask) for image, mask, _ in pieces]
    joined_all = jnp.concatenate([done[key][0] for key in keys]).reshape(-1, width)
    latent_all = jnp.concatenate([done[key][0][:, patch:] for key in keys]).reshape(-1, width)
    mixed_all = jnp.concatenate([done[key][3] for key in keys]).reshape(-1, lanes)
    dkv_all = jnp.concatenate([grads[key][1] for key in keys]).reshape(-1, 2 * lanes)
    dquery_all = jnp.concatenate([grads[key][2] for key in keys]).reshape(-1, lanes)
    branch_all = jnp.concatenate(
        [jnp.stack([branch[far_masks().index(mask), image], branch[count + far_masks().index(mask), image]]) for image, mask in keys]
    ).reshape(-1, width)
    dkv_cols = product_left(joined_all, dkv_all).reshape(width, 2, lanes)[:, :, :head_width].reshape(width, -1)
    dquery_cols = product_left(latent_all, dquery_all)[:, :head_width] * HEAD ** (-0.5)
    dout_cols = product_left(branch_all, mixed_all)[:, :head_width]
    grad_key, grad_value, grad_query, grad_out = home(
        jnp.concatenate([dkv_cols, dquery_cols, dout_cols], axis=1), 4
    )

    grad_media, gain_zero, bias_zero = norm_back(media_features.astype(F32), gains[0], grad_joined[:, :patch])
    grad_latent, gain_one, bias_one = norm_back(latent_float, gains[1], grad_joined[:, patch:])
    grad_latents = grad_attended + grad_latent
    sums = sum_small(jnp.stack([gain_zero, gain_one, gain_two, bias_zero, bias_one, bias_two]))
    place = lax.axis_index("gx") * devices_y + lax.axis_index("gy")
    sums = lax.dynamic_slice_in_dim(sums, place * shard, shard, axis=1)
    return (
        outputs, grad_media, grad_latents, grad_query, grad_key, grad_value, grad_out.T, grad_up, grad_down.T,
        sums[:3], sums[3:],
    )


def solution(mesh):
    split = ("gx", "gy")
    images, first, second = P(split, None, None), P(split, None), P(None, split)
    return jax.shard_map(
        local,
        mesh=mesh,
        in_specs=(images, images, images, P(split), first, first, first, second, first, second, second, second),
        out_specs=(images, images, images, first, first, first, second, first, second, second, second),
        check_vma=False,
    )
```

time: 1150 us -> 719 us (0.63)
  waiting for transfers between devices: 611 us -> 238 us
  blocking collectives: 188 us -> 0 us
  matrix products: 161 us -> 48.7 us
  Pallas kernels: 0 us -> 107 us
  local copies, waits for them, and re-layouts: 77.4 us -> 143 us
  starting transfers between devices: 38 us -> 74.4 us
  other arithmetic: 52.3 us -> 84 us
    reduce_scatter x10 -> x3, waiting for transfers between devices: 244 us -> 0.01 us  [home(): lax.psum_scatter(grads.astype(BF16), 'gx', scatter_dimension=0, tiled=True)]
    ppermute x0 -> x62, waiting for transfers between devices: none -> 210 us  [swap(): return lax.ppermute(block, axis, [(i, i ^ mask) for i in range(count)])]
    unnamed x20 -> x6, waiting for transfers between devices: 198 us -> 0.1 us
    all_gather x6 -> x0, blocking collectives: 152 us -> none  [the longest x1 43.4 us: head_plan(): lax.all_gather(norm_gains, ('gx', 'gy'), axis=1, tiled=True)]
    all_gather x6 -> x3, waiting for transfers between devices: 139 us -> 0.01 us  [the longest x1 0.01 us: local(): lax.all_gather(four.reshape(devices_y * shard, 4 * head_width), 'gx', axi...]
    pallas_call x0 -> x16, Pallas kernels: none -> 107 us  [the longest x8 63.7 us: attend(): pl.pallas_call(functools.partial(attend_kernel, heads, patch, HEAD ** (-0...]
    ppermute x0 -> x62, starting transfers between devices: none -> 52.8 us  [swap(): return lax.ppermute(block, axis, [(i, i ^ mask) for i in range(count)])]
    dot_general x6 -> x2, matrix products: 59.3 us -> 7.34 us  [product_right(): lax.dot_general(left, right, (((1,), (1,)), ((), ())), preferred_element_...]
  transfers between devices with their start and end apart: 28 -> 73, of which waited for: 18 -> 33; matrix products, arithmetic and copies ran while one was open for 17% -> 29% of each run, Pallas kernels for 0% -> 15%
where the time goes in v1:
time: 719 us; the launch traced here: 712 us
  waiting for transfers between devices  238 us (33%)
  local copies, waits for them, and re-layouts  143 us (20%)
  Pallas kernels  107 us (15%)
  other arithmetic  84 us (12%)
  starting transfers between devices  74.4 us (10%)
  matrix products  48.7 us (7%)
  between operations  17.2 us (2%)
    ppermute x62, waiting for transfers between devices, swap(): return lax.ppermute(block, axis, [(i, i ^ mask) for i in range(count)])  210 us
    unnamed x375, local copies, waits for them, and re-layouts  67.9 us
    pallas_call x8, Pallas kernels, attend(): pl.pallas_call(functools.partial(attend_kernel, heads, patch, HEAD ** (-0...  63.7 us
    ppermute x62, starting transfers between devices, swap(): return lax.ppermute(block, axis, [(i, i ^ mask) for i in range(count)])  52.8 us
    pallas_call x8, Pallas kernels, attend_back(): pl.pallas_call(functools.partial(attend_back_kernel, heads, rows - lat, H...  43.1 us
    another operation x16, other arithmetic, local(): pieces.append((image, mask, jnp.stack([held[mask], swap(held[mask], 1)])))  29.2 us
    dot_general x5, matrix products, product_left(): lax.dot_general(left, right, (((0,), (0,)), ((), ())), preferred_element_...  27.2 us
    all_to_all x3, waiting for transfers between devices, home(): part = lax.all_to_all(part, 'gy', split_axis=0, concat_axis=0, tiled=True)  22.5 us
  transfers between devices with their start and end apart: 73, of which 33 were waited for; matrix products, arithmetic and copies ran while one was open for 29% of the time, Pallas kernels for 15%

profile of v1, /device:TPU:0, one launch (start us, length us, event | category | flops | bytes accessed | tf_op | source)
XLA Modules:
  0.0 712.4 jit_solution(1590362635587847132)
XLA Ops:
  15.6 5.3 all-to-all-start
  26.4 5.5 all-to-all-done
  36.7 4.3 all-to-all-start.1
  43.6 2.8 collective-permute-start.33
  48.5 24.2 %collective-permute-done.2 = f32[2,288]{1,0:T(2,128)S(1)} collective-permute-done((f32[2,288]{1,0:T(2,128)S(1)}, f32[2,288]{1,0:T(2,128)S(1)}, u32[]{:S(2)}, u32[]{:S(2)}) %collective-permute-start.2) | collective-permute-done | bytes 2336 | tf_op jit(solution)/shard_map/ppermute | solution.py:31
  91.6 5.1 collective-permute-done.31
  99.4 9.3 %collective-permute-done.32 = bf16[2,64,1536]{2,1,0:T(8,128)(2,1)S(1)} collective-permute-done((bf16[2,64,1536]{2,1,0:T(8,128)(2,1)S(1)}, bf16[2,64,1536]{2,1,0:T(8,128)(2,1)S(1)}, u32[]{:S(2)}, u32[]{:S(2)}) %collective-permute-start.32) | collective-permute-done | bytes 393248 | tf_op jit(solution)/shard_map/ppermute | solution.py:31
  119.3 10.5 %collective-permute-done.13 = bf16[320,1536]{1,0:T(8,128)(2,1)} collective-permute-done((bf16[320,1536]{1,0:T(8,128)(2,1)}, bf16[320,1536]{1,0:T(8,128)(2,1)}, u32[]{:S(2)}, u32[]{:S(2)}) %collective-permute-start.13) | collective-permute-done | bytes 983072 | tf_op jit(solution)/shard_map/ppermute | solution.py:31
  135.8 2.7 collective-permute-done.9
  140.4 7.0 collective-permute-done.15
  147.8 11.4 %collective-permute-done.17 = bf16[320,1536]{1,0:T(8,128)(2,1)} collective-permute-done((bf16[320,1536]{1,0:T(8,128)(2,1)}, bf16[320,1536]{1,0:T(8,128)(2,1)}, u32[]{:S(2)}, u32[]{:S(2)}) %collective-permute-start.17) | collective-permute-done | bytes 983072 | tf_op jit(solution)/shard_map/ppermute | solution.py:31
  161.0 2.7 fusion.32.media_ref
  167.9 2.6 fusion.31.media_ref
  180.9 3.6 pad.4
  184.5 4.7 copy.81.weights_ref
  190.7 6.6 shard_map.203
  200.2 6.6 shard_map.204
  209.7 6.6 shard_map.206
  220.0 6.6 shard_map.208
  229.6 7.3 %shard_map.210 = (bf16[2,320,1536]{2,1,0:T(8,128)(2,1)S(1)}, bf16[2,320,512]{2,1,0:T(8,128)(2,1)S(1)}, bf16[2,64,256]{2,1,0:T(8,128)(2,1)S(1)}, bf16[2,64,256]{2,1,0:T(8,128)(2,1)S(1)}, bf16[2,64,1536]{2,1,0:T(8,128)(2,1)S(1)}) custom-call(bf16[2,256,1536]{2,1,0:T(8,128)(2,1)S(1)} %copy-done.26, bf16[2,64,1536]{2,1,0:T(8,128)(2,1)S(1)} %copy-done.44, ...), custom_call_target="tpu_custom_call" | custom-call | flops 1509949440 | bytes 3932160 | tf_op jit(solution)/shard_map/pallas_call | solution.py:165
  243.0 6.5 shard_map.205
  253.8 17.0 %shard_map.209 = (bf16[2,320,1536]{2,1,0:T(8,128)(2,1)S(1)}, bf16[2,320,512]{2,1,0:T(8,128)(2,1)S(1)}, bf16[2,64,256]{2,1,0:T(8,128)(2,1)S(1)}, bf16[2,64,256]{2,1,0:T(8,128)(2,1)S(1)}, bf16[2,64,1536]{2,1,0:T(8,128)(2,1)S(1)}) custom-call(bf16[2,256,1536]{2,1,0:T(8,128)(2,1)S(1)} %copy-done.23, bf16[2,64,1536]{2,1,0:T(8,128)(2,1)S(1)} %copy-done.41, ...), custom_call_target="tpu_custom_call" | custom-call | flops 1509949440 | bytes 3932160 | tf_op jit(solution)/shard_map/pallas_call | solution.py:165
  275.0 6.5 shard_map.207
  294.0 8.5 %collective-permute-done.20 = bf16[2,64,1536]{2,1,0:T(8,128)(2,1)S(1)} collective-permute-done((bf16[2,64,1536]{2,1,0:T(8,128)(2,1)S(1)}, bf16[2,64,1536]{2,1,0:T(8,128)(2,1)S(1)}, u32[]{:S(2)}, u32[]{:S(2)}) %collective-permute-start.20) | collective-permute-done | bytes 393248 | tf_op jit(solution)/shard_map/ppermute | solution.py:31
  302.5 8.5 %collective-permute-done.22 = bf16[2,64,1536]{2,1,0:T(8,128)(2,1)S(1)} collective-permute-done((bf16[2,64,1536]{2,1,0:T(8,128)(2,1)S(1)}, bf16[2,64,1536]{2,1,0:T(8,128)(2,1)S(1)}, u32[]{:S(2)}, u32[]{:S(2)}) %collective-permute-start.22) | collective-permute-done | bytes 393248 | tf_op jit(solution)/shard_map/ppermute | solution.py:31
  317.7 9.4 %collective-permute-done.25 = bf16[2,64,1536]{2,1,0:T(8,128)(2,1)S(1)} collective-permute-done((bf16[2,64,1536]{2,1,0:T(8,128)(2,1)S(1)}, bf16[2,64,1536]{2,1,0:T(8,128)(2,1)S(1)}, u32[]{:S(2)}, u32[]{:S(2)}) %collective-permute-start.25) | collective-permute-done | bytes 393248 | tf_op jit(solution)/shard_map/ppermute | solution.py:31
  327.1 5.8 collective-permute-done.24
  337.8 7.5 %multiply_convert_fusion = (bf16[1024,768]{1,0:T(8,128)(2,1)}, f32[1024,768]{1,0:T(8,128)}) fusion(bf16[1024,1536]{1,0:T(8,128)(2,1)} %bitcast.40, bf16[1536,768]{1,0:T(8,128)(2,1)} %all-gather.6.cloned.1.call-done), kind=kOutput, calls=%fused_computation.27 | convolution fusion | flops 2419851264 | bytes 10223616 | tf_op jit(solution)/shard_map/dot_general | solution.py:18
  345.3 6.6 fusion.15
  353.1 6.0 convolution_convert_fusion.3
  364.9 4.5 convolution_convert_fusion
  372.7 2.9 convolution_convert_fusion.1
  378.0 3.9 convolution_convert_fusion.2
  392.4 4.0 collective-permute-done.36
  397.4 7.9 %collective-permute-done.38 = bf16[2,64,1536]{2,1,0:T(8,128)(2,1)S(1)} collective-permute-done((bf16[2,64,1536]{2,1,0:T(8,128)(2,1)S(1)}, bf16[2,64,1536]{2,1,0:T(8,128)(2,1)S(1)}, u32[]{:S(2)}, u32[]{:S(2)}) %collective-permute-start.38) | collective-permute-done | bytes 393248 | tf_op jit(solution)/shard_map/ppermute | solution.py:31
  407.8 5.5 collective-permute-done.28
  413.4 8.1 %collective-permute-done.30 = bf16[2,64,1536]{2,1,0:T(8,128)(2,1)S(1)} collective-permute-done((bf16[2,64,1536]{2,1,0:T(8,128)(2,1)S(1)}, bf16[2,64,1536]{2,1,0:T(8,128)(2,1)S(1)}, u32[]{:S(2)}, u32[]{:S(2)}) %collective-permute-start.30) | collective-permute-done | bytes 393248 | tf_op jit(solution)/shard_map/ppermute | solution.py:31
  427.8 9.4 %collective-permute-done.41 = bf16[2,64,1536]{2,1,0:T(8,128)(2,1)S(1)} collective-permute-done((bf16[2,64,1536]{2,1,0:T(8,128)(2,1)S(1)}, bf16[2,64,1536]{2,1,0:T(8,128)(2,1)S(1)}, u32[]{:S(2)}, u32[]{:S(2)}) %collective-permute-start.41) | collective-permute-done | bytes 393248 | tf_op jit(solution)/shard_map/ppermute | solution.py:31
  437.2 6.3 collective-permute-done.40
  447.3 5.7 shard_map.212
  455.6 5.3 shard_map.213
  462.5 5.3 shard_map.214
  469.4 5.3 shard_map.215
  476.3 5.3 shard_map.216
  483.4 5.3 shard_map.211
  491.3 5.4 shard_map.217
  498.8 5.6 shard_map.218
  520.4 3.0 convolution_bitcast_fusion
  531.6 7.8 %copy.71 = bf16[512,5120]{1,0:T(8,128)(2,1)} copy(bf16[512,5120]{0,1:T(8,128)(2,1)} %bitcast.310) | data formatting | bytes 10485760 | tf_op jit(solution)/shard_map/dot_general | solution.py:22
  539.3 13.2 %fusion.80 = bf16[1536,2,256]{0,2,1:T(8,128)(2,1)S(1)} fusion(bf16[5120,1536,1]{1,0,2:T(8,128)(2,1)} %bitcast.365, bf16[2,256,5120]{2,1,0:T(8,128)(2,1)} %bitcast.319), kind=kOutput, calls=%fused_computation.320 | convolution fusion | flops 8053063680 | bytes 22544384 | tf_op jit(solution)/shard_map/dot_general | solution.py:22
  555.4 3.2 pad_maximum_fusion
  563.7 3.6 all-to-all-start.3
  567.7 2.9 fusion.25
  579.4 18.6 %collective-permute-done.48 = bf16[320,1536]{1,0:T(8,128)(2,1)S(1)} collective-permute-done((bf16[320,1536]{1,0:T(8,128)(2,1)S(1)}, bf16[320,1536]{1,0:T(8,128)(2,1)S(1)}, u32[]{:S(2)}, u32[]{:S(2)}) %collective-permute-start.48) | collective-permute-done | bytes 983072 | tf_op jit(solution)/shard_map/ppermute | solution.py:31
  599.2 2.5 add_convert_fusion.5
  601.7 3.8 all-to-all-start.4
  607.6 3.1 add_convert_fusion.2
  613.9 15.3 %all-to-all-done.4 = bf16[8,48,768]{2,1,0:T(8,128)(2,1)S(1)} async-done(((bf16[8,48,768]{2,1,0:T(8,128)(2,1)}), bf16[8,48,768]{2,1,0:T(8,128)(2,1)S(1)}, u32[]{:S(2)}, u32[]{:S(2)}) %all-to-all-start.4) | async-done | bytes 589856 | tf_op jit(solution)/shard_map/all_to_all | solution.py:310
  630.4 26.8 %collective-permute-done.49 = bf16[320,1536]{1,0:T(8,128)(2,1)} collective-permute-done((bf16[320,1536]{1,0:T(8,128)(2,1)}, bf16[320,1536]{1,0:T(8,128)(2,1)}, u32[]{:S(2)}, u32[]{:S(2)}) %collective-permute-start.49) | collective-permute-done | bytes 983072 | tf_op jit(solution)/shard_map/ppermute | solution.py:31
  668.9 4.5 fusion.7
  677.7 4.1 collective-permute-done.60
  682.7 4.2 all-to-all-start.2
  686.9 2.6 fusion.46
  690.2 7.2 %all-to-all-done.2 = bf16[8,48,768]{2,1,0:T(8,128)(2,1)} async-done(((bf16[8,48,768]{2,1,0:T(8,128)(2,1)}), bf16[8,48,768]{2,1,0:T(8,128)(2,1)}, u32[]{:S(2)}, u32[]{:S(2)}) %all-to-all-start.2) | async-done | bytes 589856 | tf_op jit(solution)/shard_map/all_to_all | solution.py:310
  (667 shorter events, 255.7 us)
Async XLA Ops:
  15.6 16.2 %all-to-all-start = ((bf16[8,48,768]{2,1,0:T(8,128)(2,1)}), bf16[8,48,768]{2,1,0:T(8,128)(2,1)S(1)}, u32[]{:S(2)}, u32[]{:S(2)}) async-start(bf16[8,48,768]{2,1,0:T(8,128)(2,1)} %reshape.237), calls=%async_computation | async-start | bytes 1179648 | tf_op jit(solution)/shard_map/all_to_all | solution.py:255
  20.9 160.0 %all-gather.4.cloned.1.call-start = ((), (), s32[]{:S(2)}) async-start(), calls=%async_computation.8 | async-start | bytes 2949120 | tf_op jit(solution)/shard_map/all_gather | solution.py:256
  22.9 90.8 %collective-permute-start.11 = (bf16[320,1536]{1,0:T(8,128)(2,1)}, bf16[320,1536]{1,0:T(8,128)(2,1)}, u32[]{:S(2)}, u32[]{:S(2)}) collective-permute-start(bf16[320,1536]{1,0:T(8,128)(2,1)} %get-tuple-element.168), channel_id=1, source_target_pairs={{0,4},{1,5},{2,6},{3,7},{4,0},{5,1},{6,2},{7,3},{8,12},{9,13},{10,... | collective-permute-start | bytes 2949128 | tf_op jit(solution)/shard_map/ppermute | solution.py:31
  24.9 90.6 %collective-permute-start.7 = (bf16[320,1536]{1,0:T(8,128)(2,1)}, bf16[320,1536]{1,0:T(8,128)(2,1)}, u32[]{:S(2)}, u32[]{:S(2)}) collective-permute-start(bf16[320,1536]{1,0:T(8,128)(2,1)} %get-tuple-element.168), channel_id=1, source_target_pairs={{0,2},{1,3},{2,0},{3,1},{4,6},{5,7},{6,4},{7,5},{8,10},{9,11},{10,... | collective-permute-start | bytes 2949128 | tf_op jit(solution)/shard_map/ppermute | solution.py:31
  26.3 89.3 %collective-permute-start = (bf16[320,1536]{1,0:T(8,128)(2,1)}, bf16[320,1536]{1,0:T(8,128)(2,1)}, u32[]{:S(2)}, u32[]{:S(2)}) collective-permute-start(bf16[320,1536]{1,0:T(8,128)(2,1)} %get-tuple-element.168), channel_id=1, source_target_pairs={{0,1},{1,0},{2,3},{3,2},{4,5},{5,4},{6,7},{7,6},{8,9},{9,8},{10,11... | collective-permute-start | bytes 2949128 | tf_op jit(solution)/shard_map/ppermute | solution.py:31
  33.0 14.2 %collective-permute-start.1 = (f32[1,288]{1,0:T(1,128)S(1)}, f32[1,288]{1,0:T(1,128)S(1)}, u32[]{:S(2)}, u32[]{:S(2)}) collective-permute-start(f32[1,288]{1,0:T(1,128)S(1)} %reshape.235), channel_id=1, source_target_pairs={{0,1},{1,0},{2,3},{3,2},{4,5},{5,4},{6,7},{7,6},{8,9},{9,8},{10,11... | collective-permute-start | bytes 3464 | tf_op jit(solution)/shard_map/ppermute | solution.py:31
  36.7 44.3 %all-to-all-start.1 = ((bf16[8,2,48,768]{3,2,1,0:T(8,128)(2,1)}), bf16[8,2,48,768]{3,2,1,0:T(8,128)(2,1)}, u32[]{:S(2)}, u32[]{:S(2)}) async-start(bf16[8,2,48,768]{3,2,1,0:T(8,128)(2,1)} %copy.68), calls=%async_computation.1 | async-start | bytes 2359296 | tf_op jit(solution)/shard_map/all_to_all | solution.py:261
  41.0 296.8 %all-gather.6.cloned.1.call-start = ((), (), s32[]{:S(2)}) async-start(), calls=%async_computation.9 | async-start | bytes 2949120 | tf_op jit(solution)/shard_map/all_gather | solution.py:262
  43.6 55.2 %collective-permute-start.33 = (bf16[2,64,1536]{2,1,0:T(8,128)(2,1)S(1)}, bf16[2,64,1536]{2,1,0:T(8,128)(2,1)}, u32[]{:S(2)}, u32[]{:S(2)}) collective-permute-start(bf16[2,64,1536]{2,1,0:T(8,128)(2,1)S(1)} %get-tuple-element.158), channel_id=1, source_target_pairs={{0,6},{1,7},{2,4},{3,5},{4,2},{5,3},{6,0},{7,1},{8,14},{9,15},{10,... | collective-permute-start | bytes 1179656 | tf_op jit(solution)/shard_map/ppermute | solution.py:31
  47.3 25.4 %collective-permute-start.2 = (f32[2,288]{1,0:T(2,128)S(1)}, f32[2,288]{1,0:T(2,128)S(1)}, u32[]{:S(2)}, u32[]{:S(2)}) collective-permute-start(f32[2,288]{1,0:T(2,128)S(1)} %pad_maximum_fusion.27), channel_id=1, source_target_pairs={{0,2},{1,3},{2,0},{3,1},{4,6},{5,7},{6,4},{7,5},{8,10},{9,11},{10,... | collective-permute-start | bytes 6920 | tf_op jit(solution)/shard_map/ppermute | solution.py:31
  83.4 261.9 %all-gather.8.cloned.1.call-start = ((), (), s32[]{:S(2)}) async-start(), calls=%async_computation.10 | async-start | bytes 2949120 | tf_op jit(solution)/shard_map/all_gather | solution.py:263
  88.2 8.4 %collective-permute-start.31 = (bf16[2,64,1536]{2,1,0:T(8,128)(2,1)S(1)}, bf16[2,64,1536]{2,1,0:T(8,128)(2,1)S(1)}, u32[]{:S(2)}, u32[]{:S(2)}) collective-permute-start(bf16[2,64,1536]{2,1,0:T(8,128)(2,1)S(1)} %get-tuple-element.158), channel_id=1, source_target_pairs={{0,2},{1,3},{2,0},{3,1},{4,6},{5,7},{6,4},{7,5},{8,10},{9,11},{10,... | collective-permute-start | bytes 1179656 | tf_op jit(solution)/shard_map/ppermute | solution.py:31
  96.6 12.1 %collective-permute-start.32 = (bf16[2,64,1536]{2,1,0:T(8,128)(2,1)S(1)}, bf16[2,64,1536]{2,1,0:T(8,128)(2,1)S(1)}, u32[]{:S(2)}, u32[]{:S(2)}) collective-permute-start(bf16[2,64,1536]{2,1,0:T(8,128)(2,1)S(1)} %get-tuple-element.158), channel_id=1, source_target_pairs={{0,4},{1,5},{2,6},{3,7},{4,0},{5,1},{6,2},{7,3},{8,12},{9,13},{10,... | collective-permute-start | bytes 1179656 | tf_op jit(solution)/shard_map/ppermute | solution.py:31
  98.8 31.0 %collective-permute-start.13 = (bf16[320,1536]{1,0:T(8,128)(2,1)}, bf16[320,1536]{1,0:T(8,128)(2,1)}, u32[]{:S(2)}, u32[]{:S(2)}) collective-permute-start(bf16[320,1536]{1,0:T(8,128)(2,1)} %get-tuple-element.169), channel_id=1, source_target_pairs={{0,4},{1,5},{2,6},{3,7},{4,0},{5,1},{6,2},{7,3},{8,12},{9,13},{10,... | collective-permute-start | bytes 2949128 | tf_op jit(solution)/shard_map/ppermute | solution.py:31
  108.7 21.2 %collective-permute-start.6 = (bf16[320,1536]{1,0:T(8,128)(2,1)}, bf16[320,1536]{1,0:T(8,128)(2,1)S(1)}, u32[]{:S(2)}, u32[]{:S(2)}) collective-permute-start(bf16[320,1536]{1,0:T(8,128)(2,1)} %get-tuple-element.169), channel_id=1, source_target_pairs={{0,1},{1,0},{2,3},{3,2},{4,5},{5,4},{6,7},{7,6},{8,9},{9,8},{10,11... | collective-permute-start | bytes 2949128 | tf_op jit(solution)/shard_map/ppermute | solution.py:31
  113.7 24.9 %collective-permute-start.9 = (bf16[320,1536]{1,0:T(8,128)(2,1)}, bf16[320,1536]{1,0:T(8,128)(2,1)}, u32[]{:S(2)}, u32[]{:S(2)}) collective-permute-start(bf16[320,1536]{1,0:T(8,128)(2,1)} %get-tuple-element.169), channel_id=1, source_target_pairs={{0,2},{1,3},{2,0},{3,1},{4,6},{5,7},{6,4},{7,5},{8,10},{9,11},{10,... | collective-permute-start | bytes 2949128 | tf_op jit(solution)/shard_map/ppermute | solution.py:31
  115.4 18.6 %collective-permute-start.12 = (bf16[320,1536]{1,0:T(8,128)(2,1)}, bf16[320,1536]{1,0:T(8,128)(2,1)}, u32[]{:S(2)}, u32[]{:S(2)}) collective-permute-start(bf16[320,1536]{1,0:T(8,128)(2,1)} %collective-permute-done.11), channel_id=1, source_target_pairs={{0,1},{1,0},{2,3},{3,2},{4,5},{5,4},{6,7},{7,6},{8,9},{9,8},{10,11... | collective-permute-start | bytes 2949128 | tf_op jit(solution)/shard_map/ppermute | solution.py:31
  115.7 31.7 %collective-permute-start.15 = (bf16[320,1536]{1,0:T(8,128)(2,1)}, bf16[320,1536]{1,0:T(8,128)(2,1)}, u32[]{:S(2)}, u32[]{:S(2)}) collective-permute-start(bf16[320,1536]{1,0:T(8,128)(2,1)} %collective-permute-done.7), channel_id=1, source_target_pairs={{0,4},{1,5},{2,6},{3,7},{4,0},{5,1},{6,2},{7,3},{8,12},{9,13},{10,... | collective-permute-start | bytes 2949128 | tf_op jit(solution)/shard_map/ppermute | solution.py:31
  129.9 17.5 %collective-permute-start.8 = (bf16[320,1536]{1,0:T(8,128)(2,1)}, bf16[320,1536]{1,0:T(8,128)(2,1)}, u32[]{:S(2)}, u32[]{:S(2)}) collective-permute-start(bf16[320,1536]{1,0:T(8,128)(2,1)} %collective-permute-done.7), channel_id=1, source_target_pairs={{0,1},{1,0},{2,3},{3,2},{4,5},{5,4},{6,7},{7,6},{8,9},{9,8},{10,11... | collective-permute-start | bytes 2949128 | tf_op jit(solution)/shard_map/ppermute | solution.py:31
  129.9 29.4 %collective-permute-start.17 = (bf16[320,1536]{1,0:T(8,128)(2,1)}, bf16[320,1536]{1,0:T(8,128)(2,1)}, u32[]{:S(2)}, u32[]{:S(2)}) collective-permute-start(bf16[320,1536]{1,0:T(8,128)(2,1)} %collective-permute-done.13), channel_id=1, source_target_pairs={{0,2},{1,3},{2,0},{3,1},{4,6},{5,7},{6,4},{7,5},{8,10},{9,11},{10,... | collective-permute-start | bytes 2949128 | tf_op jit(solution)/shard_map/ppermute | solution.py:31
  133.7 430.0 %reduce-scatter.6.cloned.1.call-start = ((), (), s32[]{:S(2)}) async-start(), calls=%async_computation.12 | async-start | bytes 2949120 | tf_op jit(solution)/shard_map/reduce_scatter | solution.py:308
  134.0 29.7 %collective-permute-start.14 = (bf16[320,1536]{1,0:T(8,128)(2,1)}, bf16[320,1536]{1,0:T(8,128)(2,1)S(1)}, u32[]{:S(2)}, u32[]{:S(2)}) collective-permute-start(bf16[320,1536]{1,0:T(8,128)(2,1)} %collective-permute-done.13), channel_id=1, source_target_pairs={{0,1},{1,0},{2,3},{3,2},{4,5},{5,4},{6,7},{7,6},{8,9},{9,8},{10,11... | collective-permute-start | bytes 2949128 | tf_op jit(solution)/shard_map/ppermute | solution.py:31
  138.5 33.7 %collective-permute-start.34 = (bf16[4,2,64,1536]{3,2,1,0:T(8,128)(2,1)}, bf16[4,2,64,1536]{3,2,1,0:T(8,128)(2,1)S(1)}, u32[]{:S(2)}, u32[]{:S(2)}) collective-permute-start(bf16[4,2,64,1536]{3,2,1,0:T(8,128)(2,1)} %pad_maximum_fusion.3), channel_id=1, source_target_pairs={{0,1},{1,0},{2,3},{3,2},{4,5},{5,4},{6,7},{7,6},{8,9},{9,8},{10,11... | collective-permute-start | bytes 4718600 | tf_op jit(solution)/shard_map/ppermute | solution.py:31
  147.3 20.6 %collective-permute-start.10 = (bf16[320,1536]{1,0:T(8,128)(2,1)}, bf16[320,1536]{1,0:T(8,128)(2,1)S(1)}, u32[]{:S(2)}, u32[]{:S(2)}) collective-permute-start(bf16[320,1536]{1,0:T(8,128)(2,1)} %collective-permute-done.9), channel_id=1, source_target_pairs={{0,1},{1,0},{2,3},{3,2},{4,5},{5,4},{6,7},{7,6},{8,9},{9,8},{10,11... | collective-permute-start | bytes 2949128 | tf_op jit(solution)/shard_map/ppermute | solution.py:31
  147.3 25.0 %collective-permute-start.16 = (bf16[320,1536]{1,0:T(8,128)(2,1)}, bf16[320,1536]{1,0:T(8,128)(2,1)S(1)}, u32[]{:S(2)}, u32[]{:S(2)}) collective-permute-start(bf16[320,1536]{1,0:T(8,128)(2,1)} %collective-permute-done.15), channel_id=1, source_target_pairs={{0,1},{1,0},{2,3},{3,2},{4,5},{5,4},{6,7},{7,6},{8,9},{9,8},{10,11... | collective-permute-start | bytes 2949128 | tf_op jit(solution)/shard_map/ppermute | solution.py:31
  159.2 17.5 %collective-permute-start.18 = (bf16[320,1536]{1,0:T(8,128)(2,1)}, bf16[320,1536]{1,0:T(8,128)(2,1)S(1)}, u32[]{:S(2)}, u32[]{:S(2)}) collective-permute-start(bf16[320,1536]{1,0:T(8,128)(2,1)} %collective-permute-done.17), channel_id=1, source_target_pairs={{0,1},{1,0},{2,3},{3,2},{4,5},{5,4},{6,7},{7,6},{8,9},{9,8},{10,11... | collective-permute-start | bytes 2949128 | tf_op jit(solution)/shard_map/ppermute | solution.py:31
  283.9 6.0 collective-permute-start.19
  290.4 12.0 %collective-permute-start.20 = (bf16[2,64,1536]{2,1,0:T(8,128)(2,1)S(1)}, bf16[2,64,1536]{2,1,0:T(8,128)(2,1)S(1)}, u32[]{:S(2)}, u32[]{:S(2)}) collective-permute-start(bf16[2,64,1536]{2,1,0:T(8,128)(2,1)S(1)} %get-tuple-element.189), channel_id=1, source_target_pairs={{0,2},{1,3},{2,0},{3,1},{4,6},{5,7},{6,4},{7,5},{8,10},{9,11},{10,... | collective-permute-start | bytes 1179656 | tf_op jit(solution)/shard_map/ppermute | solution.py:31
  292.3 18.8 %collective-permute-start.22 = (bf16[2,64,1536]{2,1,0:T(8,128)(2,1)S(1)}, bf16[2,64,1536]{2,1,0:T(8,128)(2,1)S(1)}, u32[]{:S(2)}, u32[]{:S(2)}) collective-permute-start(bf16[2,64,1536]{2,1,0:T(8,128)(2,1)S(1)} %get-tuple-element.190), channel_id=1, source_target_pairs={{0,6},{1,7},{2,4},{3,5},{4,2},{5,3},{6,0},{7,1},{8,14},{9,15},{10,... | collective-permute-start | bytes 1179656 | tf_op jit(solution)/shard_map/ppermute | solution.py:31
  293.4 19.0 %collective-permute-start.21 = (bf16[2,64,1536]{2,1,0:T(8,128)(2,1)S(1)}, bf16[2,64,1536]{2,1,0:T(8,128)(2,1)S(1)}, u32[]{:S(2)}, u32[]{:S(2)}) collective-permute-start(bf16[2,64,1536]{2,1,0:T(8,128)(2,1)S(1)} %get-tuple-element.191), channel_id=1, source_target_pairs={{0,4},{1,5},{2,6},{3,7},{4,0},{5,1},{6,2},{7,3},{8,12},{9,13},{10,... | collective-permute-start | bytes 1179656 | tf_op jit(solution)/shard_map/ppermute | solution.py:31
  314.1 13.0 %collective-permute-start.25 = (bf16[2,64,1536]{2,1,0:T(8,128)(2,1)S(1)}, bf16[2,64,1536]{2,1,0:T(8,128)(2,1)S(1)}, u32[]{:S(2)}, u32[]{:S(2)}) collective-permute-start(bf16[2,64,1536]{2,1,0:T(8,128)(2,1)S(1)} %get-tuple-element.160), channel_id=1, source_target_pairs={{0,6},{1,7},{2,4},{3,5},{4,2},{5,3},{6,0},{7,1},{8,14},{9,15},{10,... | collective-permute-start | bytes 1179656 | tf_op jit(solution)/shard_map/ppermute | solution.py:31
  315.9 17.0 %collective-permute-start.24 = (bf16[2,64,1536]{2,1,0:T(8,128)(2,1)S(1)}, bf16[2,64,1536]{2,1,0:T(8,128)(2,1)S(1)}, u32[]{:S(2)}, u32[]{:S(2)}) collective-permute-start(bf16[2,64,1536]{2,1,0:T(8,128)(2,1)S(1)} %get-tuple-element.160), channel_id=1, source_target_pairs={{0,4},{1,5},{2,6},{3,7},{4,0},{5,1},{6,2},{7,3},{8,12},{9,13},{10,... | collective-permute-start | bytes 1179656 | tf_op jit(solution)/shard_map/ppermute | solution.py:31
  317.3 15.6 %collective-permute-start.23 = (bf16[2,64,1536]{2,1,0:T(8,128)(2,1)S(1)}, bf16[2,64,1536]{2,1,0:T(8,128)(2,1)S(1)}, u32[]{:S(2)}, u32[]{:S(2)}) collective-permute-start(bf16[2,64,1536]{2,1,0:T(8,128)(2,1)S(1)} %get-tuple-element.160), channel_id=1, source_target_pairs={{0,2},{1,3},{2,0},{3,1},{4,6},{5,7},{6,4},{7,5},{8,10},{9,11},{10,... | collective-permute-start | bytes 1179656 | tf_op jit(solution)/shard_map/ppermute | solution.py:31
  359.2 242.5 %reduce-scatter.8.cloned.1.call-start = ((), (), s32[]{:S(2)}) async-start(), calls=%async_computation.13 | async-start | bytes 2949120 | tf_op jit(solution)/shard_map/reduce_scatter | solution.py:308
  371.3 10.7 %collective-permute-start.35 = (bf16[4,2,64,1536]{3,2,1,0:T(8,128)(2,1)}, bf16[4,2,64,1536]{3,2,1,0:T(8,128)(2,1)}, u32[]{:S(2)}, u32[]{:S(2)}) collective-permute-start(bf16[4,2,64,1536]{3,2,1,0:T(8,128)(2,1)} %bitcast.58), channel_id=1, source_target_pairs={{0,1},{1,0},{2,3},{3,2},{4,5},{5,4},{6,7},{7,6},{8,9},{9,8},{10,11... | collective-permute-start | bytes 4718600 | tf_op jit(solution)/shard_map/ppermute | solution.py:31
  376.9 11.1 %collective-permute-start.27 = (bf16[4,2,64,1536]{3,2,1,0:T(8,128)(2,1)}, bf16[4,2,64,1536]{3,2,1,0:T(8,128)(2,1)}, u32[]{:S(2)}, u32[]{:S(2)}) collective-permute-start(bf16[4,2,64,1536]{3,2,1,0:T(8,128)(2,1)} %bitcast.46), channel_id=1, source_target_pairs={{0,1},{1,0},{2,3},{3,2},{4,5},{5,4},{6,7},{7,6},{8,9},{9,8},{10,11... | collective-permute-start | bytes 4718600 | tf_op jit(solution)/shard_map/ppermute | solution.py:31
  382.0 300.7 %reduce-scatter.4.cloned.1.call-start = ((), (), s32[]{:S(2)}) async-start(), calls=%async_computation.11 | async-start | bytes 2949120 | tf_op jit(solution)/shard_map/reduce_scatter | solution.py:308
  384.4 12.0 %collective-permute-start.36 = (bf16[2,64,1536]{2,1,0:T(8,128)(2,1)S(1)}, bf16[2,64,1536]{2,1,0:T(8,128)(2,1)S(1)}, u32[]{:S(2)}, u32[]{:S(2)}) collective-permute-start(bf16[2,64,1536]{2,1,0:T(8,128)(2,1)S(1)} %get-tuple-element.183), channel_id=1, source_target_pairs={{0,2},{1,3},{2,0},{3,1},{4,6},{5,7},{6,4},{7,5},{8,10},{9,11},{10,... | collective-permute-start | bytes 1179656 | tf_op jit(solution)/shard_map/ppermute | solution.py:31
  385.7 19.7 %collective-permute-start.38 = (bf16[2,64,1536]{2,1,0:T(8,128)(2,1)S(1)}, bf16[2,64,1536]{2,1,0:T(8,128)(2,1)S(1)}, u32[]{:S(2)}, u32[]{:S(2)}) collective-permute-start(bf16[2,64,1536]{2,1,0:T(8,128)(2,1)S(1)} %get-tuple-element.184), channel_id=1, source_target_pairs={{0,6},{1,7},{2,4},{3,5},{4,2},{5,3},{6,0},{7,1},{8,14},{9,15},{10,... | collective-permute-start | bytes 1179656 | tf_op jit(solution)/shard_map/ppermute | solution.py:31
  386.9 20.3 %collective-permute-start.37 = (bf16[2,64,1536]{2,1,0:T(8,128)(2,1)S(1)}, bf16[2,64,1536]{2,1,0:T(8,128)(2,1)S(1)}, u32[]{:S(2)}, u32[]{:S(2)}) collective-permute-start(bf16[2,64,1536]{2,1,0:T(8,128)(2,1)S(1)} %get-tuple-element.185), channel_id=1, source_target_pairs={{0,4},{1,5},{2,6},{3,7},{4,0},{5,1},{6,2},{7,3},{8,12},{9,13},{10,... | collective-permute-start | bytes 1179656 | tf_op jit(solution)/shard_map/ppermute | solution.py:31
  389.9 23.5 %collective-permute-start.28 = (bf16[2,64,1536]{2,1,0:T(8,128)(2,1)S(1)}, bf16[2,64,1536]{2,1,0:T(8,128)(2,1)S(1)}, u32[]{:S(2)}, u32[]{:S(2)}) collective-permute-start(bf16[2,64,1536]{2,1,0:T(8,128)(2,1)S(1)} %get-tuple-element.186), channel_id=1, source_target_pairs={{0,2},{1,3},{2,0},{3,1},{4,6},{5,7},{6,4},{7,5},{8,10},{9,11},{10,... | collective-permute-start | bytes 1179656 | tf_op jit(solution)/shard_map/ppermute | solution.py:31
  391.2 30.4 %collective-permute-start.30 = (bf16[2,64,1536]{2,1,0:T(8,128)(2,1)S(1)}, bf16[2,64,1536]{2,1,0:T(8,128)(2,1)S(1)}, u32[]{:S(2)}, u32[]{:S(2)}) collective-permute-start(bf16[2,64,1536]{2,1,0:T(8,128)(2,1)S(1)} %get-tuple-element.187), channel_id=1, source_target_pairs={{0,6},{1,7},{2,4},{3,5},{4,2},{5,3},{6,0},{7,1},{8,14},{9,15},{10,... | collective-permute-start | bytes 1179656 | tf_op jit(solution)/shard_map/ppermute | solution.py:31
  396.5 26.4 %collective-permute-start.29 = (bf16[2,64,1536]{2,1,0:T(8,128)(2,1)S(1)}, bf16[2,64,1536]{2,1,0:T(8,128)(2,1)S(1)}, u32[]{:S(2)}, u32[]{:S(2)}) collective-permute-start(bf16[2,64,1536]{2,1,0:T(8,128)(2,1)S(1)} %get-tuple-element.188), channel_id=1, source_target_pairs={{0,4},{1,5},{2,6},{3,7},{4,0},{5,1},{6,2},{7,3},{8,12},{9,13},{10,... | collective-permute-start | bytes 1179656 | tf_op jit(solution)/shard_map/ppermute | solution.py:31
  424.2 13.0 %collective-permute-start.41 = (bf16[2,64,1536]{2,1,0:T(8,128)(2,1)S(1)}, bf16[2,64,1536]{2,1,0:T(8,128)(2,1)S(1)}, u32[]{:S(2)}, u32[]{:S(2)}) collective-permute-start(bf16[2,64,1536]{2,1,0:T(8,128)(2,1)S(1)} %get-tuple-element.194), channel_id=1, source_target_pairs={{0,6},{1,7},{2,4},{3,5},{4,2},{5,3},{6,0},{7,1},{8,14},{9,15},{10,... | collective-permute-start | bytes 1179656 | tf_op jit(solution)/shard_map/ppermute | solution.py:31
  425.9 17.6 %collective-permute-start.40 = (bf16[2,64,1536]{2,1,0:T(8,128)(2,1)S(1)}, bf16[2,64,1536]{2,1,0:T(8,128)(2,1)S(1)}, u32[]{:S(2)}, u32[]{:S(2)}) collective-permute-start(bf16[2,64,1536]{2,1,0:T(8,128)(2,1)S(1)} %get-tuple-element.194), channel_id=1, source_target_pairs={{0,4},{1,5},{2,6},{3,7},{4,0},{5,1},{6,2},{7,3},{8,12},{9,13},{10,... | collective-permute-start | bytes 1179656 | tf_op jit(solution)/shard_map/ppermute | solution.py:31
  426.7 16.8 %collective-permute-start.39 = (bf16[2,64,1536]{2,1,0:T(8,128)(2,1)S(1)}, bf16[2,64,1536]{2,1,0:T(8,128)(2,1)S(1)}, u32[]{:S(2)}, u32[]{:S(2)}) collective-permute-start(bf16[2,64,1536]{2,1,0:T(8,128)(2,1)S(1)} %get-tuple-element.194), channel_id=1, source_target_pairs={{0,2},{1,3},{2,0},{3,1},{4,6},{5,7},{6,4},{7,5},{8,10},{9,11},{10,... | collective-permute-start | bytes 1179656 | tf_op jit(solution)/shard_map/ppermute | solution.py:31
  455.3 112.0 %collective-permute-start.44 = (bf16[320,1536]{1,0:T(8,128)(2,1)}, bf16[320,1536]{1,0:T(8,128)(2,1)}, u32[]{:S(2)}, u32[]{:S(2)}) collective-permute-start(bf16[320,1536]{1,0:T(8,128)(2,1)} %slice_bitcast_fusion.6), channel_id=1, source_target_pairs={{0,1},{1,0},{2,3},{3,2},{4,5},{5,4},{6,7},{7,6},{8,9},{9,8},{10,11... | collective-permute-start | bytes 2949128 | tf_op jit(solution)/shard_map/ppermute | solution.py:31
  462.0 117.4 %collective-permute-start.46 = (bf16[320,1536]{1,0:T(8,128)(2,1)}, bf16[320,1536]{1,0:T(8,128)(2,1)}, u32[]{:S(2)}, u32[]{:S(2)}) collective-permute-start(bf16[320,1536]{1,0:T(8,128)(2,1)} %slice_bitcast_fusion.5), channel_id=1, source_target_pairs={{0,1},{1,0},{2,3},{3,2},{4,5},{5,4},{6,7},{7,6},{8,9},{9,8},{10,11... | collective-permute-start | bytes 2949128 | tf_op jit(solution)/shard_map/ppermute | solution.py:31
  468.8 101.8 %collective-permute-start.47 = (bf16[320,1536]{1,0:T(8,128)(2,1)}, bf16[320,1536]{1,0:T(8,128)(2,1)}, u32[]{:S(2)}, u32[]{:S(2)}) collective-permute-start(bf16[320,1536]{1,0:T(8,128)(2,1)} %slice_bitcast_fusion.4), channel_id=1, source_target_pairs={{0,1},{1,0},{2,3},{3,2},{4,5},{5,4},{6,7},{7,6},{8,9},{9,8},{10,11... | collective-permute-start | bytes 2949128 | tf_op jit(solution)/shard_map/ppermute | solution.py:31
  475.8 183.8 %collective-permute-start.50 = (bf16[320,1536]{1,0:T(8,128)(2,1)}, bf16[320,1536]{1,0:T(8,128)(2,1)}, u32[]{:S(2)}, u32[]{:S(2)}) collective-permute-start(bf16[320,1536]{1,0:T(8,128)(2,1)} %slice_bitcast_fusion.3), channel_id=1, source_target_pairs={{0,1},{1,0},{2,3},{3,2},{4,5},{5,4},{6,7},{7,6},{8,9},{9,8},{10,11... | collective-permute-start | bytes 2949128 | tf_op jit(solution)/shard_map/ppermute | solution.py:31
  482.7 92.9 %collective-permute-start.51 = (bf16[320,1536]{1,0:T(8,128)(2,1)}, bf16[320,1536]{1,0:T(8,128)(2,1)}, u32[]{:S(2)}, u32[]{:S(2)}) collective-permute-start(bf16[320,1536]{1,0:T(8,128)(2,1)} %slice_bitcast_fusion.2), channel_id=1, source_target_pairs={{0,1},{1,0},{2,3},{3,2},{4,5},{5,4},{6,7},{7,6},{8,9},{9,8},{10,11... | collective-permute-start | bytes 2949128 | tf_op jit(solution)/shard_map/ppermute | solution.py:31
  563.7 38.0 %all-to-all-start.3 = ((bf16[8,48,768]{2,1,0:T(8,128)(2,1)}), bf16[8,48,768]{2,1,0:T(8,128)(2,1)S(1)}, u32[]{:S(2)}, u32[]{:S(2)}) async-start(bf16[8,48,768]{2,1,0:T(8,128)(2,1)} %bitcast.361), calls=%async_computation.5 | async-start | bytes 1179648 | tf_op jit(solution)/shard_map/all_to_all | solution.py:310
  570.6 34.9 %collective-permute-start.53 = (bf16[320,1536]{1,0:T(8,128)(2,1)}, bf16[320,1536]{1,0:T(8,128)(2,1)}, u32[]{:S(2)}, u32[]{:S(2)}) collective-permute-start(bf16[320,1536]{1,0:T(8,128)(2,1)} %slice_bitcast_fusion.1), channel_id=1, source_target_pairs={{0,1},{1,0},{2,3},{3,2},{4,5},{5,4},{6,7},{7,6},{8,9},{9,8},{10,11... | collective-permute-start | bytes 2949128 | tf_op jit(solution)/shard_map/ppermute | solution.py:31
  572.3 25.8 %collective-permute-start.48 = (bf16[320,1536]{1,0:T(8,128)(2,1)S(1)}, bf16[320,1536]{1,0:T(8,128)(2,1)S(1)}, u32[]{:S(2)}, u32[]{:S(2)}) collective-permute-start(bf16[320,1536]{1,0:T(8,128)(2,1)S(1)} %fusion.23), channel_id=1, source_target_pairs={{0,4},{1,5},{2,6},{3,7},{4,0},{5,1},{6,2},{7,3},{8,12},{9,13},{10,... | collective-permute-start | bytes 2949128 | tf_op jit(solution)/shard_map/ppermute | solution.py:31
  575.5 32.0 %collective-permute-start.55 = (bf16[320,1536]{1,0:T(8,128)(2,1)}, bf16[320,1536]{1,0:T(8,128)(2,1)}, u32[]{:S(2)}, u32[]{:S(2)}) collective-permute-start(bf16[320,1536]{1,0:T(8,128)(2,1)} %fusion.19), channel_id=1, source_target_pairs={{0,2},{1,3},{2,0},{3,1},{4,6},{5,7},{6,4},{7,5},{8,10},{9,11},{10,... | collective-permute-start | bytes 2949128 | tf_op jit(solution)/shard_map/ppermute | solution.py:31
  579.4 31.3 %collective-permute-start.43 = (bf16[320,1536]{1,0:T(8,128)(2,1)}, bf16[320,1536]{1,0:T(8,128)(2,1)}, u32[]{:S(2)}, u32[]{:S(2)}) collective-permute-start(bf16[320,1536]{1,0:T(8,128)(2,1)} %slice_bitcast_fusion.7), channel_id=1, source_target_pairs={{0,1},{1,0},{2,3},{3,2},{4,5},{5,4},{6,7},{7,6},{8,9},{9,8},{10,11... | collective-permute-start | bytes 2949128 | tf_op jit(solution)/shard_map/ppermute | solution.py:31
  598.0 32.4 %collective-permute-start.45 = (bf16[320,1536]{1,0:T(8,128)(2,1)}, bf16[320,1536]{1,0:T(8,128)(2,1)}, u32[]{:S(2)}, u32[]{:S(2)}) collective-permute-start(bf16[320,1536]{1,0:T(8,128)(2,1)} %fusion.25), channel_id=1, source_target_pairs={{0,4},{1,5},{2,6},{3,7},{4,0},{5,1},{6,2},{7,3},{8,12},{9,13},{10,... | collective-permute-start | bytes 2949128 | tf_op jit(solution)/shard_map/ppermute | solution.py:31
  601.7 27.5 %all-to-all-start.4 = ((bf16[8,48,768]{2,1,0:T(8,128)(2,1)}), bf16[8,48,768]{2,1,0:T(8,128)(2,1)S(1)}, u32[]{:S(2)}, u32[]{:S(2)}) async-start(bf16[8,48,768]{2,1,0:T(8,128)(2,1)} %bitcast.362), calls=%async_computation.7 | async-start | bytes 1179648 | tf_op jit(solution)/shard_map/all_to_all | solution.py:310
  605.5 54.0 %collective-permute-start.52 = (bf16[320,1536]{1,0:T(8,128)(2,1)}, bf16[320,1536]{1,0:T(8,128)(2,1)}, u32[]{:S(2)}, u32[]{:S(2)}) collective-permute-start(bf16[320,1536]{1,0:T(8,128)(2,1)} %fusion.21), channel_id=1, source_target_pairs={{0,2},{1,3},{2,0},{3,1},{4,6},{5,7},{6,4},{7,5},{8,10},{9,11},{10,... | collective-permute-start | bytes 2949128 | tf_op jit(solution)/shard_map/ppermute | solution.py:31
  607.5 49.6 %collective-permute-start.49 = (bf16[320,1536]{1,0:T(8,128)(2,1)}, bf16[320,1536]{1,0:T(8,128)(2,1)}, u32[]{:S(2)}, u32[]{:S(2)}) collective-permute-start(bf16[320,1536]{1,0:T(8,128)(2,1)} %add_convert_fusion.5), channel_id=1, source_target_pairs={{0,2},{1,3},{2,0},{3,1},{4,6},{5,7},{6,4},{7,5},{8,10},{9,11},{10,... | collective-permute-start | bytes 2949128 | tf_op jit(solution)/shard_map/ppermute | solution.py:31
  610.8 48.8 %collective-permute-start.56 = (bf16[320,1536]{1,0:T(8,128)(2,1)}, bf16[320,1536]{1,0:T(8,128)(2,1)}, u32[]{:S(2)}, u32[]{:S(2)}) collective-permute-start(bf16[320,1536]{1,0:T(8,128)(2,1)} %add_convert_fusion.2), channel_id=1, source_target_pairs={{0,4},{1,5},{2,6},{3,7},{4,0},{5,1},{6,2},{7,3},{8,12},{9,13},{10,... | collective-permute-start | bytes 2949128 | tf_op jit(solution)/shard_map/ppermute | solution.py:31
  668.4 5.0 collective-permute-start.58
  681.7 7.8 %collective-permute-start.61 = (f32[6,1536]{1,0:T(8,128)S(1)}, f32[6,1536]{1,0:T(8,128)S(1)}, u32[]{:S(2)}, u32[]{:S(2)}) collective-permute-start(f32[6,1536]{1,0:T(8,128)S(1)} %add.209), channel_id=1, source_target_pairs={{0,16},{8,24},{16,0},{24,8},{1,17},{9,25},{17,1},{25,9},{2,18},{10... | collective-permute-start | bytes 110600 | tf_op jit(solution)/shard_map/ppermute | solution.py:31
  682.7 14.7 %all-to-all-start.2 = ((bf16[8,48,768]{2,1,0:T(8,128)(2,1)}), bf16[8,48,768]{2,1,0:T(8,128)(2,1)}, u32[]{:S(2)}, u32[]{:S(2)}) async-start(bf16[8,48,768]{2,1,0:T(8,128)(2,1)} %bitcast.363), calls=%async_computation.3 | async-start | bytes 1179648 | tf_op jit(solution)/shard_map/all_to_all | solution.py:310
  (166 other events, 1314.8 us)
Sparse Core Ops, SparseCore 0:
  33.0 49.6 all-gather.3
  84.3 49.8 all-gather.5
  135.7 49.2 all-gather.7
  359.3 46.8 reduce-scatter.5
  408.4 47.5 reduce-scatter.7
  561.0 47.1 reduce-scatter.3

commit v2 on v1

v2 whole, which is shorter than its diff:
```python
import functools
import math

import jax
import jax.numpy as jnp
from jax import lax
from jax.experimental import pallas as pl
from jax.experimental.pallas import tpu as pltpu
from jax.sharding import PartitionSpec as P

HEAD = 96
EPSILON = 1e-05
BF16 = jnp.bfloat16
F32 = jnp.float32
VMEM = 56 * 2**20
LITTLE = pl.CostEstimate(flops=1024, bytes_accessed=1024, transcendentals=0)


def product(left, right):
    return jnp.dot(left, right, preferred_element_type=F32)


def product_left(left, right):
    return lax.dot_general(left, right, (((0,), (0,)), ((), ())), preferred_element_type=F32)


def product_right(left, right):
    return lax.dot_general(left, right, (((1,), (1,)), ((), ())), preferred_element_type=F32)


def tie(*values):
    return lax.optimization_barrier(values)


def swap(block, mask, axis="gy"):
    count = lax.axis_size(axis)
    return lax.ppermute(block, axis, [(i, i ^ mask) for i in range(count)])


def far_masks():
    return [mask for mask in range(lax.axis_size("gy")) if mask % 2 == 0]


def spread(block):
    return {mask: swap(block, mask) if mask else block for mask in far_masks()}


def regroup_kernel(*refs):
    first_ref, *from_refs, to_ref = refs
    cols = from_refs[0].shape[1] // to_ref.shape[0]
    extra = first_ref.shape[0]
    for device in range(to_ref.shape[0]):
        to_ref[device, :extra] = first_ref[...]
        to_ref[device, extra:] = jnp.concatenate(
            [from_ref[:, device * cols : (device + 1) * cols] for from_ref in from_refs], axis=1
        )


def regroup(first, devices, *weights):
    shard, width = weights[0].shape
    return pl.pallas_call(
        regroup_kernel,
        out_shape=jax.ShapeDtypeStruct((devices, first.shape[0] + shard, first.shape[1]), BF16),
        compiler_params=pltpu.CompilerParams(vmem_limit_bytes=VMEM),
        cost_estimate=LITTLE,
    )(first, *weights)


def ungroup_kernel(from_ref, *to_refs):
    devices, _, width = from_ref.shape
    cols = width // len(to_refs)
    for index, to_ref in enumerate(to_refs):
        to_ref[...] = jnp.concatenate(
            [from_ref[device, :, index * cols : (index + 1) * cols] for device in range(devices)], axis=1
        ).astype(F32)


def ungroup(blocks, count):
    devices, shard, width = blocks.shape
    return pl.pallas_call(
        ungroup_kernel,
        out_shape=[jax.ShapeDtypeStruct((shard, devices * width // count), F32)] * count,
        compiler_params=pltpu.CompilerParams(vmem_limit_bytes=VMEM),
        cost_estimate=LITTLE,
    )(blocks)


def bits_of(count):
    bits, bit = [], 1
    while bit < count:
        bits.append(bit)
        bit *= 2
    return bits


def gather_small(rows, axis):
    place = lax.axis_index(axis)
    for bit in bits_of(lax.axis_size(axis)):
        other = swap(rows, bit, axis)
        upper = (place & bit) != 0
        rows = jnp.concatenate([jnp.where(upper, other, rows), jnp.where(upper, rows, other)])
    return rows


def sum_small(rows, axis):
    for bit in bits_of(lax.axis_size(axis)):
        rows = rows + swap(rows, bit, axis)
    return rows


def normed(rows, gain, bias):
    average = jnp.mean(rows, axis=-1, keepdims=True)
    centred = rows - average
    spread_of = jnp.mean(centred * centred, axis=-1, keepdims=True)
    return centred * lax.rsqrt(spread_of + EPSILON) * gain + bias


def head_mask(rows, lanes, start):
    lane = lax.broadcasted_iota(jnp.int32, (rows, lanes), 1)
    return (lane >= start) & (lane < start + HEAD)


def stacked(rows, heads, start):
    count, lanes = rows.shape
    return jnp.concatenate(
        [jnp.where(head_mask(count, lanes, start + h * HEAD), rows, jnp.zeros_like(rows)) for h in range(heads)]
    )


def unstacked(rows, heads, start):
    count, lanes = rows.shape[0] // heads, rows.shape[1]
    total = jnp.zeros((count, lanes), rows.dtype)
    for h in range(heads):
        total = jnp.where(head_mask(count, lanes, start + h * HEAD), rows[h * count : (h + 1) * count], total)
    return total


def softmax_rows(scores):
    top = jnp.max(scores, axis=-1, keepdims=True)
    raised = jnp.exp(scores - top)
    return raised / jnp.sum(raised, axis=-1, keepdims=True)


def norm_kernel(patch, rows, raw_ref, small_ref, *refs):
    joined_ref = refs[-1]
    media = normed(raw_ref[0, :patch].astype(F32), small_ref[0, 0:1], small_ref[1, 0:1])
    latent = normed(raw_ref[0, patch:rows].astype(F32), small_ref[0, 1:2], small_ref[1, 1:2])
    joined_ref[0, :patch] = media.astype(BF16)
    joined_ref[0, patch:] = latent.astype(BF16)


def norm_rows(slot, raw, small, patch, rows, total, carried):
    width = raw.shape[2]
    given = [] if carried is None else [carried]
    return pl.pallas_call(
        functools.partial(norm_kernel, patch, rows),
        grid=(1,),
        in_specs=[pl.BlockSpec(raw.shape, lambda i: (0, 0, 0)), pl.BlockSpec(small.shape, lambda i: (0, 0, 0))]
        + [pl.BlockSpec(memory_space=pl.ANY)] * len(given),
        out_specs=pl.BlockSpec((1, rows, width), lambda i: (slot, 0, 0)),
        out_shape=jax.ShapeDtypeStruct((total, rows, width), BF16),
        input_output_aliases={2 + i: i for i in range(len(given))},
        compiler_params=pltpu.CompilerParams(vmem_limit_bytes=VMEM),
        cost_estimate=LITTLE,
    )(raw, small, *given)


def attend_kernel(heads, patch, scale, given, joined_ref, mine_ref, theirs_ref, *refs):
    kv_ref, qm_ref, *out_refs = refs[given:]
    cols = mine_ref.shape[1] // 2
    count, rows, width = joined_ref.shape
    lat = rows - patch
    joined = joined_ref[...].reshape(count * rows, width)
    latent = joined_ref[:, patch:].reshape(count * lat, width)
    total = None
    for index, weights_ref in enumerate((mine_ref, theirs_ref)):
        place = slice(index * cols, (index + 1) * cols)
        kv = product(joined, weights_ref[:, :cols]).astype(BF16).reshape(count, rows, cols)
        query = (product(latent, weights_ref[:, cols:]) * scale).astype(BF16).reshape(count, lat, cols)
        kv_ref[:, :, place] = kv
        mixed = []
        for image in range(count):
            probs = softmax_rows(product_right(stacked(query[image], heads, 0), kv[image]))
            mixed.append(unstacked(product(probs.astype(BF16), kv[image]), heads, heads * HEAD).astype(BF16))
        mixed = jnp.concatenate(mixed)
        lane = lax.broadcasted_iota(jnp.int32, mixed.shape, 1)
        qm = jnp.where(lane < heads * HEAD, query.reshape(count * lat, cols), mixed)
        qm_ref[:, :, place] = qm.reshape(count, lat, cols)
        term = product_right(mixed, weights_ref[:, cols:])
        total = term if total is None else total + term
    total = total.astype(BF16).reshape(count, lat, width)
    for index, out_ref in enumerate(out_refs):

        @pl.when(pl.program_id(0) == index // count)
        def _(out_ref=out_ref, image=index % count):
            out_ref[0] = total[image]


def attend(joined, mine, theirs, heads, patch, first, steps, per, carried):
    total, rows, width = joined.shape
    lat, cols = rows - patch, mine.shape[1]
    whole = lambda shape: pl.BlockSpec(shape, lambda i: (0,) * len(shape))
    part = lambda *shape: pl.BlockSpec((per,) + shape, lambda i: (i + first, 0, 0))
    given = list(carried or ())
    return pl.pallas_call(
        functools.partial(attend_kernel, heads, patch, HEAD ** (-0.5), len(given)),
        grid=(steps,),
        in_specs=[part(rows, width), whole(mine.shape), whole(theirs.shape)]
        + [pl.BlockSpec(memory_space=pl.ANY)] * len(given),
        out_specs=[part(rows, cols), part(lat, cols)] + [whole((1, lat, width))] * (steps * per),
        out_shape=[
            jax.ShapeDtypeStruct((total, rows, cols), BF16),
            jax.ShapeDtypeStruct((total, lat, cols), BF16),
        ]
        + [jax.ShapeDtypeStruct((1, lat, width), BF16)] * (steps * per),
        input_output_aliases={3 + i: i for i in range(len(given))},
        compiler_params=pltpu.CompilerParams(vmem_limit_bytes=VMEM),
        cost_estimate=LITTLE,
    )(joined, mine, theirs, *given)


def attend_back_kernel(heads, patch, scale, given, branch_ref, kv_ref, qm_ref, mine_ref, theirs_ref, *refs):
    dkv_ref, dquery_ref, *back_refs = refs[given:]
    cols = mine_ref.shape[1] // 2
    count, lat, width = branch_ref.shape
    rows = kv_ref.shape[1]
    branch = branch_ref[...].reshape(count * lat, width)
    back, extra = None, None
    for index, weights_ref in enumerate((mine_ref, theirs_ref)):
        place = slice(index * cols, (index + 1) * cols)
        all_mixed = product(branch, weights_ref[:, cols:]).astype(BF16)
        for image in range(count):
            kv = kv_ref[image, :, place]
            query = stacked(qm_ref[image, :, place], heads, 0)
            probs = softmax_rows(product_right(query, kv))
            grad_mixed = stacked(all_mixed[image * lat : (image + 1) * lat], heads, heads * HEAD)
            grad_probs = product_right(grad_mixed, kv)
            inner = jnp.sum(grad_probs * probs, axis=-1, keepdims=True)
            grad_scores = (probs * (grad_probs - inner)).astype(BF16)
            dquery_ref[image, :, place] = unstacked(product(grad_scores, kv), heads, 0).astype(BF16)
            dkv_ref[image, :, place] = product_left(
                jnp.concatenate([grad_scores, probs.astype(BF16)]), jnp.concatenate([query, grad_mixed])
            ).astype(BF16)
        term = product_right(dkv_ref[:, :, place].reshape(count * rows, cols), weights_ref[:, :cols])
        more = product_right(dquery_ref[:, :, place].reshape(count * lat, cols), weights_ref[:, cols:]) * scale
        back = term if back is None else back + term
        extra = more if extra is None else extra + more
    back = back.reshape(count, rows, width)
    extra = extra.reshape(count, lat, width)
    for index, back_ref in enumerate(back_refs):

        @pl.when(pl.program_id(0) == index // count)
        def _(back_ref=back_ref, image=index % count):
            back_ref[0, :patch] = back[image, :patch].astype(BF16)
            back_ref[0, patch:] = (back[image, patch:] + extra[image]).astype(BF16)


def attend_back(first, steps, per, branch, kv, qm, mine, theirs, heads, patch, carried):
    total, rows, cols = kv.shape
    lat, width = branch.shape[1:]
    whole = lambda shape: pl.BlockSpec(shape, lambda i: (0,) * len(shape))
    part = lambda *shape: pl.BlockSpec((per,) + shape, lambda i: (first - i, 0, 0))
    given = list(carried or ())
    return pl.pallas_call(
        functools.partial(attend_back_kernel, heads, patch, HEAD ** (-0.5), len(given)),
        grid=(steps,),
        in_specs=[part(lat, width), part(rows, cols), part(lat, cols), whole(mine.shape), whole(theirs.shape)]
        + [pl.BlockSpec(memory_space=pl.ANY)] * len(given),
        out_specs=[part(rows, cols), part(lat, cols)] + [whole((1, rows, width))] * (steps * per),
        out_shape=[
            jax.ShapeDtypeStruct((total, rows, cols), BF16),
            jax.ShapeDtypeStruct((total, lat, cols), BF16),
        ]
        + [jax.ShapeDtypeStruct((1, rows, width), BF16)] * (steps * per),
        input_output_aliases={5 + i: i for i in range(len(given))},
        compiler_params=pltpu.CompilerParams(vmem_limit_bytes=VMEM),
        cost_estimate=LITTLE,
    )(branch, kv, qm, mine, theirs, *given)


def feed_kernel(tile, hidden_ref, cot_ref, mine_ref, theirs_ref, active_ref, upper_ref, *refs):
    *part_refs, total_ref = refs
    half = mine_ref.shape[1] // 2
    hidden, cot = hidden_ref[...], cot_ref[...]
    for index, weights_ref in enumerate((mine_ref, theirs_ref)):
        for start in range(0, half, tile):
            up = weights_ref[:, start : start + tile]
            down = weights_ref[:, half + start : half + start + tile]
            upper = product(hidden, up)
            cdf = 0.5 * (1.0 + lax.erf(upper * (0.5**0.5)))
            slope = cdf + upper * jnp.exp(-0.5 * upper * upper) * (0.5 / math.pi) ** 0.5
            grad_upper = (slope * product(cot, down)).astype(BF16)
            place = slice(index * half + start, index * half + start + tile)
            active_ref[:, place] = (upper * cdf).astype(BF16)
            upper_ref[:, place] = grad_upper
            term = product_right(grad_upper, up)
            if index == 0 and start == 0:
                total_ref[...] = term
            else:
                total_ref[...] += term
    rows = part_refs[0].shape[0]
    for index, part_ref in enumerate(part_refs):
        part_ref[...] = total_ref[index * rows : (index + 1) * rows].astype(BF16)


def feed(hidden, cot, mine, theirs, parts):
    rows, width = hidden.shape
    cols = mine.shape[1]
    whole = lambda shape: pl.BlockSpec(shape, lambda i: (0,) * len(shape))
    return pl.pallas_call(
        functools.partial(feed_kernel, math.gcd(cols // 2, 384)),
        grid=(1,),
        in_specs=[whole(hidden.shape), whole(cot.shape), whole(mine.shape), whole(theirs.shape)],
        out_specs=[whole((rows, cols))] * 2 + [whole((rows // parts, width))] * parts,
        out_shape=[jax.ShapeDtypeStruct((rows, cols), BF16)] * 2
        + [jax.ShapeDtypeStruct((rows // parts, width), BF16)] * parts,
        scratch_shapes=[pltpu.VMEM((rows, width), F32)],
        compiler_params=pltpu.CompilerParams(vmem_limit_bytes=VMEM),
        cost_estimate=LITTLE,
    )(hidden, cot, mine, theirs)


def feed_grads_kernel(hidden_ref, cot_ref, upper_ref, active_ref, *refs):
    *given_ref, to_ref = refs
    half = upper_ref.shape[1]
    for index, (left_ref, right_ref) in enumerate(((hidden_ref, upper_ref), (cot_ref, active_ref))):
        place = slice(index * half, (index + 1) * half)
        term = product_left(left_ref[...], right_ref[...])
        if given_ref:
            term = term + given_ref[0][:, place].astype(F32)
        to_ref[:, place] = term.astype(BF16)


def row_tiles(width):
    return width // math.gcd(width, 384)


def feed_grads(hidden, cot, upper, active, which, given=None):
    rows, width = hidden.shape
    half = upper.shape[1] // 2
    steps = row_tiles(width)
    left = pl.BlockSpec((rows, width // steps), lambda i: (0, i))
    right = pl.BlockSpec((rows, half), lambda i: (0, which))
    tile = pl.BlockSpec((width // steps, 2 * half), lambda i: (i, 0))
    more = [] if given is None else [given]
    return pl.pallas_call(
        feed_grads_kernel,
        grid=(steps,),
        in_specs=[left, left, right, right] + [tile] * len(more),
        out_specs=tile,
        out_shape=jax.ShapeDtypeStruct((width, 2 * half), BF16),
        compiler_params=pltpu.CompilerParams(vmem_limit_bytes=VMEM),
        cost_estimate=LITTLE,
    )(hidden, cot, upper, active, *more)


def attend_grads_kernel(heads, patch, scale, which, joined_ref, branch_ref, dkv_ref, dquery_ref, qm_ref, *refs):
    *given_refs, kv_ref, qo_ref = refs
    count, rows, tile = joined_ref.shape
    cols = kv_ref.shape[1]
    place = slice(which * cols, (which + 1) * cols)
    joined = joined_ref[...].reshape(count * rows, tile)
    latent = joined_ref[:, patch:].reshape(count * (rows - patch), tile)
    kv = product_left(joined, dkv_ref[:, :, place].reshape(count * rows, cols))
    query = product_left(latent, dquery_ref[:, :, place].reshape(latent.shape[0], cols)) * scale
    out = product_left(branch_ref[...], qm_ref[:, :, place].reshape(latent.shape[0], cols))
    lane = lax.broadcasted_iota(jnp.int32, out.shape, 1)
    qo = jnp.where(lane < heads * HEAD, query, out)
    if given_refs:
        kv = kv + given_refs[0][...].astype(F32)
        qo = qo + given_refs[1][...].astype(F32)
    kv_ref[...] = kv.astype(BF16)
    qo_ref[...] = qo.astype(BF16)


def attend_grads(joined, branch, dkv, dquery, qm, heads, patch, which, given=()):
    total, rows, width = joined.shape
    lat, cols = rows - patch, dkv.shape[2] // 2
    steps = row_tiles(width)
    half = lambda count: pl.BlockSpec((total, count, 2 * cols), lambda i: (0, 0, 0))
    tile = pl.BlockSpec((width // steps, cols), lambda i: (i, 0))
    return pl.pallas_call(
        functools.partial(attend_grads_kernel, heads, patch, HEAD ** (-0.5), which),
        grid=(steps,),
        in_specs=[
            pl.BlockSpec((total, rows, width // steps), lambda i: (0, 0, i)),
            pl.BlockSpec((total * lat, width // steps), lambda i: (0, i)),
            half(rows), half(lat), half(lat),
        ]
        + [tile] * len(given),
        out_specs=[tile] * 2,
        out_shape=[jax.ShapeDtypeStruct((width, cols), BF16)] * 2,
        compiler_params=pltpu.CompilerParams(vmem_limit_bytes=VMEM),
        cost_estimate=LITTLE,
    )(joined, branch, dkv, dquery, qm, *given)


def norm_back(rows, gain, grad):
    average = jnp.mean(rows, axis=-1, keepdims=True)
    centred = rows - average
    inverse = lax.rsqrt(jnp.mean(centred * centred, axis=-1, keepdims=True) + EPSILON)
    unit = centred * inverse
    scaled = grad * gain
    first = jnp.mean(scaled, axis=-1, keepdims=True)
    second = jnp.mean(scaled * unit, axis=-1, keepdims=True)
    back = inverse * (scaled - first - unit * second)
    axes = tuple(range(rows.ndim - 1))
    return back, jnp.sum(grad * unit, axis=axes), jnp.sum(grad, axis=axes)


def in_thirds(values):
    parts, rest = [], values
    for _ in range(3):
        part = lax.reduce_precision(rest, exponent_bits=8, mantissa_bits=7)
        parts.append(part.astype(BF16))
        rest = rest - part
    return jnp.stack(parts)


def local(media_features, latents, cotangent, image_counts, w_query, w_key, w_value, w_out, w_up, w_down,
          norm_gains, norm_biases):
    devices_x, devices_y = lax.axis_size("gx"), lax.axis_size("gy")
    masks = far_masks()
    img_count, lat, width = latents.shape
    patch = media_features.shape[1]
    rows = patch + lat
    shard = w_query.shape[0]
    head_width = width // devices_y
    heads = head_width // HEAD
    ff_width = w_up.shape[1] // devices_y
    total = img_count * len(masks)

    four_width = 4 * head_width
    small = in_thirds(jnp.stack([norm_gains, norm_biases])).reshape(-1)
    extra = -(-small.size // (16 * four_width)) * 16
    small = jnp.pad(small, (0, extra * four_width - small.size)).reshape(extra, four_width)
    four = regroup(small, devices_y, w_key, w_value, w_query, w_out.T)
    four = lax.all_to_all(four, "gy", split_axis=0, concat_axis=0, tiled=True)
    mine = lax.all_gather(four[:, extra:].reshape(devices_y * shard, four_width), "gx", axis=0, tiled=True)

    two = jnp.concatenate(
        [part.reshape(shard, devices_y, ff_width).transpose(1, 0, 2) for part in (w_up, w_down.T)], axis=2
    )
    two, four = tie(two, four)
    small = four[:, :extra].reshape(devices_y, -1)[:, : 18 * shard].reshape(devices_y, 3, 6 * shard)
    small = gather_small(jnp.sum(small.astype(F32), axis=1).reshape(1, -1), "gx")
    small = small.reshape(devices_x, devices_y, 6, shard).transpose(2, 0, 1, 3).reshape(2, 3, width)

    two = lax.all_to_all(two, "gy", split_axis=0, concat_axis=0, tiled=True)
    live = (jnp.arange(img_count, dtype=jnp.int32) < image_counts[0]).astype(BF16)
    cot_own = cotangent * live[:, None, None]
    own = [
        jnp.concatenate([part[i : i + 1] for part in (media_features, latents, cot_own)], axis=1) for i in range(img_count)
    ]
    two, small, *own = tie(two, small, *own)
    ff_rows = two.reshape(devices_y * shard, 2 * ff_width)
    gains, biases = small[0], small[1]

    raw = {(0, i): own[i] for i in range(img_count)}
    joined_all = None
    if len(masks) == 4 and img_count == 2:
        slots = [(0, 0), (0, 1), (2, 0), (4, 0), (2, 1), (4, 1), (6, 0), (6, 1)]
        batches = (2, 1, 1)
        for slot in range(2):
            joined_all = norm_rows(slot, raw[slots[slot]], small, patch, rows, total, joined_all)
        raw[2, 0], raw[4, 0], ff_rows, later, joined_all = tie(
            swap(own[0], 2), swap(own[0], 4), ff_rows, own[1], joined_all
        )
        raw[2, 1], raw[4, 1], raw[6, 0] = swap(later, 2), swap(later, 4), swap(raw[2, 0], 4)
        raw[6, 1] = swap(raw[4, 1], 2)
    else:
        slots = [(mask, i) for mask in masks for i in range(img_count)]
        batches = (total // img_count - 1, 1)
        for mask in masks[1:]:
            raw.update({(mask, i): swap(own[i], mask) for i in range(img_count)})
    ff_mine = lax.all_gather(ff_rows, "gx", axis=0, tiled=True)
    theirs = swap(mine, 1)

    carried, out_parts, step = None, {}, 0
    for count in batches:
        here = range(step * img_count, (step + count) * img_count)
        if carried:
            joined_all, carried[0], *arrived = tie(joined_all, carried[0], *[raw[slots[slot]] for slot in here])
            raw.update({slots[slot]: part for slot, part in zip(here, arrived)})
        for slot in here:
            if slots[slot][0] or len(masks) != 4:
                joined_all = norm_rows(slot, raw[slots[slot]], small, patch, rows, total, joined_all)
        kv_all, qm_all, *parts = attend(joined_all, mine, theirs, heads, patch, step, count, img_count, carried)
        carried = [kv_all, qm_all]
        out_parts.update({slots[slot]: part for slot, part in zip(here, parts)})
        step += count

    def collect(parts):
        return jnp.concatenate(
            [
                sum(swap(parts[mask, i], mask).astype(F32) if mask else parts[mask, i].astype(F32) for mask in masks)
                for i in range(img_count)
            ]
        )

    cot_all = jnp.concatenate([raw[mask, i][:, rows:] for mask in masks for i in range(img_count)]).reshape(-1, width)
    latent_float = latents.astype(F32)
    attended = collect(out_parts) + latent_float
    hidden_own = normed(attended, gains[2], biases[2]).astype(BF16)
    *hidden, ff_mine = tie(*spread(hidden_own).values(), ff_mine)
    ff_theirs = swap(ff_mine, 1)
    hidden = jnp.concatenate(hidden).reshape(-1, width)

    def collect_pairs(parts):
        parts = [part.reshape(img_count, lat, width) for part in parts]
        return [parts[0]] + [swap(part, mask) for mask, part in zip(masks[1:], parts[1:])]

    total_of = lambda parts: sum(part.astype(F32) for part in parts)

    active, grad_upper, *hidden_parts = feed(hidden, cot_all, ff_mine, ff_theirs, len(masks))
    ff_operands = hidden, cot_all, grad_upper, active
    given = swap(feed_grads(*ff_operands, 1), 1)
    *hidden_parts, given = tie(*collect_pairs(hidden_parts), given)
    grad_norm_input, gain_two, bias_two = norm_back(attended, gains[2], total_of(hidden_parts))
    grad_attended = cot_own.astype(F32) + grad_norm_input
    grad_branch, given = tie(grad_attended.astype(BF16), given)
    branch = spread(grad_branch)
    ff_grads = feed_grads(*ff_operands, 0, given)
    ff_part = lax.psum_scatter(ff_grads, "gx", scatter_dimension=0, tiled=True)
    ffn_parts = product_right(active[:, :ff_width], ff_mine[:, ff_width:]) + product_right(
        active[:, ff_width:], ff_theirs[:, ff_width:]
    )
    *branch, ffn_parts, _ = tie(*branch.values(), ffn_parts.astype(BF16), ff_grads)
    branch = jnp.concatenate([branch[masks.index(mask)][i : i + 1] for mask, i in slots])

    steps = total // img_count
    arrays = branch, kv_all, qm_all, mine, theirs, heads, patch
    *carried, last, last_but_one = attend_back(steps - 1, 1, img_count, *arrays, None)
    dkv_all, dquery_all, *back = attend_back(steps - 2, steps - 1, img_count, *arrays, carried)
    back = [part for step in range(steps - 1) for part in back[step * img_count : (step + 1) * img_count]]
    order = [slots[step * img_count + i] for step in reversed(range(steps)) for i in range(img_count)]
    back = dict(zip(order, [last, last_but_one, *back]))

    def plus(left, right):
        return (left.astype(F32) + right.astype(F32)).astype(BF16)

    if len(masks) == 4 and img_count == 2:
        through = plus(back[2, 0], swap(back[6, 0], 4)), plus(back[4, 1], swap(back[6, 1], 2))
        dkv_all, dquery_all, *through = tie(dkv_all, dquery_all, *through)
        arrived = [
            back[0, 0], swap(through[0], 2), swap(back[4, 0], 4),
            back[0, 1], swap(back[2, 1], 2), swap(through[1], 4),
        ]
    else:
        arrived = [swap(back[mask, i], mask) if mask else back[mask, i] for i in range(img_count) for mask in masks]

    at_operands = joined_all, branch.reshape(total * lat, width), dkv_all, dquery_all, qm_all, heads, patch
    given = [swap(part, 1) for part in attend_grads(*at_operands, 1)]
    at_grads = attend_grads(*at_operands, 0, given)
    early, late = (lax.all_to_all(part, "gx", split_axis=0, concat_axis=0, tiled=True) for part in at_grads)
    *arrived, early, ff_part, ffn_parts = tie(*arrived, early, ff_part, ffn_parts)
    each = len(arrived) // img_count
    grad_joined = jnp.concatenate([total_of(arrived[i * each : (i + 1) * each]) for i in range(img_count)])

    grad_media, gain_zero, bias_zero = norm_back(media_features.astype(F32), gains[0], grad_joined[:, :patch])
    grad_latent, gain_one, bias_one = norm_back(latent_float, gains[1], grad_joined[:, patch:])
    grad_latents = grad_attended + grad_latent
    sums = sum_small(jnp.stack([gain_zero, gain_one, gain_two, bias_zero, bias_one, bias_two]), "gy")

    def home(part):
        return lax.all_to_all(part.reshape(devices_y, shard, -1), "gy", split_axis=0, concat_axis=0, tiled=True)

    result = attended + total_of(collect_pairs(ffn_parts.reshape(len(masks), img_count * lat, width)))
    outputs = (result * live.astype(F32)[:, None, None]).astype(BF16)
    grad_up, grad_down = ungroup(home(ff_part), 2)
    grad_down = grad_down.T
    late, sums, grad_up, grad_down, outputs, grad_media = tie(late, sums, grad_up, grad_down, outputs, grad_media)
    sums = sum_small(sums, "gx")
    place = lax.axis_index("gx") * devices_y + lax.axis_index("gy")
    sums = lax.dynamic_slice_in_dim(sums, place * shard, shard, axis=1)
    shares = jnp.concatenate(
        [
            jnp.sum(part.reshape(devices_x, devices_y * shard, 2 * head_width).astype(F32), axis=0)
            for part in (early, late)
        ],
        axis=1,
    )
    grad_key, grad_value, grad_query, grad_out = ungroup(home(shares.astype(BF16)), 4)
    return (
        outputs, grad_media, grad_latents, grad_query, grad_key, grad_value, grad_out.T, grad_up, grad_down,
        sums[:3], sums[3:],
    )


def solution(mesh):
    split = ("gx", "gy")
    images, first, second = P(split, None, None), P(split, None), P(None, split)
    return jax.shard_map(
        local,
        mesh=mesh,
        in_specs=(images, images, images, P(split), first, first, first, second, first, second, second, second),
        out_specs=(images, images, images, first, first, first, second, first, second, second, second),
        check_vma=False,
    )
```

time: 719 us -> 502 us (0.70)
  local copies, waits for them, and re-layouts: 143 us -> 32.9 us
  waiting for transfers between devices: 238 us -> 169 us
  Pallas kernels: 107 us -> 151 us
  matrix products: 48.7 us -> 7.36 us
  other arithmetic: 84 us -> 47.3 us
    pallas_call x8 -> x18, Pallas kernels: 43.1 us -> 118 us  [the longest x2 34.3 us: attend_back(): pl.pallas_call(functools.partial(attend_back_kernel, heads, patch, HEAD *...]
    ppermute x62 -> x42, waiting for transfers between devices: 210 us -> 147 us  [swap(): return lax.ppermute(block, axis, [(i, i ^ mask) for i in range(count)])]
    unnamed x375 -> x140, local copies, waits for them, and re-layouts: 67.9 us -> 15.9 us
    dot_general x7 -> x0, matrix products: 41.3 us -> none  [the longest x5 27.2 us: product_left(): lax.dot_general(left, right, (((0,), (0,)), ((), ())), preferred_element_...]
    another operation x40 -> x1, other arithmetic: 40.6 us -> 0.01 us  [in_thirds(): return jnp.stack(parts)]
    pallas_call x8 -> x3, Pallas kernels: 63.7 us -> 33.4 us  [attend(): pl.pallas_call(functools.partial(attend_kernel, heads, patch, HEAD ** (-0...]
    all_to_all x3 -> x4, waiting for transfers between devices: 22.5 us -> 5.47 us  [the longest x2 4.66 us: home(): lax.all_to_all(part.reshape(devices_y, shard, -1), 'gy', split_axis=0, co...]
    slice x14 -> x4, local copies, waits for them, and re-layouts: 18.2 us -> 2.5 us  [the longest x3 1.65 us: local(): part[i:i + 1]]
  transfers between devices with their start and end apart: 73 -> 51, of which waited for: 33 -> 28; matrix products, arithmetic and copies ran while one was open for 29% -> 15% of each run, Pallas kernels for 15% -> 24%
where the time goes in v2:
time: 502 us; the launch traced here: 493 us
  waiting for transfers between devices  169 us (34%)
  Pallas kernels  151 us (30%)
  starting transfers between devices  69.9 us (14%)
  other arithmetic  47.3 us (9%)
  local copies, waits for them, and re-layouts  32.9 us (7%)
  between operations  15.7 us (3%)
  matrix products  7.36 us (1%)
    ppermute x42, waiting for transfers between devices, swap(): return lax.ppermute(block, axis, [(i, i ^ mask) for i in range(count)])  147 us
    ppermute x42, starting transfers between devices, swap(): return lax.ppermute(block, axis, [(i, i ^ mask) for i in range(count)])  43.3 us
    pallas_call x2, Pallas kernels, attend_back(): pl.pallas_call(functools.partial(attend_back_kernel, heads, patch, HEAD *...  34.3 us
    pallas_call x3, Pallas kernels, attend(): pl.pallas_call(functools.partial(attend_kernel, heads, patch, HEAD ** (-0...  33.4 us
    pallas_call x8, Pallas kernels, norm_rows(): pl.pallas_call(functools.partial(norm_kernel, patch, rows), grid=(1,), in...  23.8 us
    pallas_call x2, Pallas kernels, attend_grads(): pl.pallas_call(functools.partial(attend_grads_kernel, heads, patch, HEAD...  22 us
    unnamed x140, local copies, waits for them, and re-layouts  15.9 us
    pallas_call x1, Pallas kernels, feed(): pl.pallas_call(functools.partial(feed_kernel, math.gcd(cols // 2, 384)),...  15.9 us
  transfers between devices with their start and end apart: 51, of which 28 were waited for; matrix products, arithmetic and copies ran while one was open for 15% of the time, Pallas kernels for 24%

profile of v2, /device:TPU:0, one launch (start us, length us, event | category | flops | bytes accessed | tf_op | source)
XLA Modules:
  0.0 493.2 jit_solution(13586295753913972321)
XLA Ops:
  8.7 2.2 shard_map.203
  10.9 5.3 %all-to-all-start = ((bf16[8,64,768]{2,1,0:T(8,128)(2,1)}), bf16[8,64,768]{2,1,0:T(8,128)(2,1)S(1)}, u32[]{:S(2)}, u32[]{:S(2)}) async-start(bf16[8,64,768]{2,1,0:T(8,128)(2,1)} %shard_map.203), calls=%async_computation | async-start | bytes 1572864 | tf_op jit(solution)/shard_map/all_to_all | solution.py:438
  19.9 8.9 %all-to-all-done = bf16[8,64,768]{2,1,0:T(8,128)(2,1)S(1)} async-done(((bf16[8,64,768]{2,1,0:T(8,128)(2,1)}), bf16[8,64,768]{2,1,0:T(8,128)(2,1)S(1)}, u32[]{:S(2)}, u32[]{:S(2)}) %all-to-all-start) | async-done | bytes 786464 | tf_op jit(solution)/shard_map/all_to_all | solution.py:438
  32.5 3.6 all-to-all-start.1
  38.1 2.6 collective-permute-start.1
  40.7 2.6 pad_maximum_fusion.2
  46.0 6.8 %all-to-all-done.1 = bf16[8,48,1536]{2,1,0:T(8,128)(2,1)S(1)} async-done(((bf16[8,48,1536]{2,1,0:T(8,128)(2,1)}), bf16[8,48,1536]{2,1,0:T(8,128)(2,1)S(1)}, u32[]{:S(2)}, u32[]{:S(2)}) %all-to-all-start.1) | async-done | bytes 1179680 | tf_op jit(solution)/shard_map/all_to_all | solution.py:449
  53.9 3.0 shard_map.204.refs_0_
  57.0 3.0 shard_map.205.refs_0_
  60.0 18.2 %collective-permute-done.3.raw_ref = bf16[1,384,1536]{2,1,0:T(8,128)(2,1)} collective-permute-done((bf16[1,384,1536]{2,1,0:T(8,128)(2,1)}, bf16[1,384,1536]{2,1,0:T(8,128)(2,1)}, u32[]{:S(2)}, u32[]{:S(2)}) %collective-permute-start.3) | collective-permute-done | bytes 1179680 | tf_op jit(solution)/shard_map/ppermute | solution.py:37
  78.2 1.8 collective-permute-done.2.raw_ref
  84.0 25.3 %collective-permute-done.6.raw_ref = bf16[1,384,1536]{2,1,0:T(8,128)(2,1)S(1)} collective-permute-done((bf16[1,384,1536]{2,1,0:T(8,128)(2,1)S(1)}, bf16[1,384,1536]{2,1,0:T(8,128)(2,1)S(1)}, u32[]{:S(2)}, u32[]{:S(2)}) %collective-permute-start.6) | collective-permute-done | bytes 1179680 | tf_op jit(solution)/shard_map/ppermute | solution.py:37
  110.9 2.9 shard_map.206.refs_0_
  113.8 2.9 shard_map.207.joined_ref.refs_0_
  118.2 15.4 %shard_map.208 = (bf16[8,320,768]{2,1,0:T(8,128)(2,1)}, bf16[8,64,768]{2,1,0:T(8,128)(2,1)}, bf16[1,64,1536]{2,1,0:T(8,128)(2,1)}, bf16[1,64,1536]{2,1,0:T(8,128...) custom-call(bf16[8,320,1536]{2,1,0:T(8,128)(2,1)} %shard_map.207.joined_ref.refs_0_, ...), custom_call_target="tpu_custom_call" | custom-call | flops 1024 | bytes 1024 | tf_op jit(solution)/shard_map/pallas_call | solution.py:205
  135.6 3.0 shard_map.209.refs_0_
  138.6 2.9 shard_map.210.joined_ref.refs_0_
  141.5 9.0 %shard_map.211 = (bf16[8,320,768]{2,1,0:T(8,128)(2,1)}, bf16[8,64,768]{2,1,0:T(8,128)(2,1)}, bf16[1,64,1536]{2,1,0:T(8,128)(2,1)}, bf16[1,64,1536]{2,1,0:T(8,128)(2,1)}) custom-call(bf16[8,320,1536]{2,1,0:T(8,128)(2,1)} %shard_map.210.joined_ref.refs_0_, ...), custom_call_target="tpu_custom_call", output_to_operand_aliasing={{0}: (3, {}), {1}: (4, {})} | custom-call | flops 1024 | bytes 1024 | tf_op jit(solution)/shard_map/pallas_call | solution.py:205
  151.5 2.9 shard_map.212.refs_0_
  154.4 3.0 shard_map.213.joined_ref
  157.5 9.0 %shard_map.214 = (bf16[8,320,768]{2,1,0:T(8,128)(2,1)}, bf16[8,64,768]{2,1,0:T(8,128)(2,1)}, bf16[1,64,1536]{2,1,0:T(8,128)(2,1)}, bf16[1,64,1536]{2,1,0:T(8,128)(2,1)}) custom-call(bf16[8,320,1536]{2,1,0:T(8,128)(2,1)} %shard_map.213.joined_ref, ...), custom_call_target="tpu_custom_call", output_to_operand_aliasing={{0}: (3, {}), {1}: (4, {})} | custom-call | flops 1024 | bytes 1024 | tf_op jit(solution)/shard_map/pallas_call | solution.py:205
  172.2 3.4 collective-permute-done.11
  175.6 2.9 collective-permute-done.12
  179.5 2.1 collective-permute-done.14
  186.9 9.5 %collective-permute-done.17 = bf16[2,64,1536]{2,1,0:T(8,128)(2,1)S(1)} collective-permute-done((bf16[2,64,1536]{2,1,0:T(8,128)(2,1)S(1)}, bf16[2,64,1536]{2,1,0:T(8,128)(2,1)S(1)}, u32[]{:S(2)}, u32[]{:S(2)}) %collective-permute-start.17) | collective-permute-done | bytes 393248 | tf_op jit(solution)/shard_map/ppermute | solution.py:37
  196.3 4.9 collective-permute-done.16
  207.9 2.7 pad_maximum_fusion
  210.5 2.2 copy-done.8
  212.7 15.9 %shard_map.215 = (bf16[512,1536]{1,0:T(8,128)(2,1)}, bf16[512,1536]{1,0:T(8,128)(2,1)}, bf16[128,1536]{1,0:T(8,128)(2,1)}, bf16[128,1536]{1,0:T(8,128)(2,1)}, bf...) custom-call(bf16[512,1536]{1,0:T(8,128)(2,1)} %bitcast.50, bf16[512,1536]{1,0:T(8,128)(2,1)} %bitcast.53, ...), custom_call_target="tpu_custom_call" | custom-call | flops 1024 | bytes 1024 | tf_op jit(solution)/shard_map/pallas_call | solution.py:310
  228.7 6.8 %shard_map.216 = bf16[1536,1536]{1,0:T(8,128)(2,1)} custom-call(bf16[512,1536]{1,0:T(8,128)(2,1)} %bitcast.51, bf16[512,1536]{1,0:T(8,128)(2,1)} %bitcast.54, bf16[512,1536]{1,0:T(8,128)(2,1)} %get-tuple-element.148.upper_ref, bf16[512,1536]{1,0:T(8,128)(2,1)} %get-tuple-element.149.active_ref), custom_call_target="tpu_custom_call" | custom-call | flops 1024 | bytes 1024 | tf_op jit(solution)/shard_map/pallas_call | solution.py:346
  239.4 8.5 %collective-permute-done.19 = bf16[2,64,1536]{2,1,0:T(8,128)(2,1)S(1)} collective-permute-done((bf16[2,64,1536]{2,1,0:T(8,128)(2,1)S(1)}, bf16[2,64,1536]{2,1,0:T(8,128)(2,1)S(1)}, u32[]{:S(2)}, u32[]{:S(2)}) %collective-permute-start.19) | collective-permute-done | bytes 393248 | tf_op jit(solution)/shard_map/ppermute | solution.py:37
  247.9 8.0 %collective-permute-done.20 = bf16[2,64,1536]{2,1,0:T(8,128)(2,1)S(1)} collective-permute-done((bf16[2,64,1536]{2,1,0:T(8,128)(2,1)S(1)}, bf16[2,64,1536]{2,1,0:T(8,128)(2,1)S(1)}, u32[]{:S(2)}, u32[]{:S(2)}) %collective-permute-start.20) | collective-permute-done | bytes 393248 | tf_op jit(solution)/shard_map/ppermute | solution.py:37
  258.6 8.2 %shard_map.217 = bf16[1536,1536]{1,0:T(8,128)(2,1)} custom-call(bf16[512,1536]{1,0:T(8,128)(2,1)} %bitcast.52, bf16[512,1536]{1,0:T(8,128)(2,1)} %bitcast.55, bf16[512,1536]{1,0:T(8,128)(2,1)} %get-tuple-element.148.upper_ref, bf16[512,1536]{1,0:T(8,128)(2,1)} %get-tuple-element.149.active_ref, bf16[1536,1536]{1,0:T(8,128)(2,1)} %copy-done.10), custom_call_target="tpu_custom_call" | custom-call | flops 1024 | bytes 1024 | tf_op jit(solution)/shard_map/pallas_call | solution.py:346
  268.2 3.1 fusion.12
  274.9 4.2 fusion.11
  279.2 5.3 %collective-permute-done.25 = bf16[2,64,1536]{2,1,0:T(8,128)(2,1)S(1)} collective-permute-done((bf16[2,64,1536]{2,1,0:T(8,128)(2,1)S(1)}, bf16[2,64,1536]{2,1,0:T(8,128)(2,1)S(1)}, u32[]{:S(2)}, u32[]{:S(2)}) %collective-permute-start.25) | collective-permute-done | bytes 393248 | tf_op jit(solution)/shard_map/ppermute | solution.py:37
  284.4 6.3 %collective-permute-done.24 = bf16[2,64,1536]{2,1,0:T(8,128)(2,1)S(1)} collective-permute-done((bf16[2,64,1536]{2,1,0:T(8,128)(2,1)S(1)}, bf16[2,64,1536]{2,1,0:T(8,128)(2,1)S(1)}, u32[]{:S(2)}, u32[]{:S(2)}) %collective-permute-start.24) | collective-permute-done | bytes 393248 | tf_op jit(solution)/shard_map/ppermute | solution.py:37
  292.0 9.8 %shard_map.218 = (bf16[8,320,768]{2,1,0:T(8,128)(2,1)}, bf16[8,64,768]{2,1,0:T(8,128)(2,1)}, bf16[1,320,1536]{2,1,0:T(8,128)(2,1)}, bf16[1,320,1536]{2,1,0:T(8,128)(2,1)}) custom-call(bf16[8,64,1536]{2,1,0:T(8,128)(2,1)} %copy-done.3, bf16[8,320,768]{2,1,0:T(8,128)(2,1)} %get-tuple-element.161.kv_ref, bf16[8,64,768]{2,1,0:T(8,128)(2,1)} %get-tuple-element.162.qm_ref, ...), custom_call_target="tpu_custom_call" | custom-call | flops 1024 | bytes 1024 | tf_op jit(solution)/shard_map/pallas_call | solution.py:264
  303.9 24.4 %shard_map.219 = (bf16[8,320,768]{2,1,0:T(8,128)(2,1)}, bf16[8,64,768]{2,1,0:T(8,128)(2,1)}, bf16[1,320,1536]{2,1,0:T(8,128)(2,1)}, bf16[1,320,1536]{2,1,0:T(8,1...) custom-call(bf16[8,64,1536]{2,1,0:T(8,128)(2,1)} %copy-done.3, ...), custom_call_target="tpu_custom_call", output_to_operand_aliasing={{0}: (5, {}), {1}: (6, {})} | custom-call | flops 1024 | bytes 1024 | tf_op jit(solution)/shard_map/pallas_call | solution.py:264
  328.4 2.4 add_convert_fusion.1
  332.1 10.7 %shard_map.220 = (bf16[1536,384]{1,0:T(8,128)(2,1)}, bf16[1536,384]{1,0:T(8,128)(2,1)}) custom-call(bf16[8,320,1536]{2,1,0:T(8,128)(2,1)} %shard_map.213.joined_ref, bf16[512,1536]{1,0:T(8,128)(2,1)} %bitcast.48, bf16[8,320,768]{2,1,0:T(8,128)(2,1)} %get-tuple-element.171.dkv_ref, bf16[8,64,768]{2,1,0:T(8,128)(2,1)} %get-tuple-element.172.dquery_ref, ...), custom_call_target="tpu_custom_call" | custom-call | flops 1024 | bytes 1024 | tf_op jit(solution)/shard_map/pallas_call | solution.py:382
  343.2 2.5 collective-permute-done.28.refs_0_
  348.5 11.3 %shard_map.221 = (bf16[1536,384]{1,0:T(8,128)(2,1)}, bf16[1536,384]{1,0:T(8,128)(2,1)}) custom-call(bf16[8,320,1536]{2,1,0:T(8,128)(2,1)} %shard_map.213.joined_ref, bf16[512,1536]{1,0:T(8,128)(2,1)} %bitcast.49, bf16[8,320,768]{2,1,0:T(8,128)(2,1)} %get-tuple-element.171.dkv_ref, bf16[8,64,768]{2,1,0:T(8,128)(2,1)} %get-tuple-element.172.dquery_ref, ...), custom_call_target="tpu_custom_call" | custom-call | flops 1024 | bytes 1024 | tf_op jit(solution)/shard_map/pallas_call | solution.py:382
  359.8 4.4 all-to-all-start.3
  372.3 17.3 %collective-permute-done.31 = bf16[1,320,1536]{2,1,0:T(8,128)(2,1)} collective-permute-done((bf16[1,320,1536]{2,1,0:T(8,128)(2,1)}, bf16[1,320,1536]{2,1,0:T(8,128)(2,1)}, u32[]{:S(2)}, u32[]{:S(2)}) %collective-permute-start.31) | collective-permute-done | bytes 983072 | tf_op jit(solution)/shard_map/ppermute | solution.py:37
  390.9 20.0 %collective-permute-done.30 = bf16[1,320,1536]{2,1,0:T(8,128)(2,1)} collective-permute-done((bf16[1,320,1536]{2,1,0:T(8,128)(2,1)S(1)}, bf16[1,320,1536]{2,1,0:T(8,128)(2,1)}, u32[]{:S(2)}, u32[]{:S(2)}) %collective-permute-start.30) | collective-permute-done | bytes 983072 | tf_op jit(solution)/shard_map/ppermute | solution.py:37
  411.0 4.3 all-to-all-start.4
  415.2 2.6 fusion.39
  417.9 2.8 collective-permute-start.39
  421.4 1.9 convert_add_fusion.1
  423.3 1.9 convert_add_fusion
  425.2 3.3 fusion.6
  432.6 4.7 all-to-all-start.2
  445.3 4.5 fusion.8
  450.9 3.2 collective-permute-done.35
  458.2 2.2 fusion.30
  460.5 2.7 shard_map.222
  465.3 2.2 reduce.1
  467.5 1.9 pad_maximum_fusion.5
  469.4 4.2 all-to-all-start.5
  474.5 2.4 collective-permute-start.41
  476.8 2.2 fusion.24
  481.1 3.0 all-to-all-done.5.from_ref
  484.1 2.2 shard_map.223
  (282 shorter events, 94.1 us)
Async XLA Ops:
  10.9 17.9 %all-to-all-start = ((bf16[8,64,768]{2,1,0:T(8,128)(2,1)}), bf16[8,64,768]{2,1,0:T(8,128)(2,1)S(1)}, u32[]{:S(2)}, u32[]{:S(2)}) async-start(bf16[8,64,768]{2,1,0:T(8,128)(2,1)} %shard_map.203), calls=%async_computation | async-start | bytes 1572864 | tf_op jit(solution)/shard_map/all_to_all | solution.py:438
  16.2 64.3 %all-gather.3.cloned.1.call-start = ((), (), s32[]{:S(2)}) async-start(), calls=%async_computation.7 | async-start | bytes 2949120 | tf_op jit(solution)/shard_map/all_gather | solution.py:439
  19.9 11.8 %copy-start.5 = (bf16[2,64,1536]{2,1,0:T(8,128)(2,1)S(1)}, bf16[2,64,1536]{2,1,0:T(8,128)(2,1)}, u32[]{:S(2)}) copy-start(bf16[2,64,1536]{2,1,0:T(8,128)(2,1)} %param.13) | copy-start | bytes 1179652
  30.0 10.6 %copy-start.27 = (bf16[1,64,1536]{2,1,0:T(8,128)(2,1)S(1)}, bf16[1,64,1536]{2,1,0:T(8,128)(2,1)}, u32[]{:S(2)}) copy-start(bf16[1,64,1536]{2,1,0:T(8,128)(2,1)} %get-tuple-element.235) | copy-start | bytes 589828
  30.0 10.6 %copy-start.28 = (bf16[1,64,1536]{2,1,0:T(8,128)(2,1)S(1)}, bf16[1,64,1536]{2,1,0:T(8,128)(2,1)}, u32[]{:S(2)}) copy-start(bf16[1,64,1536]{2,1,0:T(8,128)(2,1)} %get-tuple-element.236) | copy-start | bytes 589828
  30.1 6.0 %collective-permute-start = (f32[1,2304]{1,0:T(1,128)S(1)}, f32[1,2304]{1,0:T(1,128)}, u32[]{:S(2)}, u32[]{:S(2)}) collective-permute-start(f32[1,2304]{1,0:T(1,128)S(1)} %reshape.306), channel_id=1, source_target_pairs={{0,8},{8,0},{16,24},{24,16},{1,9},{9,1},{17,25},{25,17},{2,10},{10... | collective-permute-start | bytes 27656 | tf_op jit(solution)/shard_map/ppermute | solution.py:37
  32.5 20.3 %all-to-all-start.1 = ((bf16[8,48,1536]{2,1,0:T(8,128)(2,1)}), bf16[8,48,1536]{2,1,0:T(8,128)(2,1)S(1)}, u32[]{:S(2)}, u32[]{:S(2)}) async-start(bf16[8,48,1536]{2,1,0:T(8,128)(2,1)} %pad_maximum_fusion.1), calls=%async_computation.1 | async-start | bytes 2359296 | tf_op jit(solution)/shard_map/all_to_all | solution.py:449
  36.0 165.2 %all-gather.5.cloned.1.call-start = ((), (), s32[]{:S(2)}) async-start(), calls=%async_computation.8 | async-start | bytes 5898240 | tf_op jit(solution)/shard_map/all_gather | solution.py:476
  38.1 6.3 %collective-permute-start.1 = (f32[2,2304]{1,0:T(2,128)}, f32[2,2304]{1,0:T(2,128)}, u32[]{:S(2)}, u32[]{:S(2)}) collective-permute-start(f32[2,2304]{1,0:T(2,128)} %pad_maximum_fusion.7), channel_id=1, source_target_pairs={{0,16},{8,24},{16,0},{24,8},{1,17},{9,25},{17,1},{25,9},{2,18},{10... | collective-permute-start | bytes 55304 | tf_op jit(solution)/shard_map/ppermute | solution.py:37
  52.8 25.4 %collective-permute-start.3 = (bf16[1,384,1536]{2,1,0:T(8,128)(2,1)}, bf16[1,384,1536]{2,1,0:T(8,128)(2,1)}, u32[]{:S(2)}, u32[]{:S(2)}) collective-permute-start(bf16[1,384,1536]{2,1,0:T(8,128)(2,1)} %get-tuple-element.110.raw_ref), channel_id=1, source_target_pairs={{0,4},{1,5},{2,6},{3,7},{4,0},{5,1},{6,2},{7,3},{8,12},{9,13},{10,... | collective-permute-start | bytes 3538952 | tf_op jit(solution)/shard_map/ppermute | solution.py:37
  53.3 26.7 %collective-permute-start.2 = (bf16[1,384,1536]{2,1,0:T(8,128)(2,1)}, bf16[1,384,1536]{2,1,0:T(8,128)(2,1)}, u32[]{:S(2)}, u32[]{:S(2)}) collective-permute-start(bf16[1,384,1536]{2,1,0:T(8,128)(2,1)} %get-tuple-element.110.raw_ref), channel_id=1, source_target_pairs={{0,2},{1,3},{2,0},{3,1},{4,6},{5,7},{6,4},{7,5},{8,10},{9,11},{10,... | collective-permute-start | bytes 3538952 | tf_op jit(solution)/shard_map/ppermute | solution.py:37
  57.0 23.6 %copy-start.7 = (bf16[1,384,1536]{2,1,0:T(8,128)(2,1)S(1)}, bf16[1,384,1536]{2,1,0:T(8,128)(2,1)}, u32[]{:S(2)}) copy-start(bf16[1,384,1536]{2,1,0:T(8,128)(2,1)} %get-tuple-element.118.raw_ref) | copy-start | bytes 3538948
  80.0 330.9 %reduce-scatter.2.cloned.1.call-start = ((), (), s32[]{:S(2)}) async-start(), calls=%async_computation.9 | async-start | bytes 5898240 | tf_op jit(solution)/shard_map/reduce_scatter | solution.py:524
  80.5 36.3 %collective-permute-start.4 = (bf16[1536,768]{1,0:T(8,128)(2,1)}, bf16[1536,768]{1,0:T(8,128)(2,1)S(1)}, u32[]{:S(2)}, u32[]{:S(2)}) collective-permute-start(bf16[1536,768]{1,0:T(8,128)(2,1)} %all-gather.3.cloned.1.call-done.mine_ref), channel_id=1, source_target_pairs={{0,1},{1,0},{2,3},{3,2},{4,5},{5,4},{6,7},{7,6},{8,9},{9,8},{10,11... | collective-permute-start | bytes 7077896 | tf_op jit(solution)/shard_map/ppermute | solution.py:37
  80.5 28.8 %collective-permute-start.6 = (bf16[1,384,1536]{2,1,0:T(8,128)(2,1)S(1)}, bf16[1,384,1536]{2,1,0:T(8,128)(2,1)S(1)}, u32[]{:S(2)}, u32[]{:S(2)}) collective-permute-start(bf16[1,384,1536]{2,1,0:T(8,128)(2,1)S(1)} %copy-done.7), channel_id=1, source_target_pairs={{0,4},{1,5},{2,6},{3,7},{4,0},{5,1},{6,2},{7,3},{8,12},{9,13},{10,... | collective-permute-start | bytes 3538952 | tf_op jit(solution)/shard_map/ppermute | solution.py:37
  82.0 51.5 %collective-permute-start.5 = (bf16[1,384,1536]{2,1,0:T(8,128)(2,1)S(1)}, bf16[1,384,1536]{2,1,0:T(8,128)(2,1)}, u32[]{:S(2)}, u32[]{:S(2)}) collective-permute-start(bf16[1,384,1536]{2,1,0:T(8,128)(2,1)S(1)} %copy-done.7), channel_id=1, source_target_pairs={{0,2},{1,3},{2,0},{3,1},{4,6},{5,7},{6,4},{7,5},{8,10},{9,11},{10,... | collective-permute-start | bytes 3538952 | tf_op jit(solution)/shard_map/ppermute | solution.py:37
  83.7 66.8 %collective-permute-start.7 = (bf16[1,384,1536]{2,1,0:T(8,128)(2,1)}, bf16[1,384,1536]{2,1,0:T(8,128)(2,1)S(1)}, u32[]{:S(2)}, u32[]{:S(2)}) collective-permute-start(bf16[1,384,1536]{2,1,0:T(8,128)(2,1)} %collective-permute-done.2.raw_ref), channel_id=1, source_target_pairs={{0,4},{1,5},{2,6},{3,7},{4,0},{5,1},{6,2},{7,3},{8,12},{9,13},{10,... | collective-permute-start | bytes 3538952 | tf_op jit(solution)/shard_map/ppermute | solution.py:37
  109.3 41.2 %collective-permute-start.8 = (bf16[1,384,1536]{2,1,0:T(8,128)(2,1)S(1)}, bf16[1,384,1536]{2,1,0:T(8,128)(2,1)S(1)}, u32[]{:S(2)}, u32[]{:S(2)}) collective-permute-start(bf16[1,384,1536]{2,1,0:T(8,128)(2,1)S(1)} %collective-permute-done.6.raw_ref), channel_id=1, source_target_pairs={{0,2},{1,3},{2,0},{3,1},{4,6},{5,7},{6,4},{7,5},{8,10},{9,11},{10,... | collective-permute-start | bytes 3538952 | tf_op jit(solution)/shard_map/ppermute | solution.py:37
  133.5 37.1 %collective-permute-start.9 = (bf16[1,64,1536]{2,1,0:T(8,128)(2,1)}, bf16[1,64,1536]{2,1,0:T(8,128)(2,1)S(1)}, u32[]{:S(2)}, u32[]{:S(2)}) collective-permute-start(bf16[1,64,1536]{2,1,0:T(8,128)(2,1)} %get-tuple-element.129), channel_id=1, source_target_pairs={{0,2},{1,3},{2,0},{3,1},{4,6},{5,7},{6,4},{7,5},{8,10},{9,11},{10,... | collective-permute-start | bytes 589832 | tf_op jit(solution)/shard_map/ppermute | solution.py:37
  134.1 38.0 %collective-permute-start.10 = (bf16[1,64,1536]{2,1,0:T(8,128)(2,1)}, bf16[1,64,1536]{2,1,0:T(8,128)(2,1)S(1)}, u32[]{:S(2)}, u32[]{:S(2)}) collective-permute-start(bf16[1,64,1536]{2,1,0:T(8,128)(2,1)} %get-tuple-element.130), channel_id=1, source_target_pairs={{0,4},{1,5},{2,6},{3,7},{4,0},{5,1},{6,2},{7,3},{8,12},{9,13},{10,... | collective-permute-start | bytes 589832 | tf_op jit(solution)/shard_map/ppermute | solution.py:37
  157.5 11.2 %copy-start.62 = (bf16[1,64,1536]{2,1,0:T(8,128)(2,1)S(1)}, bf16[1,64,1536]{2,1,0:T(8,128)(2,1)}, u32[]{:S(2)}) copy-start(bf16[1,64,1536]{2,1,0:T(8,128)(2,1)} %get-tuple-element.135) | copy-start | bytes 589828
  157.5 11.7 %copy-start.61 = (bf16[1,64,1536]{2,1,0:T(8,128)(2,1)S(1)}, bf16[1,64,1536]{2,1,0:T(8,128)(2,1)}, u32[]{:S(2)}) copy-start(bf16[1,64,1536]{2,1,0:T(8,128)(2,1)} %get-tuple-element.136) | copy-start | bytes 589828
  157.5 18.1 %copy-start.33 = (bf16[1,64,1536]{2,1,0:T(8,128)(2,1)S(1)}, bf16[1,64,1536]{2,1,0:T(8,128)(2,1)}, u32[]{:S(2)}) copy-start(bf16[1,64,1536]{2,1,0:T(8,128)(2,1)} %get-tuple-element.128) | copy-start | bytes 589828
  157.5 24.1 %copy-start.32 = (bf16[1,64,1536]{2,1,0:T(8,128)(2,1)S(1)}, bf16[1,64,1536]{2,1,0:T(8,128)(2,1)}, u32[]{:S(2)}) copy-start(bf16[1,64,1536]{2,1,0:T(8,128)(2,1)} %get-tuple-element.134) | copy-start | bytes 589828
  166.5 9.0 %collective-permute-start.11 = (bf16[1,64,1536]{2,1,0:T(8,128)(2,1)}, bf16[1,64,1536]{2,1,0:T(8,128)(2,1)S(1)}, u32[]{:S(2)}, u32[]{:S(2)}) collective-permute-start(bf16[1,64,1536]{2,1,0:T(8,128)(2,1)} %get-tuple-element.133), channel_id=1, source_target_pairs={{0,6},{1,7},{2,4},{3,5},{4,2},{5,3},{6,0},{7,1},{8,14},{9,15},{10,... | collective-permute-start | bytes 589832 | tf_op jit(solution)/shard_map/ppermute | solution.py:37
  168.0 14.5 %copy-start.47 = (f32[2,64]{1,0:T(2,128)}, f32[2,64]{1,0:T(2,128)S(1)}, u32[]{:S(2)}) copy-start(f32[2,64]{1,0:T(2,128)S(1)} %broadcast_multiply_fusion.6) | copy-start | bytes 1540
  168.7 9.9 %collective-permute-start.12 = (bf16[1,64,1536]{2,1,0:T(8,128)(2,1)S(1)}, bf16[1,64,1536]{2,1,0:T(8,128)(2,1)S(1)}, u32[]{:S(2)}, u32[]{:S(2)}) collective-permute-start(bf16[1,64,1536]{2,1,0:T(8,128)(2,1)S(1)} %copy-done.62), channel_id=1, source_target_pairs={{0,2},{1,3},{2,0},{3,1},{4,6},{5,7},{6,4},{7,5},{8,10},{9,11},{10,... | collective-permute-start | bytes 589832 | tf_op jit(solution)/shard_map/ppermute | solution.py:37
  169.2 10.2 %collective-permute-start.13 = (bf16[1,64,1536]{2,1,0:T(8,128)(2,1)S(1)}, bf16[1,64,1536]{2,1,0:T(8,128)(2,1)S(1)}, u32[]{:S(2)}, u32[]{:S(2)}) collective-permute-start(bf16[1,64,1536]{2,1,0:T(8,128)(2,1)S(1)} %copy-done.61), channel_id=1, source_target_pairs={{0,4},{1,5},{2,6},{3,7},{4,0},{5,1},{6,2},{7,3},{8,12},{9,13},{10,... | collective-permute-start | bytes 589832 | tf_op jit(solution)/shard_map/ppermute | solution.py:37
  170.7 10.9 %collective-permute-start.14 = (bf16[1,64,1536]{2,1,0:T(8,128)(2,1)}, bf16[1,64,1536]{2,1,0:T(8,128)(2,1)S(1)}, u32[]{:S(2)}, u32[]{:S(2)}) collective-permute-start(bf16[1,64,1536]{2,1,0:T(8,128)(2,1)} %get-tuple-element.137), channel_id=1, source_target_pairs={{0,6},{1,7},{2,4},{3,5},{4,2},{5,3},{6,0},{7,1},{8,14},{9,15},{10,... | collective-permute-start | bytes 589832 | tf_op jit(solution)/shard_map/ppermute | solution.py:37
  183.3 13.0 %collective-permute-start.17 = (bf16[2,64,1536]{2,1,0:T(8,128)(2,1)S(1)}, bf16[2,64,1536]{2,1,0:T(8,128)(2,1)S(1)}, u32[]{:S(2)}, u32[]{:S(2)}) collective-permute-start(bf16[2,64,1536]{2,1,0:T(8,128)(2,1)S(1)} %add_convert_fusion.2), channel_id=1, source_target_pairs={{0,6},{1,7},{2,4},{3,5},{4,2},{5,3},{6,0},{7,1},{8,14},{9,15},{10,... | collective-permute-start | bytes 1179656 | tf_op jit(solution)/shard_map/ppermute | solution.py:37
  184.8 16.4 %collective-permute-start.16 = (bf16[2,64,1536]{2,1,0:T(8,128)(2,1)S(1)}, bf16[2,64,1536]{2,1,0:T(8,128)(2,1)S(1)}, u32[]{:S(2)}, u32[]{:S(2)}) collective-permute-start(bf16[2,64,1536]{2,1,0:T(8,128)(2,1)S(1)} %add_convert_fusion.2), channel_id=1, source_target_pairs={{0,4},{1,5},{2,6},{3,7},{4,0},{5,1},{6,2},{7,3},{8,12},{9,13},{10,... | collective-permute-start | bytes 1179656 | tf_op jit(solution)/shard_map/ppermute | solution.py:37
  186.3 14.9 %collective-permute-start.15 = (bf16[2,64,1536]{2,1,0:T(8,128)(2,1)S(1)}, bf16[2,64,1536]{2,1,0:T(8,128)(2,1)}, u32[]{:S(2)}, u32[]{:S(2)}) collective-permute-start(bf16[2,64,1536]{2,1,0:T(8,128)(2,1)S(1)} %add_convert_fusion.2), channel_id=1, source_target_pairs={{0,2},{1,3},{2,0},{3,1},{4,6},{5,7},{6,4},{7,5},{8,10},{9,11},{10,... | collective-permute-start | bytes 1179656 | tf_op jit(solution)/shard_map/ppermute | solution.py:37
  201.2 9.3 %collective-permute-start.18 = (bf16[1536,1536]{1,0:T(8,128)(2,1)}, bf16[1536,1536]{1,0:T(8,128)(2,1)S(1)}, u32[]{:S(2)}, u32[]{:S(2)}) collective-permute-start(bf16[1536,1536]{1,0:T(8,128)(2,1)} %all-gather.5.cloned.1.call-done.mine_ref), channel_id=1, source_target_pairs={{0,1},{1,0},{2,3},{3,2},{4,5},{5,4},{6,7},{7,6},{8,9},{9,8},{10,11... | collective-permute-start | bytes 14155784 | tf_op jit(solution)/shard_map/ppermute | solution.py:37
  228.6 27.3 %copy-start.31 = (bf16[128,1536]{1,0:T(8,128)(2,1)S(1)}, bf16[128,1536]{1,0:T(8,128)(2,1)}, u32[]{:S(2)}) copy-start(bf16[128,1536]{1,0:T(8,128)(2,1)} %get-tuple-element.144) | copy-start | bytes 1179652
  228.6 27.3 %copy-start.39 = (f32[2,64]{1,0:T(2,128)S(1)}, f32[2,64]{1,0:T(2,128)}, u32[]{:S(2)}) copy-start(f32[2,64]{1,0:T(2,128)} %copy-done.38) | copy-start | bytes 1540
  228.6 27.3 %copy-start.45 = (f32[2,64]{1,0:T(2,128)S(1)}, f32[2,64]{1,0:T(2,128)}, u32[]{:S(2)}) copy-start(f32[2,64]{1,0:T(2,128)} %copy-done.44) | copy-start | bytes 1540
  235.5 20.5 %collective-permute-start.22 = (bf16[1536,1536]{1,0:T(8,128)(2,1)}, bf16[1536,1536]{1,0:T(8,128)(2,1)S(1)}, u32[]{:S(2)}, u32[]{:S(2)}) collective-permute-start(bf16[1536,1536]{1,0:T(8,128)(2,1)} %shard_map.216), channel_id=1, source_target_pairs={{0,1},{1,0},{2,3},{3,2},{4,5},{5,4},{6,7},{7,6},{8,9},{9,8},{10,11... | collective-permute-start | bytes 14155784 | tf_op jit(solution)/shard_map/ppermute | solution.py:37
  235.9 12.0 %collective-permute-start.19 = (bf16[2,64,1536]{2,1,0:T(8,128)(2,1)S(1)}, bf16[2,64,1536]{2,1,0:T(8,128)(2,1)S(1)}, u32[]{:S(2)}, u32[]{:S(2)}) collective-permute-start(bf16[2,64,1536]{2,1,0:T(8,128)(2,1)S(1)} %bitcast.75), channel_id=1, source_target_pairs={{0,2},{1,3},{2,0},{3,1},{4,6},{5,7},{6,4},{7,5},{8,10},{9,11},{10,... | collective-permute-start | bytes 1179656 | tf_op jit(solution)/shard_map/ppermute | solution.py:37
  236.7 19.2 %collective-permute-start.20 = (bf16[2,64,1536]{2,1,0:T(8,128)(2,1)S(1)}, bf16[2,64,1536]{2,1,0:T(8,128)(2,1)S(1)}, u32[]{:S(2)}, u32[]{:S(2)}) collective-permute-start(bf16[2,64,1536]{2,1,0:T(8,128)(2,1)S(1)} %bitcast.74), channel_id=1, source_target_pairs={{0,4},{1,5},{2,6},{3,7},{4,0},{5,1},{6,2},{7,3},{8,12},{9,13},{10,... | collective-permute-start | bytes 1179656 | tf_op jit(solution)/shard_map/ppermute | solution.py:37
  237.9 18.1 %collective-permute-start.21 = (bf16[2,64,1536]{2,1,0:T(8,128)(2,1)S(1)}, bf16[2,64,1536]{2,1,0:T(8,128)(2,1)S(1)}, u32[]{:S(2)}, u32[]{:S(2)}) collective-permute-start(bf16[2,64,1536]{2,1,0:T(8,128)(2,1)S(1)} %bitcast.73), channel_id=1, source_target_pairs={{0,6},{1,7},{2,4},{3,5},{4,2},{5,3},{6,0},{7,1},{8,14},{9,15},{10,... | collective-permute-start | bytes 1179656 | tf_op jit(solution)/shard_map/ppermute | solution.py:37
  271.4 13.0 %collective-permute-start.25 = (bf16[2,64,1536]{2,1,0:T(8,128)(2,1)S(1)}, bf16[2,64,1536]{2,1,0:T(8,128)(2,1)S(1)}, u32[]{:S(2)}, u32[]{:S(2)}) collective-permute-start(bf16[2,64,1536]{2,1,0:T(8,128)(2,1)S(1)} %copy-done.20), channel_id=1, source_target_pairs={{0,6},{1,7},{2,4},{3,5},{4,2},{5,3},{6,0},{7,1},{8,14},{9,15},{10,... | collective-permute-start | bytes 1179656 | tf_op jit(solution)/shard_map/ppermute | solution.py:37
  272.9 17.9 %collective-permute-start.24 = (bf16[2,64,1536]{2,1,0:T(8,128)(2,1)S(1)}, bf16[2,64,1536]{2,1,0:T(8,128)(2,1)S(1)}, u32[]{:S(2)}, u32[]{:S(2)}) collective-permute-start(bf16[2,64,1536]{2,1,0:T(8,128)(2,1)S(1)} %copy-done.20), channel_id=1, source_target_pairs={{0,4},{1,5},{2,6},{3,7},{4,0},{5,1},{6,2},{7,3},{8,12},{9,13},{10,... | collective-permute-start | bytes 1179656 | tf_op jit(solution)/shard_map/ppermute | solution.py:37
  274.2 16.6 %collective-permute-start.23 = (bf16[2,64,1536]{2,1,0:T(8,128)(2,1)S(1)}, bf16[2,64,1536]{2,1,0:T(8,128)(2,1)S(1)}, u32[]{:S(2)}, u32[]{:S(2)}) collective-permute-start(bf16[2,64,1536]{2,1,0:T(8,128)(2,1)S(1)} %copy-done.20), channel_id=1, source_target_pairs={{0,2},{1,3},{2,0},{3,1},{4,6},{5,7},{6,4},{7,5},{8,10},{9,11},{10,... | collective-permute-start | bytes 1179656 | tf_op jit(solution)/shard_map/ppermute | solution.py:37
  301.9 26.5 %collective-permute-start.26 = (bf16[1,320,1536]{2,1,0:T(8,128)(2,1)}, bf16[1,320,1536]{2,1,0:T(8,128)(2,1)S(1)}, u32[]{:S(2)}, u32[]{:S(2)}) collective-permute-start(bf16[1,320,1536]{2,1,0:T(8,128)(2,1)} %get-tuple-element.168), channel_id=1, source_target_pairs={{0,4},{1,5},{2,6},{3,7},{4,0},{5,1},{6,2},{7,3},{8,12},{9,13},{10,... | collective-permute-start | bytes 2949128 | tf_op jit(solution)/shard_map/ppermute | solution.py:37
  303.2 27.7 %collective-permute-start.27 = (bf16[1,320,1536]{2,1,0:T(8,128)(2,1)}, bf16[1,320,1536]{2,1,0:T(8,128)(2,1)S(1)}, u32[]{:S(2)}, u32[]{:S(2)}) collective-permute-start(bf16[1,320,1536]{2,1,0:T(8,128)(2,1)} %get-tuple-element.170), channel_id=1, source_target_pairs={{0,2},{1,3},{2,0},{3,1},{4,6},{5,7},{6,4},{7,5},{8,10},{9,11},{10,... | collective-permute-start | bytes 2949128 | tf_op jit(solution)/shard_map/ppermute | solution.py:37
  342.7 3.1 collective-permute-start.28
  342.7 4.7 collective-permute-start.29
  359.8 51.1 %all-to-all-start.3 = ((bf16[4,384,384]{2,1,0:T(8,128)(2,1)}), bf16[4,384,384]{2,1,0:T(8,128)(2,1)}, u32[]{:S(2)}, u32[]{:S(2)}) async-start(bf16[4,384,384]{2,1,0:T(8,128)(2,1)} %bitcast.61), calls=%async_computation.3 | async-start | bytes 2359296 | tf_op jit(solution)/shard_map/all_to_all | solution.py:555
  364.6 25.0 %collective-permute-start.31 = (bf16[1,320,1536]{2,1,0:T(8,128)(2,1)}, bf16[1,320,1536]{2,1,0:T(8,128)(2,1)}, u32[]{:S(2)}, u32[]{:S(2)}) collective-permute-start(bf16[1,320,1536]{2,1,0:T(8,128)(2,1)} %get-tuple-element.178), channel_id=1, source_target_pairs={{0,4},{1,5},{2,6},{3,7},{4,0},{5,1},{6,2},{7,3},{8,12},{9,13},{10,... | collective-permute-start | bytes 2949128 | tf_op jit(solution)/shard_map/ppermute | solution.py:37
  366.0 25.0 %collective-permute-start.32 = (bf16[1,320,1536]{2,1,0:T(8,128)(2,1)}, bf16[1,320,1536]{2,1,0:T(8,128)(2,1)}, u32[]{:S(2)}, u32[]{:S(2)}) collective-permute-start(bf16[1,320,1536]{2,1,0:T(8,128)(2,1)} %get-tuple-element.180), channel_id=1, source_target_pairs={{0,2},{1,3},{2,0},{3,1},{4,6},{5,7},{6,4},{7,5},{8,10},{9,11},{10,... | collective-permute-start | bytes 2949128 | tf_op jit(solution)/shard_map/ppermute | solution.py:37
  366.7 44.2 %collective-permute-start.30 = (bf16[1,320,1536]{2,1,0:T(8,128)(2,1)S(1)}, bf16[1,320,1536]{2,1,0:T(8,128)(2,1)}, u32[]{:S(2)}, u32[]{:S(2)}) collective-permute-start(bf16[1,320,1536]{2,1,0:T(8,128)(2,1)S(1)} %copy-done.25), channel_id=1, source_target_pairs={{0,2},{1,3},{2,0},{3,1},{4,6},{5,7},{6,4},{7,5},{8,10},{9,11},{10,... | collective-permute-start | bytes 2949128 | tf_op jit(solution)/shard_map/ppermute | solution.py:37
  368.0 42.9 %collective-permute-start.33 = (bf16[1,320,1536]{2,1,0:T(8,128)(2,1)}, bf16[1,320,1536]{2,1,0:T(8,128)(2,1)}, u32[]{:S(2)}, u32[]{:S(2)}) collective-permute-start(bf16[1,320,1536]{2,1,0:T(8,128)(2,1)} %add_convert_fusion), channel_id=1, source_target_pairs={{0,4},{1,5},{2,6},{3,7},{4,0},{5,1},{6,2},{7,3},{8,12},{9,13},{10,... | collective-permute-start | bytes 2949128 | tf_op jit(solution)/shard_map/ppermute | solution.py:37
  369.3 41.6 %copy-start.42 = (f32[2,256]{1,0:T(2,128)}, f32[2,256]{1,0:T(2,128)S(1)}, u32[]{:S(2)}) copy-start(f32[2,256]{1,0:T(2,128)S(1)} %broadcast_multiply_fusion.3) | copy-start | bytes 6148
  411.0 21.7 %all-to-all-start.4 = ((bf16[8,48,1536]{2,1,0:T(8,128)(2,1)}), bf16[8,48,1536]{2,1,0:T(8,128)(2,1)}, u32[]{:S(2)}, u32[]{:S(2)}) async-start(bf16[8,48,1536]{2,1,0:T(8,128)(2,1)} %bitcast.59), calls=%async_computation.5 | async-start | bytes 2359296 | tf_op jit(solution)/shard_map/all_to_all | solution.py:566
  417.9 40.3 %collective-permute-start.39 = (bf16[2,64,1536]{2,1,0:T(8,128)(2,1)}, bf16[2,64,1536]{2,1,0:T(8,128)(2,1)}, u32[]{:S(2)}, u32[]{:S(2)}) collective-permute-start(bf16[2,64,1536]{2,1,0:T(8,128)(2,1)} %bitcast.26), channel_id=1, source_target_pairs={{0,6},{1,7},{2,4},{3,5},{4,2},{5,3},{6,0},{7,1},{8,14},{9,15},{10,... | collective-permute-start | bytes 1179656 | tf_op jit(solution)/shard_map/ppermute | solution.py:37
  420.7 37.5 %collective-permute-start.37 = (bf16[2,64,1536]{2,1,0:T(8,128)(2,1)}, bf16[2,64,1536]{2,1,0:T(8,128)(2,1)}, u32[]{:S(2)}, u32[]{:S(2)}) collective-permute-start(bf16[2,64,1536]{2,1,0:T(8,128)(2,1)} %bitcast.24), channel_id=1, source_target_pairs={{0,2},{1,3},{2,0},{3,1},{4,6},{5,7},{6,4},{7,5},{8,10},{9,11},{10,... | collective-permute-start | bytes 1179656 | tf_op jit(solution)/shard_map/ppermute | solution.py:37
  421.2 37.0 %collective-permute-start.38 = (bf16[2,64,1536]{2,1,0:T(8,128)(2,1)}, bf16[2,64,1536]{2,1,0:T(8,128)(2,1)}, u32[]{:S(2)}, u32[]{:S(2)}) collective-permute-start(bf16[2,64,1536]{2,1,0:T(8,128)(2,1)} %bitcast.25), channel_id=1, source_target_pairs={{0,4},{1,5},{2,6},{3,7},{4,0},{5,1},{6,2},{7,3},{8,12},{9,13},{10,... | collective-permute-start | bytes 1179656 | tf_op jit(solution)/shard_map/ppermute | solution.py:37
  432.6 31.4 %all-to-all-start.2 = ((bf16[4,384,384]{2,1,0:T(8,128)(2,1)}), bf16[4,384,384]{2,1,0:T(8,128)(2,1)}, u32[]{:S(2)}, u32[]{:S(2)}) async-start(bf16[4,384,384]{2,1,0:T(8,128)(2,1)} %bitcast.60), calls=%async_computation.2 | async-start | bytes 2359296 | tf_op jit(solution)/shard_map/all_to_all | solution.py:555
  445.2 4.6 collective-permute-start.34
  449.8 4.2 collective-permute-start.35
  454.0 4.2 collective-permute-start.36
  464.0 9.6 %collective-permute-start.40 = (f32[6,1536]{1,0:T(8,128)S(1)}, f32[6,1536]{1,0:T(8,128)}, u32[]{:S(2)}, u32[]{:S(2)}) collective-permute-start(f32[6,1536]{1,0:T(8,128)S(1)} %add.159), channel_id=1, source_target_pairs={{0,8},{8,0},{16,24},{24,16},{1,9},{9,1},{17,25},{25,17},{2,10},{10... | collective-permute-start | bytes 110600 | tf_op jit(solution)/shard_map/ppermute | solution.py:37
  469.4 14.7 %all-to-all-start.5 = ((bf16[8,48,768]{2,1,0:T(8,128)(2,1)}), bf16[8,48,768]{2,1,0:T(8,128)(2,1)}, u32[]{:S(2)}, u32[]{:S(2)}) async-start(bf16[8,48,768]{2,1,0:T(8,128)(2,1)} %pad_maximum_fusion.5), calls=%async_computation.6 | async-start | bytes 1179648 | tf_op jit(solution)/shard_map/all_to_all | solution.py:566
  474.5 6.0 %collective-permute-start.41 = (f32[6,1536]{1,0:T(8,128)S(1)}, f32[6,1536]{1,0:T(8,128)S(1)}, u32[]{:S(2)}, u32[]{:S(2)}) collective-permute-start(f32[6,1536]{1,0:T(8,128)S(1)} %add.165), channel_id=1, source_target_pairs={{0,16},{8,24},{16,0},{24,8},{1,17},{9,25},{17,1},{25,9},{2,18},{10... | collective-permute-start | bytes 110600 | tf_op jit(solution)/shard_map/ppermute | solution.py:37
  (50 other events, 208.3 us)
Sparse Core Ops, SparseCore 0:
  29.8 50.6 all-gather.2
  82.1 88.1 all-gather.4
  267.0 84.4 reduce-scatter.1

commit v3 on v2

v3 whole, which is shorter than its diff:
```python
import functools
import math

import jax
import jax.numpy as jnp
from jax import lax
from jax.experimental import pallas as pl
from jax.experimental.pallas import tpu as pltpu
from jax.sharding import PartitionSpec as P

HEAD = 96
EPSILON = 1e-05
BF16 = jnp.bfloat16
F32 = jnp.float32
VMEM = 56 * 2**20
LITTLE = pl.CostEstimate(flops=1024, bytes_accessed=1024, transcendentals=0)


def product(left, right):
    return jnp.dot(left, right, preferred_element_type=F32)


def product_left(left, right):
    return lax.dot_general(left, right, (((0,), (0,)), ((), ())), preferred_element_type=F32)


def product_right(left, right):
    return lax.dot_general(left, right, (((1,), (1,)), ((), ())), preferred_element_type=F32)


def tie(*values):
    return lax.optimization_barrier(values)


def swap(block, mask, axis="gy"):
    count = lax.axis_size(axis)
    return lax.ppermute(block, axis, [(i, i ^ mask) for i in range(count)])


def far_masks():
    return [mask for mask in range(lax.axis_size("gy")) if mask % 2 == 0]


def spread(block):
    return {mask: swap(block, mask) if mask else block for mask in far_masks()}


def regroup_kernel(first_ref, *refs):
    *from_refs, to_ref = refs
    extra, half = first_ref.shape[0], len(from_refs) // 2
    groups = to_ref.shape[0] // 2
    cols = from_refs[0].shape[1] // groups
    for device in range(2 * groups):
        group, core = device // 2, device % 2
        to_ref[device, :extra] = first_ref[...]
        for index, from_ref in enumerate(from_refs[core * half : (core + 1) * half]):
            to_ref[device, extra:, index * cols : (index + 1) * cols] = from_ref[:, group * cols : (group + 1) * cols]


def regroup(first, devices, *weights):
    shard, width = weights[0].shape
    return pl.pallas_call(
        regroup_kernel,
        out_shape=jax.ShapeDtypeStruct((devices, first.shape[0] + shard, first.shape[1]), BF16),
        compiler_params=pltpu.CompilerParams(vmem_limit_bytes=VMEM),
        cost_estimate=LITTLE,
    )(first, *weights)


def ungroup_kernel(by_pair, from_ref, *to_refs):
    devices, _, width = from_ref.shape
    per = len(to_refs) // 2 if by_pair else len(to_refs)
    cols = width // per
    for index, to_ref in enumerate(to_refs):
        sources = range(index // per, devices, 2) if by_pair else range(devices)
        place = slice(index % per * cols, (index % per + 1) * cols)
        for position, device in enumerate(sources):
            to_ref[:, position * cols : (position + 1) * cols] = from_ref[device, :, place].astype(F32)


def ungroup(blocks, count, by_pair):
    devices, shard, width = blocks.shape
    return pl.pallas_call(
        functools.partial(ungroup_kernel, by_pair),
        out_shape=[jax.ShapeDtypeStruct((shard, devices * width // count), F32)] * count,
        compiler_params=pltpu.CompilerParams(vmem_limit_bytes=VMEM),
        cost_estimate=LITTLE,
    )(blocks)


def bits_of(count):
    bits, bit = [], 1
    while bit < count:
        bits.append(bit)
        bit *= 2
    return bits


def gather_small(rows, axis):
    place = lax.axis_index(axis)
    for bit in bits_of(lax.axis_size(axis)):
        other = swap(rows, bit, axis)
        upper = (place & bit) != 0
        rows = jnp.concatenate([jnp.where(upper, other, rows), jnp.where(upper, rows, other)])
    return rows


def sum_small(rows):
    rows = rows + swap(rows, 1)
    rows = sum([rows] + [swap(rows, mask) for mask in far_masks()[1:]])
    return sum([rows] + [swap(rows, mask, "gx") for mask in range(1, lax.axis_size("gx"))])


def normed(rows, gain, bias):
    average = jnp.mean(rows, axis=-1, keepdims=True)
    centred = rows - average
    spread_of = jnp.mean(centred * centred, axis=-1, keepdims=True)
    return centred * lax.rsqrt(spread_of + EPSILON) * gain + bias


def head_mask(rows, lanes, head):
    lane = lax.broadcasted_iota(jnp.int32, (rows, lanes), 1)
    return (lane >= head * HEAD) & (lane < (head + 1) * HEAD)


def stacked(rows, heads):
    count, lanes = rows.shape
    return jnp.concatenate(
        [jnp.where(head_mask(count, lanes, h), rows, jnp.zeros_like(rows)) for h in range(heads)]
    )


def unstacked(rows, heads):
    count, lanes = rows.shape[0] // heads, rows.shape[1]
    total = rows[:count]
    for h in range(1, heads):
        total = jnp.where(head_mask(count, lanes, h), rows[h * count : (h + 1) * count], total)
    return total


def softmax_rows(scores):
    top = jnp.max(scores, axis=-1, keepdims=True)
    raised = jnp.exp(scores - top)
    return raised / jnp.sum(raised, axis=-1, keepdims=True)


def load_weights(pair_ref, mine_ref, theirs_ref, kv_weights, qo_weights, sems):
    @pl.when(pair_ref[0] == 0)
    def _():
        pltpu.make_async_copy(mine_ref, kv_weights, sems.at[0]).start()
        pltpu.make_async_copy(theirs_ref, qo_weights, sems.at[1]).start()

    @pl.when(pair_ref[0] == 1)
    def _():
        pltpu.make_async_copy(theirs_ref, kv_weights, sems.at[0]).start()
        pltpu.make_async_copy(mine_ref, qo_weights, sems.at[1]).start()

    return [
        pltpu.make_async_copy(mine_ref, kv_weights, sems.at[0]),
        pltpu.make_async_copy(theirs_ref, qo_weights, sems.at[1]),
    ]


def attend_kernel(heads, patch, scale, raws, given, pair_ref, mine_ref, theirs_ref, small_ref, *refs):
    *refs, kv_weights, qo_weights, sems = refs
    joined_ref, kv_ref, qm_ref, *out_refs = refs[raws + given :]
    count, rows, width = joined_ref.shape
    copies = load_weights(pair_ref, mine_ref, theirs_ref, kv_weights, qo_weights, sems)
    for image, raw_ref in enumerate(refs[:raws]):
        media = normed(raw_ref[0, :patch].astype(F32), small_ref[0, 0:1], small_ref[1, 0:1])
        latent = normed(raw_ref[0, patch:rows].astype(F32), small_ref[0, 1:2], small_ref[1, 1:2])
        joined_ref[image, :patch] = media.astype(BF16)
        joined_ref[image, patch:] = latent.astype(BF16)
    for copy in copies:
        copy.wait()
    lat, cols = rows - patch, kv_weights.shape[1] // 2
    joined = joined_ref[...].reshape(count * rows, width)
    latent = joined_ref[:, patch:].reshape(count * lat, width)
    kv_ref[...] = product(joined, kv_weights[...]).astype(BF16).reshape(count, rows, 2 * cols)
    query = (product(latent, qo_weights[:, :cols]) * scale).astype(BF16)
    qm_ref[:, :, :cols] = query.reshape(count, lat, cols)
    mixed = []
    for image in range(count):
        probs = softmax_rows(product_right(stacked(query[image * lat : (image + 1) * lat], heads), kv_ref[image, :, :cols]))
        mixed.append(unstacked(product(probs.astype(BF16), kv_ref[image, :, cols:]), heads).astype(BF16))
    mixed = jnp.concatenate(mixed)
    qm_ref[:, :, cols:] = mixed.reshape(count, lat, cols)
    total = product_right(mixed, qo_weights[:, cols:]).astype(BF16).reshape(count, lat, width)
    for image, out_ref in enumerate(out_refs):
        out_ref[0] = total[image]


SMALL = pl.BlockSpec(memory_space=pltpu.SMEM)
ANY = pl.BlockSpec(memory_space=pl.ANY)


def weight_scratch(mine):
    return [pltpu.VMEM(mine.shape, BF16)] * 2 + [pltpu.SemaphoreType.DMA((2,))]


def attend(pair, mine, theirs, small, raws, heads, patch, rows, step, total, carried):
    width, cols = mine.shape
    lat, per = rows - patch, len(raws)
    part = lambda *shape: pl.BlockSpec((per,) + shape, lambda i: (step, 0, 0))
    given = list(carried or ())
    return pl.pallas_call(
        functools.partial(attend_kernel, heads, patch, HEAD ** (-0.5), per, len(given)),
        grid=(1,),
        in_specs=[SMALL, ANY, ANY, whole(small.shape)] + [whole(raw.shape) for raw in raws] + [ANY] * len(given),
        out_specs=[part(rows, width), part(rows, cols), part(lat, cols)] + [whole((1, lat, width))] * per,
        out_shape=[
            jax.ShapeDtypeStruct((total, rows, width), BF16),
            jax.ShapeDtypeStruct((total, rows, cols), BF16),
            jax.ShapeDtypeStruct((total, lat, cols), BF16),
        ]
        + [jax.ShapeDtypeStruct((1, lat, width), BF16)] * per,
        scratch_shapes=weight_scratch(mine),
        input_output_aliases={4 + per + i: i for i in range(len(given))},
        compiler_params=pltpu.CompilerParams(vmem_limit_bytes=VMEM),
        cost_estimate=LITTLE,
    )(pair, mine, theirs, small, *raws, *given)


def attend_back_kernel(heads, patch, scale, given, pair_ref, mine_ref, theirs_ref, branch_ref, kv_ref, qm_ref, *refs):
    *refs, kv_weights, qo_weights, sems = refs

    @pl.when(pl.program_id(0) == 0)
    def _():
        for copy in load_weights(pair_ref, mine_ref, theirs_ref, kv_weights, qo_weights, sems):
            copy.wait()

    dkv_ref, dquery_ref, *back_refs = refs[given:]
    count, lat, width = branch_ref.shape
    rows, cols = kv_ref.shape[1], kv_ref.shape[2] // 2
    branch = branch_ref[...].reshape(count * lat, width)
    all_mixed = product(branch, qo_weights[:, cols:]).astype(BF16)
    for image in range(count):
        keys, values = kv_ref[image, :, :cols], kv_ref[image, :, cols:]
        query = stacked(qm_ref[image, :, :cols], heads)
        probs = softmax_rows(product_right(query, keys))
        grad_mixed = stacked(all_mixed[image * lat : (image + 1) * lat], heads)
        grad_probs = product_right(grad_mixed, values)
        inner = jnp.sum(grad_probs * probs, axis=-1, keepdims=True)
        grad_scores = (probs * (grad_probs - inner)).astype(BF16)
        dquery_ref[image] = unstacked(product(grad_scores, keys), heads).astype(BF16)
        dkv_ref[image, :, :cols] = product_left(grad_scores, query).astype(BF16)
        dkv_ref[image, :, cols:] = product_left(probs.astype(BF16), grad_mixed).astype(BF16)
    back = product_right(dkv_ref[...].reshape(count * rows, 2 * cols), kv_weights[...]).reshape(count, rows, width)
    extra = product_right(dquery_ref[...].reshape(count * lat, cols), qo_weights[:, :cols]) * scale
    extra = extra.reshape(count, lat, width)
    for index, back_ref in enumerate(back_refs):

        @pl.when(pl.program_id(0) == index // count)
        def _(back_ref=back_ref, image=index % count):
            back_ref[0, :patch] = back[image, :patch].astype(BF16)
            back_ref[0, patch:] = (back[image, patch:] + extra[image]).astype(BF16)


def attend_back(pair, mine, theirs, branch, kv, qm, heads, patch, first, steps, per, carried):
    total, rows, cols = kv.shape
    lat, width = branch.shape[1:]
    part = lambda *shape: pl.BlockSpec((per,) + shape, lambda i: (first - i, 0, 0))
    given = list(carried or ())
    dkv, dquery, *backs = pl.pallas_call(
        functools.partial(attend_back_kernel, heads, patch, HEAD ** (-0.5), len(given)),
        grid=(steps,),
        in_specs=[SMALL, ANY, ANY, part(lat, width), part(rows, cols), part(lat, cols)] + [ANY] * len(given),
        out_specs=[part(rows, cols), part(lat, cols // 2)] + [whole((1, rows, width))] * (steps * per),
        out_shape=[
            jax.ShapeDtypeStruct((total, rows, cols), BF16),
            jax.ShapeDtypeStruct((total, lat, cols // 2), BF16),
        ]
        + [jax.ShapeDtypeStruct((1, rows, width), BF16)] * (steps * per),
        scratch_shapes=weight_scratch(mine),
        input_output_aliases={6 + i: i for i in range(len(given))},
        compiler_params=pltpu.CompilerParams(vmem_limit_bytes=VMEM),
        cost_estimate=LITTLE,
    )(pair, mine, theirs, branch, kv, qm, *given)
    return dkv, dquery, backs


def feed_kernel(tile, parts, cot_ref, cot_other_ref, weights_ref, *refs):
    hidden_refs, refs = refs[:parts], refs[parts:]
    all_ref, cots_ref, active_ref, upper_ref, *part_refs, ups, downs, total_ref, sems = refs
    cols = weights_ref.shape[1] // 2
    copies = []
    for index, start in enumerate(range(0, cols, tile)):
        copies.append(pltpu.make_async_copy(weights_ref.at[:, pl.ds(start, tile)], ups.at[index], sems.at[0, index]))
        copies.append(
            pltpu.make_async_copy(weights_ref.at[:, pl.ds(cols + start, tile)], downs.at[index], sems.at[1, index])
        )
    for copy in copies:
        copy.start()
    start = 0
    for hidden_ref in hidden_refs:
        all_ref[start : start + hidden_ref.shape[0]] = hidden_ref[...]
        start += hidden_ref.shape[0]
    cots_ref[: start // 2] = cot_ref[...]
    cots_ref[start // 2 :] = cot_other_ref[...]
    hidden, cot = all_ref[...], cots_ref[...]
    for index in range(cols // tile):
        copies[2 * index].wait()
        copies[2 * index + 1].wait()
        up = ups[index]
        upper = product(hidden, up)
        cdf = 0.5 * (1.0 + lax.erf(upper * (0.5**0.5)))
        slope = cdf + upper * jnp.exp(-0.5 * upper * upper) * (0.5 / math.pi) ** 0.5
        grad_upper = (slope * product(cot, downs[index])).astype(BF16)
        place = slice(index * tile, (index + 1) * tile)
        active_ref[:, place] = (upper * cdf).astype(BF16)
        upper_ref[:, place] = grad_upper
        term = product_right(grad_upper, up)
        if index == 0:
            total_ref[...] = term
        else:
            total_ref[...] += term
    start = 0
    for part_ref in part_refs:
        part_ref[...] = total_ref[start : start + part_ref.shape[0]].astype(BF16)
        start += part_ref.shape[0]


def feed(hidden, cot, cot_other, weights):
    width = cot.shape[1]
    rows = 2 * cot.shape[0]
    cols = weights.shape[1] // 2
    tile = 256 if cols % 256 == 0 else math.gcd(cols, 384)
    shapes = [(rows, width)] * 2 + [(rows, cols)] * 2 + [part.shape for part in hidden]
    return pl.pallas_call(
        functools.partial(feed_kernel, tile, len(hidden)),
        grid=(1,),
        in_specs=[whole(cot.shape)] * 2 + [ANY] + [whole(part.shape) for part in hidden],
        out_specs=[whole(shape) for shape in shapes],
        out_shape=[jax.ShapeDtypeStruct(shape, BF16) for shape in shapes],
        scratch_shapes=[pltpu.VMEM((cols // tile, width, tile), BF16)] * 2
        + [pltpu.VMEM((rows, width), F32), pltpu.SemaphoreType.DMA((2, cols // tile))],
        compiler_params=pltpu.CompilerParams(vmem_limit_bytes=VMEM),
        cost_estimate=LITTLE,
    )(cot, cot_other, weights, *hidden)


def feed_out_kernel(active_ref, weights_ref, own_ref, other_ref):
    rows = own_ref.shape[0]
    own_ref[...] = product_right(active_ref[:rows], weights_ref[...]).astype(BF16)
    other_ref[...] = product_right(active_ref[rows:], weights_ref[...]).astype(BF16)


def feed_out(active, weights):
    rows, cols = active.shape
    width = weights.shape[0]
    return pl.pallas_call(
        feed_out_kernel,
        grid=(1,),
        in_specs=[whole(active.shape), pl.BlockSpec((width, cols), lambda i: (0, 1))],
        out_specs=[whole((rows // 2, width))] * 2,
        out_shape=[jax.ShapeDtypeStruct((rows // 2, width), BF16)] * 2,
        compiler_params=pltpu.CompilerParams(vmem_limit_bytes=VMEM),
        cost_estimate=LITTLE,
    )(active, weights)


def feed_grads_kernel(hidden_ref, cot_ref, upper_ref, active_ref, to_ref):
    half = upper_ref.shape[1]
    to_ref[:, :half] = product_left(hidden_ref[...], upper_ref[...]).astype(BF16)
    to_ref[:, half:] = product_left(cot_ref[...], active_ref[...]).astype(BF16)


def row_tiles(width):
    return width // math.gcd(width, 384)


def feed_grads(hidden, cot, upper, active):
    rows, width = hidden.shape
    cols = upper.shape[1]
    steps = row_tiles(width)
    left = pl.BlockSpec((rows, width // steps), lambda i: (0, i))
    right = pl.BlockSpec((rows, cols), lambda i: (0, 0))
    return pl.pallas_call(
        feed_grads_kernel,
        grid=(steps,),
        in_specs=[left, left, right, right],
        out_specs=pl.BlockSpec((width // steps, 2 * cols), lambda i: (i, 0)),
        out_shape=jax.ShapeDtypeStruct((width, 2 * cols), BF16),
        compiler_params=pltpu.CompilerParams(vmem_limit_bytes=VMEM),
        cost_estimate=LITTLE,
    )(hidden, cot, upper, active)


def add_pieces_kernel(first_ref, *refs):
    *piece_refs, to_ref = refs
    rows = piece_refs[0].shape[0]
    for index, piece_ref in enumerate(piece_refs):
        place = slice(index * rows, (index + 1) * rows)
        to_ref[place] = (first_ref[place].astype(F32) + piece_ref[...].astype(F32)).astype(BF16)


def pick_kernel(*refs):
    *from_refs, to_ref = refs
    rows = from_refs[0].shape[1]
    for index, from_ref in enumerate(from_refs):
        to_ref[index * rows : (index + 1) * rows] = from_ref[0]


def pick(parts, block, rows):
    width = parts[0].shape[2]
    return pl.pallas_call(
        pick_kernel,
        grid=(1,),
        in_specs=[pl.BlockSpec((1, rows, width), lambda i: (0, block, 0))] * len(parts),
        out_specs=pl.BlockSpec((len(parts) * rows, width), lambda i: (0, 0)),
        out_shape=jax.ShapeDtypeStruct((len(parts) * rows, width), BF16),
        compiler_params=pltpu.CompilerParams(vmem_limit_bytes=VMEM),
        cost_estimate=LITTLE,
    )(*parts)


def attend_grads_kernel(patch, scale, pair_ref, joined_ref, branch_ref, dkv_ref, dquery_ref, qm_ref, keep_ref, *give_refs):
    count, rows, tile = joined_ref.shape
    lat, cols = rows - patch, dquery_ref.shape[2]
    joined = joined_ref[...].reshape(count * rows, tile)
    latent = joined_ref[:, patch:].reshape(count * lat, tile)
    kv = product_left(joined, dkv_ref[...].reshape(count * rows, 2 * cols)).astype(BF16)
    query = (product_left(latent, dquery_ref[...].reshape(count * lat, cols)) * scale).astype(BF16)
    out = product_left(branch_ref[...], qm_ref[:, :, cols:].reshape(count * lat, cols)).astype(BF16)

    @pl.when(pair_ref[0] == 0)
    def _():
        keep_ref[...] = kv

    @pl.when(pair_ref[0] == 1)
    def _():
        keep_ref[:, :cols] = query
        keep_ref[:, cols:] = out

    for step, give_ref in enumerate(give_refs):

        @pl.when((pl.program_id(0) == step) & (pair_ref[0] == 0))
        def _(give_ref=give_ref):
            give_ref[:, :cols] = query
            give_ref[:, cols:] = out

        @pl.when((pl.program_id(0) == step) & (pair_ref[0] == 1))
        def _(give_ref=give_ref):
            give_ref[...] = kv


def attend_grads(pair, joined, branch, dkv, dquery, qm, patch):
    total, rows, width = joined.shape
    lat, cols = rows - patch, dkv.shape[2]
    steps = row_tiles(width)
    tile = pl.BlockSpec((width // steps, cols), lambda i: (i, 0))
    return pl.pallas_call(
        functools.partial(attend_grads_kernel, patch, HEAD ** (-0.5)),
        grid=(steps,),
        in_specs=[
            SMALL,
            pl.BlockSpec((total, rows, width // steps), lambda i: (0, 0, i)),
            pl.BlockSpec((total * lat, width // steps), lambda i: (0, i)),
            whole(dkv.shape), whole(dquery.shape), whole(qm.shape),
        ],
        out_specs=[tile] + [whole((width // steps, cols))] * steps,
        out_shape=[jax.ShapeDtypeStruct((width, cols), BF16)] + [jax.ShapeDtypeStruct((width // steps, cols), BF16)] * steps,
        compiler_params=pltpu.CompilerParams(vmem_limit_bytes=VMEM),
        cost_estimate=LITTLE,
    )(pair, joined, branch, dkv, dquery, qm)


def whole(shape):
    return pl.BlockSpec(shape, lambda *_: (0,) * len(shape))


def once(kernel, operands, shapes, specs=None):
    specs = specs or [whole(operand.shape) for operand in operands]
    return pl.pallas_call(
        kernel,
        grid=(1,),
        in_specs=specs,
        out_specs=[whole(shape) for shape, _ in shapes],
        out_shape=[jax.ShapeDtypeStruct(shape, kind) for shape, kind in shapes],
        compiler_params=pltpu.CompilerParams(vmem_limit_bytes=VMEM),
        cost_estimate=LITTLE,
    )(*operands)


def attended_kernel(small_ref, latent_ref, *refs):
    *part_refs, attended_ref, hidden_ref = refs
    images = latent_ref.shape[0]
    each = len(part_refs) // images
    for image in range(images):
        total = latent_ref[image].astype(F32)
        for part_ref in part_refs[image * each : (image + 1) * each]:
            total = total + part_ref[0].astype(F32)
        attended_ref[image] = total
        hidden_ref[image] = normed(total, small_ref[0, 2:3], small_ref[1, 2:3]).astype(BF16)


def summed_kernel(other_ref, *refs):
    count = len(refs) // 2
    rows = other_ref.shape[0] // count
    for index in range(count):
        other = other_ref[index * rows : (index + 1) * rows].astype(F32)
        refs[count + index][...] = (refs[index][...].astype(F32) + other).astype(BF16)


def through_kernel(*refs):
    for index in range(2):
        left_ref, right_ref, to_ref = refs[2 * index], refs[2 * index + 1], refs[4 + index]
        to_ref[...] = (left_ref[...].astype(F32) + right_ref[...].astype(F32)).astype(BF16)


def norm_back(rows, gain, grad):
    average = jnp.mean(rows, axis=-1, keepdims=True)
    centred = rows - average
    inverse = lax.rsqrt(jnp.mean(centred * centred, axis=-1, keepdims=True) + EPSILON)
    unit = centred * inverse
    scaled = grad * gain
    first = jnp.mean(scaled, axis=-1, keepdims=True)
    second = jnp.mean(scaled * unit, axis=-1, keepdims=True)
    back = inverse * (scaled - first - unit * second)
    return back, jnp.sum(grad * unit, axis=0, keepdims=True), jnp.sum(grad, axis=0, keepdims=True)


def branch_kernel(small_ref, attended_ref, cot_ref, *refs):
    *part_refs, grad_ref, branch_ref, sums_ref = refs
    images, lat, width = attended_ref.shape
    grad = sum(part_ref[...].astype(F32) for part_ref in part_refs)
    back, gain, bias = norm_back(attended_ref[...].reshape(images * lat, width), small_ref[0, 2:3], grad)
    total = (cot_ref[...].reshape(images * lat, width).astype(F32) + back).reshape(images, lat, width)
    grad_ref[...] = total
    branch_ref[...] = total.astype(BF16)
    sums_ref[0:1] = gain
    sums_ref[1:2] = bias


def rows_back_kernel(small_ref, sums_two_ref, media_ref, latent_ref, grad_ref, *refs):
    *part_refs, media_to_ref, latent_to_ref, sums_ref = refs
    images, patch, _ = media_ref.shape
    each = len(part_refs) // images
    totals = None
    for image in range(images):
        parts = part_refs[image * each : (image + 1) * each]
        grad = sum(part_ref[0, :patch].astype(F32) for part_ref in parts)
        media, gain_zero, bias_zero = norm_back(media_ref[image].astype(F32), small_ref[0, 0:1], grad)
        media_to_ref[image] = media
        grad = sum(part_ref[0, patch:].astype(F32) for part_ref in parts)
        latent, gain_one, bias_one = norm_back(latent_ref[image].astype(F32), small_ref[0, 1:2], grad)
        latent_to_ref[image] = grad_ref[image] + latent
        terms = gain_zero, gain_one, bias_zero, bias_one
        totals = terms if totals is None else [left + right for left, right in zip(totals, terms)]
    for row, total in zip((0, 1, 3, 4), totals):
        sums_ref[row : row + 1] = total
    sums_ref[2:3] = sums_two_ref[0:1]
    sums_ref[5:6] = sums_two_ref[1:2]


def in_thirds(values):
    parts, rest = [], values
    for _ in range(3):
        part = lax.reduce_precision(rest, exponent_bits=8, mantissa_bits=7)
        parts.append(part.astype(BF16))
        rest = rest - part
    return jnp.stack(parts)


def local(media_features, latents, cotangent, image_counts, w_query, w_key, w_value, w_out, w_up, w_down,
          norm_gains, norm_biases):
    devices_x, devices_y = lax.axis_size("gx"), lax.axis_size("gy")
    masks = far_masks()
    img_count, lat, width = latents.shape
    patch = media_features.shape[1]
    rows = patch + lat
    shard = w_query.shape[0]
    head_width = width // devices_y
    heads = 2 * head_width // HEAD
    pair = (lax.axis_index("gy") % 2).astype(jnp.int32).reshape(1)
    ff_width = w_up.shape[1] // devices_y
    total = img_count * len(masks)

    four_width = 4 * head_width
    small = in_thirds(jnp.stack([norm_gains, norm_biases])).reshape(-1)
    extra = -(-small.size // (16 * four_width)) * 16
    small = jnp.pad(small, (0, extra * four_width - small.size)).reshape(extra, four_width)
    four = regroup(small, devices_y, w_key, w_value, w_query, w_out.T)
    four = lax.all_to_all(four, "gy", split_axis=0, concat_axis=0, tiled=True)
    mine = lax.all_gather(four[:, extra:].reshape(devices_y * shard, four_width), "gx", axis=0, tiled=True)

    two = jnp.concatenate(
        [part.reshape(shard, devices_y, ff_width).transpose(1, 0, 2) for part in (w_up, w_down.T)], axis=2
    )
    two, four = tie(two, four)
    small = four[:, :extra].reshape(devices_y, -1)[:, : 18 * shard].reshape(devices_y, 3, 6 * shard)
    small = gather_small(jnp.sum(small.astype(F32), axis=1).reshape(1, -1), "gx")
    small = small.reshape(devices_x, devices_y, 6, shard).transpose(2, 0, 1, 3).reshape(2, 3, width)

    two = lax.all_to_all(two, "gy", split_axis=0, concat_axis=0, tiled=True)
    live = (jnp.arange(img_count, dtype=jnp.int32) < image_counts[0]).astype(BF16)
    cot_own = cotangent * live[:, None, None]
    own = [
        jnp.concatenate([part[i : i + 1] for part in (media_features, latents, cot_own)], axis=1) for i in range(img_count)
    ]
    two, small, *own = tie(two, small, *own)
    ff_rows = two.reshape(devices_y * shard, 2 * ff_width)
    gains, biases = small[0], small[1]

    raw = {(0, i): own[i] for i in range(img_count)}
    if len(masks) == 4 and img_count == 2:
        slots = [(0, 0), (0, 1), (2, 0), (4, 0), (2, 1), (4, 1), (6, 0), (6, 1)]
        raw[2, 0], raw[4, 0], later = tie(swap(own[0], 2), swap(own[0], 4), own[1])
        raw[2, 0], raw[4, 0], ff_rows, mine = tie(raw[2, 0], raw[4, 0], ff_rows, mine)
        raw[2, 1], raw[4, 1], raw[6, 0] = swap(later, 2), swap(later, 4), swap(raw[2, 0], 4)
    else:
        slots = [(mask, i) for mask in masks for i in range(img_count)]
        for mask in masks[1:]:
            raw.update({(mask, i): swap(own[i], mask) for i in range(img_count)})
    ff_mine = lax.all_gather(ff_rows, "gx", axis=0, tiled=True)
    theirs = swap(mine, 1)

    steps, carried, out_parts = total // img_count, None, {}
    for step in range(steps):
        here = slots[step * img_count : (step + 1) * img_count]
        if carried:
            carried[0], *raws = tie(carried[0], *[raw[slot] for slot in here])
            raw.update(dict(zip(here, raws)))
        if (4, 1) in here and (6, 1) not in raw:
            raw[6, 1] = swap(raw[4, 1], 2)
        *carried, first_part, second_part = attend(
            pair, mine, theirs, small, [raw[slot] for slot in here], heads, patch, rows, step, total, carried
        )
        out_parts.update(dict(zip(here, (first_part, second_part))))
    joined_all, kv_all, qm_all = carried

    qm_all, *parts = tie(qm_all, *[raw[mask, i] for mask in masks for i in range(img_count)])
    cot_own_all = pick(parts, rows // lat, lat)
    out_parts = [
        swap(out_parts[mask, i], mask) if mask else out_parts[mask, i] for i in range(img_count) for mask in masks
    ]
    like_latents = lambda kind: (latents.shape, kind)
    attended, hidden_own = once(
        attended_kernel, [small, latents, *out_parts], [like_latents(F32), like_latents(BF16)]
    )
    hidden_own, cot_own_all = tie(hidden_own, cot_own_all)
    cot_other = swap(cot_own_all, 1)
    hidden = [part.reshape(img_count * lat, width) for part in spread(hidden_own).values()]
    hidden.append(swap(jnp.concatenate(hidden), 1))

    def plus(left, right):
        return (left.astype(F32) + right.astype(F32)).astype(BF16)

    def collect_pairs(parts):
        parts = [part.reshape(img_count, lat, width) for part in parts]
        return [parts[0]] + [swap(part, mask) for mask, part in zip(masks[1:], parts[1:])]

    total_of = lambda parts: sum(part.astype(F32) for part in parts)

    def summed(parts, other):
        return once(summed_kernel, [swap(other, 1), *parts], [(part.shape, BF16) for part in parts])

    hidden, cot_all, active, grad_upper, *hidden_parts, hidden_other = feed(hidden, cot_own_all, cot_other, ff_mine)
    ff_grads = feed_grads(hidden, cot_all, grad_upper, active)
    ff_grads, *hidden_parts = tie(ff_grads, *hidden_parts)
    hidden_parts = summed(hidden_parts, hidden_other)
    ff_part = lax.psum_scatter(ff_grads, "gx", scatter_dimension=0, tiled=True)
    hidden_parts = collect_pairs(hidden_parts)
    hidden_parts = [part.reshape(img_count * lat, width) for part in hidden_parts]
    grad_attended, grad_branch, sums_two = once(
        branch_kernel, [small, attended, cot_own, *hidden_parts],
        [like_latents(F32), like_latents(BF16), ((2, width), F32)],
    )
    branch = spread(grad_branch)
    ffn_parts = feed_out(active, ff_mine)
    *branch, ffn_part, ffn_other, ff_grads = tie(*branch.values(), *ffn_parts, ff_grads)
    branch = jnp.concatenate([branch[masks.index(mask)][i : i + 1] for mask, i in slots])

    arrays = pair, mine, theirs, branch, kv_all, qm_all, heads, patch
    back, carried, step = {}, None, steps - 1
    for count in (1, steps - 2, 1):
        *carried, results = attend_back(*arrays, step, count, img_count, carried)
        for index, part in enumerate(results):
            back[slots[(step - index // img_count) * img_count + index % img_count]] = part
        step -= count
    dkv_all, dquery_all = carried

    if (6, 0) in back:
        last = swap(back[6, 0], 4), swap(back[6, 1], 2)
        dkv_all, *last = tie(dkv_all, *last)
        through = once(
            through_kernel, [back[2, 0], last[0], back[4, 1], last[1]], [(back[2, 0].shape, BF16)] * 2
        )
    dkv_all, ff_part = tie(dkv_all, ff_part)
    keep, *give = attend_grads(
        pair, joined_all, branch.reshape(total * lat, width), dkv_all, dquery_all, qm_all, patch
    )
    if len(masks) == 4 and img_count == 2:
        keep, *direct = tie(keep, swap(back[4, 0], 4), swap(back[2, 1], 2), *through)
        through = direct[2:]
        arrived = [back[0, 0], swap(through[0], 2), direct[0], back[0, 1], direct[1], swap(through[1], 4)]
    else:
        arrived = [swap(back[mask, i], mask) if mask else back[mask, i] for i in range(img_count) for mask in masks]
    give = [swap(part, 1) for part in give]
    (at_grads,) = once(add_pieces_kernel, [keep, *give], [(keep.shape, BF16)])
    at_grads, ffn_other = tie(at_grads, ffn_other)
    shares = lax.psum_scatter(at_grads, "gx", scatter_dimension=0, tiled=True)
    ffn_part = ffn_part.reshape(len(masks), img_count * lat, width)
    ffn_parts = summed([ffn_part[i] for i in range(len(masks))], ffn_other)

    def home(part):
        return lax.all_to_all(part.reshape(devices_y, shard, -1), "gy", split_axis=0, concat_axis=0, tiled=True)

    each = len(arrived)
    *arrived, ff_part = tie(*arrived, *ffn_parts, ff_part)
    arrived, ffn_parts = arrived[:each], arrived[each:]
    grad_media, grad_latents, sums = once(
        rows_back_kernel, [small, sums_two, media_features, latents, grad_attended, *arrived],
        [(media_features.shape, F32), like_latents(F32), ((6, width), F32)],
    )
    sums = sum_small(sums)
    place = lax.axis_index("gx") * devices_y + lax.axis_index("gy")
    sums = lax.dynamic_slice_in_dim(sums, place * shard, shard, axis=1)

    shares, sums, ff_part, *ffn_parts = tie(shares, sums, home(ff_part), *collect_pairs(ffn_parts))
    grad_key, grad_value, grad_query, grad_out = ungroup(home(shares), 4, True)
    outputs = ((attended + total_of(ffn_parts)) * live.astype(F32)[:, None, None]).astype(BF16)
    grad_up, grad_down = ungroup(ff_part, 2, False)
    grad_down = grad_down.T
    return (
        outputs, grad_media, grad_latents, grad_query, grad_key, grad_value, grad_out.T, grad_up, grad_down,
        sums[:3], sums[3:],
    )


def solution(mesh):
    split = ("gx", "gy")
    images, first, second = P(split, None, None), P(split, None), P(None, split)
    return jax.shard_map(
        local,
        mesh=mesh,
        in_specs=(images, images, images, P(split), first, first, first, second, first, second, second, second),
        out_specs=(images, images, images, first, first, first, second, first, second, second, second),
        check_vma=False,
    )
```

time: 502 us -> 418 us (0.83)
  other arithmetic: 47.3 us -> 10.8 us
  waiting for transfers between devices: 169 us -> 153 us
  local copies, waits for them, and re-layouts: 32.9 us -> 20.7 us
  matrix products: 7.36 us -> 0 us
  starting transfers between devices: 69.9 us -> 63.9 us
    ppermute x42 -> x48, waiting for transfers between devices: 147 us -> 133 us  [swap(): return lax.ppermute(block, axis, [(i, i ^ mask) for i in range(count)])]
    reduce_sum x10 -> x0, other arithmetic: 12.3 us -> none  [the longest x2 5.12 us: norm_back(): second = jnp.mean(scaled * unit, axis=-1, keepdims=True)]
    another operation x8 -> x0, local copies, waits for them, and re-layouts: 10.4 us -> none  [the longest x7 7.8 us: local(): jnp.stack([gain_zero, gain_one, gain_two, bias_zero, bias_one, bias_two])]
    all_to_all x2 -> x0, starting transfers between devices: 9.14 us -> none  [local(): lax.all_to_all(part, 'gx', split_axis=0, concat_axis=0, tiled=True)]
    dot_general x2 -> x0, matrix products: 7.36 us -> none  [product_right(): lax.dot_general(left, right, (((1,), (1,)), ((), ())), preferred_element_...]
    add x10 -> x3, other arithmetic: 7.03 us -> 0.9 us  [the longest x1 0.81 us: sum_small(): rows = rows + swap(rows, 1)]
    convert_element_type x6 -> x2, other arithmetic: 7.85 us -> 2.11 us  [the longest x1 2.11 us: local(): ((attended + total_of(ffn_parts)) * live.astype(F32)[:, None, None]).asty...]
    pallas_call x13, Pallas kernels: 66.6 us -> 72.2 us  [the longest x7 29.3 us: once(): pl.pallas_call(kernel, grid=(1,), in_specs=specs, out_specs=[whole(shape)...]
  transfers between devices with their start and end apart: 51 -> 56, of which waited for: 28 -> 31; matrix products, arithmetic and copies ran while one was open for 15% -> 4% of each run, Pallas kernels for 24% -> 28%
where the time goes in v3:
time: 418 us; the launch traced here: 414 us
  waiting for transfers between devices  153 us (37%)
  Pallas kernels  150 us (36%)
  starting transfers between devices  63.9 us (15%)
  local copies, waits for them, and re-layouts  20.7 us (5%)
  between operations  15.3 us (4%)
  other arithmetic  10.8 us (3%)
    ppermute x48, waiting for transfers between devices, swap(): return lax.ppermute(block, axis, [(i, i ^ mask) for i in range(count)])  133 us
    ppermute x48, starting transfers between devices, swap(): return lax.ppermute(block, axis, [(i, i ^ mask) for i in range(count)])  47.2 us
    pallas_call x4, Pallas kernels, attend(): pl.pallas_call(functools.partial(attend_kernel, heads, patch, HEAD ** (-0...  34.1 us
    pallas_call x3, Pallas kernels, attend_back(): pl.pallas_call(functools.partial(attend_back_kernel, heads, patch, HEAD *...  32.4 us
    pallas_call x7, Pallas kernels, once(): pl.pallas_call(kernel, grid=(1,), in_specs=specs, out_specs=[whole(shape)...  29.3 us
    pallas_call x1, Pallas kernels, feed(): pl.pallas_call(functools.partial(feed_kernel, tile, len(hidden)), grid=(1...  14.8 us
    pallas_call x1, Pallas kernels, attend_grads(): pl.pallas_call(functools.partial(attend_grads_kernel, patch, HEAD ** (-0....  14.6 us
    unnamed x103, local copies, waits for them, and re-layouts  14.4 us
  transfers between devices with their start and end apart: 56, of which 31 were waited for; matrix products, arithmetic and copies ran while one was open for 4% of the time, Pallas kernels for 28%

profile of v3, /device:TPU:0, one launch (start us, length us, event | category | flops | bytes accessed | tf_op | source)
XLA Modules:
  0.0 413.9 jit_solution(6355749832514690696)
XLA Ops:
  8.7 2.1 shard_map.203
  10.8 5.3 %all-to-all-start = ((bf16[8,64,768]{2,1,0:T(8,128)(2,1)}), bf16[8,64,768]{2,1,0:T(8,128)(2,1)S(1)}, u32[]{:S(2)}, u32[]{:S(2)}) async-start(bf16[8,64,768]{2,1,0:T(8,128)(2,1)} %shard_map.203), calls=%async_computation | async-start | bytes 1572864 | tf_op jit(solution)/shard_map/all_to_all | solution.py:584
  20.6 8.1 %all-to-all-done = bf16[8,64,768]{2,1,0:T(8,128)(2,1)S(1)} async-done(((bf16[8,64,768]{2,1,0:T(8,128)(2,1)}), bf16[8,64,768]{2,1,0:T(8,128)(2,1)S(1)}, u32[]{:S(2)}, u32[]{:S(2)}) %all-to-all-start) | async-done | bytes 786464 | tf_op jit(solution)/shard_map/all_to_all | solution.py:584
  29.0 1.6 collective-permute-start
  32.3 3.6 all-to-all-start.1
  37.4 2.6 collective-permute-start.1
  39.9 2.4 pad_maximum_fusion.2
  42.4 1.9 collective-permute-done.1
  45.9 6.7 %all-to-all-done.1 = bf16[8,48,1536]{2,1,0:T(8,128)(2,1)S(1)} async-done(((bf16[8,48,1536]{2,1,0:T(8,128)(2,1)}), bf16[8,48,1536]{2,1,0:T(8,128)(2,1)S(1)}, u32[]{:S(2)}, u32[]{:S(2)}) %all-to-all-start.1) | async-done | bytes 1179680 | tf_op jit(solution)/shard_map/all_to_all | solution.py:595
  53.8 25.6 %collective-permute-done.2.refs_0_.refs_2_ = bf16[1,384,1536]{2,1,0:T(8,128)(2,1)S(1)} collective-permute-done((bf16[1,384,1536]{2,1,0:T(8,128)(2,1)S(1)}, bf16[1,384,1536]{2,1,0:T(8,128)(2,1)S(1)}, u32[]{:S(2)}, u32[]{:S(2)}) %collective-permute-start.2) | collective-permute-done | bytes 1179680 | tf_op jit(solution)/shard_map/ppermute | solution.py:37
  81.5 1.5 collective-permute-start.7
  83.0 1.5 collective-permute-start.8
  87.6 8.8 %shard_map.204 = (bf16[8,320,1536]{2,1,0:T(8,128)(2,1)}, bf16[8,320,768]{2,1,0:T(8,128)(2,1)}, bf16[8,64,768]{2,1,0:T(8,128)(2,1)}, bf16[1,64,1536]{2,1,0:T(8,128)(2,1)}, bf16[1,64,1536]{2,1,0:T(8,128)(2,1)}) custom-call(s32[1]{0:T(128)} %bitcast.8.pair_ref, bf16[1536,768]{1,0:T(8,128)(2,1)} %all-gather.3.cloned.1.call-done.mine_ref, ...), custom_call_target="tpu_custom_call" | custom-call | flops 1024 | bytes 1024 | tf_op jit(solution)/shard_map/pallas_call | solution.py:206
  96.4 8.3 %shard_map.205 = (bf16[8,320,1536]{2,1,0:T(8,128)(2,1)}, bf16[8,320,768]{2,1,0:T(8,128)(2,1)}, bf16[8,64,768]{2,1,0:T(8,128)(2,1)}, bf16[1,64,1536]{2,1,0:T(8,128)(2,1)}, bf16[1,64,1536]{2,1,0:T(8,128)(2,1)}) custom-call(s32[1]{0:T(128)} %bitcast.8.pair_ref, ...), custom_call_target="tpu_custom_call", output_to_operand_aliasing={{0}: (6, {}), {1}: (7, {}), {2}: (8, {})} | custom-call | flops 1024 | bytes 1024 | tf_op jit(solution)/shard_map/pallas_call | solution.py:206
  104.7 5.5 %collective-permute-done.7.refs_0_.refs_3_ = bf16[1,384,1536]{2,1,0:T(8,128)(2,1)} collective-permute-done((bf16[1,384,1536]{2,1,0:T(8,128)(2,1)}, bf16[1,384,1536]{2,1,0:T(8,128)(2,1)}, u32[]{:S(2)}, u32[]{:S(2)}) %collective-permute-start.7) | collective-permute-done | bytes 1179680 | tf_op jit(solution)/shard_map/ppermute | solution.py:37
  110.2 2.0 collective-permute-done.8.refs_1_.refs_5_
  112.7 1.5 collective-permute-start.5
  114.2 1.5 collective-permute-start.6
  115.6 8.8 %shard_map.206 = (bf16[8,320,1536]{2,1,0:T(8,128)(2,1)}, bf16[8,320,768]{2,1,0:T(8,128)(2,1)}, bf16[8,64,768]{2,1,0:T(8,128)(2,1)}, bf16[1,64,1536]{2,1,0:T(8,128)(2,1)}, bf16[1,64,1536]{2,1,0:T(8,128)(2,1)}) custom-call(s32[1]{0:T(128)} %bitcast.8.pair_ref, ...), custom_call_target="tpu_custom_call", output_to_operand_aliasing={{0}: (6, {}), {1}: (7, {}), {2}: (8, {})} | custom-call | flops 1024 | bytes 1024 | tf_op jit(solution)/shard_map/pallas_call | solution.py:206
  125.1 12.2 %collective-permute-done.9.refs_0_.refs_6_ = bf16[1,384,1536]{2,1,0:T(8,128)(2,1)S(1)} collective-permute-done((bf16[1,384,1536]{2,1,0:T(8,128)(2,1)}, bf16[1,384,1536]{2,1,0:T(8,128)(2,1)S(1)}, u32[]{:S(2)}, u32[]{:S(2)}) %collective-permute-start.9) | collective-permute-done | bytes 1179680 | tf_op jit(solution)/shard_map/ppermute | solution.py:37
  137.3 1.5 collective-permute-start.13
  138.8 2.5 collective-permute-done.10.refs_1_.refs_7_
  142.3 8.3 %shard_map.207 = (bf16[8,320,1536]{2,1,0:T(8,128)(2,1)}, bf16[8,320,768]{2,1,0:T(8,128)(2,1)}, bf16[8,64,768]{2,1,0:T(8,128)(2,1)}, bf16[1,64,1536]{2,1,0:T(8,128)(2,1)}, bf16[1,64,1536]{2,1,0:T(8,128)(2,1)}) custom-call(s32[1]{0:T(128)} %bitcast.8.pair_ref, ...), custom_call_target="tpu_custom_call", output_to_operand_aliasing={{0}: (6, {}), {1}: (7, {}), {2}: (8, {})} | custom-call | flops 1024 | bytes 1024 | tf_op jit(solution)/shard_map/pallas_call | solution.py:206
  150.6 1.6 collective-permute-start.11
  153.5 2.7 shard_map.209.cot_ref
  157.4 2.1 collective-permute-done.14.refs_7_
  160.2 2.8 shard_map.208
  166.5 7.2 %collective-permute-done.16 = bf16[2,64,1536]{2,1,0:T(8,128)(2,1)S(1)} collective-permute-done((bf16[2,64,1536]{2,1,0:T(8,128)(2,1)}, bf16[2,64,1536]{2,1,0:T(8,128)(2,1)S(1)}, u32[]{:S(2)}, u32[]{:S(2)}) %collective-permute-start.16) | collective-permute-done | bytes 393248 | tf_op jit(solution)/shard_map/ppermute | solution.py:37
  173.9 4.2 %collective-permute-done.18 = bf16[2,64,1536]{2,1,0:T(8,128)(2,1)S(1)} collective-permute-done((bf16[2,64,1536]{2,1,0:T(8,128)(2,1)}, bf16[2,64,1536]{2,1,0:T(8,128)(2,1)S(1)}, u32[]{:S(2)}, u32[]{:S(2)}) %collective-permute-start.18) | collective-permute-done | bytes 393248 | tf_op jit(solution)/shard_map/ppermute | solution.py:37
  179.5 3.5 collective-permute-done.19.refs_4_
  183.0 14.8 %shard_map.210 = (bf16[1024,1536]{1,0:T(8,128)(2,1)}, bf16[1024,1536]{1,0:T(8,128)(2,1)}, bf16[1024,768]{1,0:T(8,128)(2,1)}, bf16[1024,768]{1,0:T(8,128)(2,1)}, ...) custom-call(bf16[512,1536]{1,0:T(8,128)(2,1)} %shard_map.209.cot_ref, ...), custom_call_target="tpu_custom_call" | custom-call | flops 1024 | bytes 1024 | tf_op jit(solution)/shard_map/pallas_call | solution.py:329
  197.8 9.6 %shard_map.211 = bf16[1536,1536]{1,0:T(8,128)(2,1)} custom-call(bf16[1024,1536]{1,0:T(8,128)(2,1)} %get-tuple-element.213.hidden_ref, bf16[1024,1536]{1,0:T(8,128)(2,1)} %get-tuple-element.214.cot_ref, bf16[1024,768]{1,0:T(8,128)(2,1)} %get-tuple-element.215.upper_ref, bf16[1024,768]{1,0:T(8,128)(2,1)} %get-tuple-element.216.active_ref), custom_call_target="tpu_custom_call" | custom-call | flops 1024 | bytes 1024 | tf_op jit(solution)/shard_map/pallas_call | solution.py:378
  208.9 3.3 collective-permute-done.20.other_ref
  213.3 3.1 shard_map.212
  216.4 1.7 collective-permute-start.21
  219.9 8.7 %collective-permute-done.21 = bf16[2,64,1536]{2,1,0:T(8,128)(2,1)S(1)} collective-permute-done((bf16[2,64,1536]{2,1,0:T(8,128)(2,1)}, bf16[2,64,1536]{2,1,0:T(8,128)(2,1)S(1)}, u32[]{:S(2)}, u32[]{:S(2)}) %collective-permute-start.21) | collective-permute-done | bytes 393248 | tf_op jit(solution)/shard_map/ppermute | solution.py:37
  228.6 9.1 %collective-permute-done.22 = bf16[2,64,1536]{2,1,0:T(8,128)(2,1)S(1)} collective-permute-done((bf16[2,64,1536]{2,1,0:T(8,128)(2,1)}, bf16[2,64,1536]{2,1,0:T(8,128)(2,1)S(1)}, u32[]{:S(2)}, u32[]{:S(2)}) %collective-permute-start.22) | collective-permute-done | bytes 393248 | tf_op jit(solution)/shard_map/ppermute | solution.py:37
  238.5 3.6 shard_map.213
  244.2 1.5 collective-permute-start.26
  245.6 5.9 %shard_map.214 = (bf16[512,1536]{1,0:T(8,128)(2,1)}, bf16[512,1536]{1,0:T(8,128)(2,1)}) custom-call(bf16[1024,768]{1,0:T(8,128)(2,1)} %get-tuple-element.216.active_ref, bf16[1536,1536]{1,0:T(8,128)(2,1)} %all-gather.5.cloned.1.call-done.weights_ref), custom_call_target="tpu_custom_call" | custom-call | flops 1024 | bytes 1024 | tf_op jit(solution)/shard_map/pallas_call | solution.py:351
  251.6 2.8 collective-permute-done.24
  254.4 7.3 %collective-permute-done.25 = bf16[2,64,1536]{2,1,0:T(8,128)(2,1)S(1)} collective-permute-done((bf16[2,64,1536]{2,1,0:T(8,128)(2,1)}, bf16[2,64,1536]{2,1,0:T(8,128)(2,1)S(1)}, u32[]{:S(2)}, u32[]{:S(2)}) %collective-permute-start.25) | collective-permute-done | bytes 393248 | tf_op jit(solution)/shard_map/ppermute | solution.py:37
  263.0 8.9 %shard_map.215 = (bf16[8,320,768]{2,1,0:T(8,128)(2,1)}, bf16[8,64,384]{2,1,0:T(8,128)(2,1)}, bf16[1,320,1536]{2,1,0:T(8,128)(2,1)}, bf16[1,320,1536]{2,1,0:T(8,128)(2,1)}) custom-call(s32[1]{0:T(128)} %bitcast.8.pair_ref, bf16[1536,768]{1,0:T(8,128)(2,1)} %all-gather.3.cloned.1.call-done.mine_ref, bf16[1536,768]{1,0:T(8,128)(2,1)} %copy-done, ...), custom_call_target="tpu_custom_call" | custom-call | flops 1024 | bytes 1024 | tf_op jit(solution)/shard_map/pallas_call | solution.py:264
  273.8 14.6 %shard_map.216 = (bf16[8,320,768]{2,1,0:T(8,128)(2,1)}, bf16[8,64,384]{2,1,0:T(8,128)(2,1)}, bf16[1,320,1536]{2,1,0:T(8,128)(2,1)}, bf16[1,320,1536]{2,1,0:T(8,1...) custom-call(s32[1]{0:T(128)} %bitcast.8.pair_ref, ...), custom_call_target="tpu_custom_call", output_to_operand_aliasing={{0}: (6, {}), {1}: (7, {})} | custom-call | flops 1024 | bytes 1024 | tf_op jit(solution)/shard_map/pallas_call | solution.py:264
  290.7 8.9 %shard_map.217 = (bf16[8,320,768]{2,1,0:T(8,128)(2,1)}, bf16[8,64,384]{2,1,0:T(8,128)(2,1)}, bf16[1,320,1536]{2,1,0:T(8,128)(2,1)}, bf16[1,320,1536]{2,1,0:T(8,128)(2,1)}) custom-call(s32[1]{0:T(128)} %bitcast.8.pair_ref, bf16[1536,768]{1,0:T(8,128)(2,1)} %all-gather.3.cloned.1.call-done.mine_ref, ...), custom_call_target="tpu_custom_call", output_to_operand_aliasing={{0}: (6, {}), {1}: (7, {})} | custom-call | flops 1024 | bytes 1024 | tf_op jit(solution)/shard_map/pallas_call | solution.py:264
  299.7 14.6 %shard_map.218 = (bf16[1536,768]{1,0:T(8,128)(2,1)}, bf16[384,768]{1,0:T(8,128)(2,1)}, bf16[384,768]{1,0:T(8,128)(2,1)}, bf16[384,768]{1,0:T(8,128)(2,1)}, bf16[384,768]{1,0:T(8,128)(2,1)}) custom-call(s32[1]{0:T(128)} %bitcast.8.pair_ref, bf16[8,320,1536]{2,1,0:T(8,128)(2,1)} %get-tuple-element.198.joined_ref, bf16[512,1536]{1,0:T(8,128)(2,1)} %bitcast.45, ...), custom_call_target="tpu_custom_call" | custom-call | flops 1024 | bytes 1024 | tf_op jit(solution)/shard_map/pallas_call | solution.py:452
  315.4 3.6 shard_map.219
  321.2 4.3 %shard_map.220 = bf16[1536,768]{1,0:T(8,128)(2,1)} custom-call(bf16[1536,768]{1,0:T(8,128)(2,1)} %get-tuple-element.258.first_ref, bf16[384,768]{1,0:T(8,128)(2,1)} %copy-done.26, bf16[384,768]{1,0:T(8,128)(2,1)} %copy-done.27, bf16[384,768]{1,0:T(8,128)(2,1)} %copy-done.28, bf16[384,768]{1,0:T(8,128)(2,1)} %copy-done.29), custom_call_target="tpu_custom_call" | custom-call | flops 1024 | bytes 1024 | tf_op jit(solution)/shard_map/pallas_call | solution.py:474
  330.4 3.1 shard_map.221
  333.5 16.5 %collective-permute-done.35.refs_1_ = bf16[1,320,1536]{2,1,0:T(8,128)(2,1)S(1)} collective-permute-done((bf16[1,320,1536]{2,1,0:T(8,128)(2,1)}, bf16[1,320,1536]{2,1,0:T(8,128)(2,1)S(1)}, u32[]{:S(2)}, u32[]{:S(2)}) %collective-permute-start.35) | collective-permute-done | bytes 983072 | tf_op jit(solution)/shard_map/ppermute | solution.py:37
  350.7 3.8 all-to-all-start.2
  354.5 8.8 %shard_map.222 = (f32[2,256,1536]{2,1,0:T(8,128)}, f32[2,64,1536]{2,1,0:T(8,128)}, f32[6,1536]{1,0:T(8,128)}) custom-call(f32[2,3,1536]{2,1,0:T(4,128)} %reshape.253.small_ref, f32[2,1536]{1,0:T(2,128)} %get-tuple-element.265.sums_two_ref, bf16[2,256,1536]{2,1,0:T(8,128)(2,1)} %media_ref.1, bf16[2,64,1536]{2,1,0:T(8,128)(2,1)} %latent_ref.3, ...), custom_call_target="tpu_custom_call" | custom-call | flops 1024 | bytes 1024 | tf_op jit(solution)/shard_map/pallas_call | solution.py:474
  365.7 2.8 collective-permute-start.41
  369.2 1.9 collective-permute-start.45
  371.1 1.5 collective-permute-start.46
  373.7 2.5 collective-permute-start.44
  376.2 3.6 collective-permute-done.44
  381.3 2.6 collective-permute-done.42
  384.0 4.9 %collective-permute-done.46 = bf16[2,64,1536]{2,1,0:T(8,128)(2,1)S(1)} collective-permute-done((bf16[2,64,1536]{2,1,0:T(8,128)(2,1)}, bf16[2,64,1536]{2,1,0:T(8,128)(2,1)S(1)}, u32[]{:S(2)}, u32[]{:S(2)}) %collective-permute-start.46) | collective-permute-done | bytes 393248 | tf_op jit(solution)/shard_map/ppermute | solution.py:37
  390.3 3.5 all-to-all-start.3
  393.9 2.8 shard_map.224
  397.2 2.1 multiply_convert_fusion
  399.3 4.9 %all-to-all-done.3.from_ref = bf16[8,48,768]{2,1,0:T(8,128)(2,1)S(1)} async-done(((bf16[8,48,768]{2,1,0:T(8,128)(2,1)}), bf16[8,48,768]{2,1,0:T(8,128)(2,1)S(1)}, u32[]{:S(2)}, u32[]{:S(2)}) %all-to-all-start.3) | async-done | bytes 589856 | tf_op jit(solution)/shard_map/all_to_all | solution.py:707
  405.1 2.1 shard_map.223
  (211 shorter events, 57.3 us)
Async XLA Ops:
  10.8 17.9 %all-to-all-start = ((bf16[8,64,768]{2,1,0:T(8,128)(2,1)}), bf16[8,64,768]{2,1,0:T(8,128)(2,1)S(1)}, u32[]{:S(2)}, u32[]{:S(2)}) async-start(bf16[8,64,768]{2,1,0:T(8,128)(2,1)} %shard_map.203), calls=%async_computation | async-start | bytes 1572864 | tf_op jit(solution)/shard_map/all_to_all | solution.py:584
  16.1 64.9 %all-gather.3.cloned.1.call-start = ((), (), s32[]{:S(2)}) async-start(), calls=%async_computation.6 | async-start | bytes 2949120 | tf_op jit(solution)/shard_map/all_gather | solution.py:585
  20.6 10.9 %copy-start.10 = (bf16[2,64,1536]{2,1,0:T(8,128)(2,1)S(1)}, bf16[2,64,1536]{2,1,0:T(8,128)(2,1)}, u32[]{:S(2)}) copy-start(bf16[2,64,1536]{2,1,0:T(8,128)(2,1)} %latent_ref.3) | copy-start | bytes 1179652
  29.0 6.9 %collective-permute-start = (f32[1,2304]{1,0:T(1,128)S(1)}, f32[1,2304]{1,0:T(1,128)}, u32[]{:S(2)}, u32[]{:S(2)}) collective-permute-start(f32[1,2304]{1,0:T(1,128)S(1)} %reshape.251), channel_id=1, source_target_pairs={{0,8},{8,0},{16,24},{24,16},{1,9},{9,1},{17,25},{25,17},{2,10},{10... | collective-permute-start | bytes 27656 | tf_op jit(solution)/shard_map/ppermute | solution.py:37
  32.3 20.3 %all-to-all-start.1 = ((bf16[8,48,1536]{2,1,0:T(8,128)(2,1)}), bf16[8,48,1536]{2,1,0:T(8,128)(2,1)S(1)}, u32[]{:S(2)}, u32[]{:S(2)}) async-start(bf16[8,48,1536]{2,1,0:T(8,128)(2,1)} %pad_maximum_fusion.1), calls=%async_computation.1 | async-start | bytes 2359296 | tf_op jit(solution)/shard_map/all_to_all | solution.py:595
  35.9 147.1 %all-gather.5.cloned.1.call-start = ((), (), s32[]{:S(2)}) async-start(), calls=%async_computation.7 | async-start | bytes 5898240 | tf_op jit(solution)/shard_map/all_gather | solution.py:615
  37.4 6.9 %collective-permute-start.1 = (f32[2,2304]{1,0:T(2,128)}, f32[2,2304]{1,0:T(2,128)}, u32[]{:S(2)}, u32[]{:S(2)}) collective-permute-start(f32[2,2304]{1,0:T(2,128)} %pad_maximum_fusion.5), channel_id=1, source_target_pairs={{0,16},{8,24},{16,0},{24,8},{1,17},{9,25},{17,1},{25,9},{2,18},{10... | collective-permute-start | bytes 55304 | tf_op jit(solution)/shard_map/ppermute | solution.py:37
  42.4 43.8 %copy-start.2 = (bf16[1,384,1536]{2,1,0:T(8,128)(2,1)}, bf16[1,384,1536]{2,1,0:T(8,128)(2,1)S(1)}, u32[]{:S(2)}) copy-start(bf16[1,384,1536]{2,1,0:T(8,128)(2,1)S(1)} %get-tuple-element.201.refs_0_) | copy-start | bytes 3538948
  52.7 28.4 %copy-start.8 = (bf16[8,48,1536]{2,1,0:T(8,128)(2,1)}, bf16[8,48,1536]{2,1,0:T(8,128)(2,1)S(1)}, u32[]{:S(2)}) copy-start(bf16[8,48,1536]{2,1,0:T(8,128)(2,1)S(1)} %all-to-all-done.1) | copy-start | bytes 3538948
  52.7 26.8 %collective-permute-start.2 = (bf16[1,384,1536]{2,1,0:T(8,128)(2,1)S(1)}, bf16[1,384,1536]{2,1,0:T(8,128)(2,1)S(1)}, u32[]{:S(2)}, u32[]{:S(2)}) collective-permute-start(bf16[1,384,1536]{2,1,0:T(8,128)(2,1)S(1)} %get-tuple-element.201.refs_0_), channel_id=1, source_target_pairs={{0,2},{1,3},{2,0},{3,1},{4,6},{5,7},{6,4},{7,5},{8,10},{9,11},{10,... | collective-permute-start | bytes 3538952 | tf_op jit(solution)/shard_map/ppermute | solution.py:37
  53.2 27.9 %collective-permute-start.3 = (bf16[1,384,1536]{2,1,0:T(8,128)(2,1)S(1)}, bf16[1,384,1536]{2,1,0:T(8,128)(2,1)}, u32[]{:S(2)}, u32[]{:S(2)}) collective-permute-start(bf16[1,384,1536]{2,1,0:T(8,128)(2,1)S(1)} %get-tuple-element.201.refs_0_), channel_id=1, source_target_pairs={{0,4},{1,5},{2,6},{3,7},{4,0},{5,1},{6,2},{7,3},{8,12},{9,13},{10,... | collective-permute-start | bytes 3538952 | tf_op jit(solution)/shard_map/ppermute | solution.py:37
  81.1 218.6 %reduce-scatter.3.cloned.1.call-start = ((), (), s32[]{:S(2)}) async-start(), calls=%async_computation.8 | async-start | bytes 5898240 | tf_op jit(solution)/shard_map/reduce_scatter | solution.py:662
  81.4 4.8 %collective-permute-start.4 = (bf16[1536,768]{1,0:T(8,128)(2,1)}, bf16[1536,768]{1,0:T(8,128)(2,1)S(1)}, u32[]{:S(2)}, u32[]{:S(2)}) collective-permute-start(bf16[1536,768]{1,0:T(8,128)(2,1)} %all-gather.3.cloned.1.call-done.mine_ref), channel_id=1, source_target_pairs={{0,1},{1,0},{2,3},{3,2},{4,5},{5,4},{6,7},{7,6},{8,9},{9,8},{10,11... | collective-permute-start | bytes 7077896 | tf_op jit(solution)/shard_map/ppermute | solution.py:37
  81.5 28.7 %collective-permute-start.7 = (bf16[1,384,1536]{2,1,0:T(8,128)(2,1)}, bf16[1,384,1536]{2,1,0:T(8,128)(2,1)}, u32[]{:S(2)}, u32[]{:S(2)}) collective-permute-start(bf16[1,384,1536]{2,1,0:T(8,128)(2,1)} %get-tuple-element.202.refs_1_), channel_id=1, source_target_pairs={{0,2},{1,3},{2,0},{3,1},{4,6},{5,7},{6,4},{7,5},{8,10},{9,11},{10,... | collective-permute-start | bytes 3538952 | tf_op jit(solution)/shard_map/ppermute | solution.py:37
  83.0 29.1 %collective-permute-start.8 = (bf16[1,384,1536]{2,1,0:T(8,128)(2,1)}, bf16[1,384,1536]{2,1,0:T(8,128)(2,1)}, u32[]{:S(2)}, u32[]{:S(2)}) collective-permute-start(bf16[1,384,1536]{2,1,0:T(8,128)(2,1)} %get-tuple-element.202.refs_1_), channel_id=1, source_target_pairs={{0,4},{1,5},{2,6},{3,7},{4,0},{5,1},{6,2},{7,3},{8,12},{9,13},{10,... | collective-permute-start | bytes 3538952 | tf_op jit(solution)/shard_map/ppermute | solution.py:37
  84.5 52.8 %collective-permute-start.9 = (bf16[1,384,1536]{2,1,0:T(8,128)(2,1)}, bf16[1,384,1536]{2,1,0:T(8,128)(2,1)S(1)}, u32[]{:S(2)}, u32[]{:S(2)}) collective-permute-start(bf16[1,384,1536]{2,1,0:T(8,128)(2,1)} %copy-done.5), channel_id=1, source_target_pairs={{0,4},{1,5},{2,6},{3,7},{4,0},{5,1},{6,2},{7,3},{8,12},{9,13},{10,... | collective-permute-start | bytes 3538952 | tf_op jit(solution)/shard_map/ppermute | solution.py:37
  112.1 29.1 %collective-permute-start.10 = (bf16[1,384,1536]{2,1,0:T(8,128)(2,1)}, bf16[1,384,1536]{2,1,0:T(8,128)(2,1)S(1)}, u32[]{:S(2)}, u32[]{:S(2)}) collective-permute-start(bf16[1,384,1536]{2,1,0:T(8,128)(2,1)} %collective-permute-done.8.refs_1_.refs_5_), channel_id=1, source_target_pairs={{0,2},{1,3},{2,0},{3,1},{4,6},{5,7},{6,4},{7,5},{8,10},{9,11},{10,... | collective-permute-start | bytes 3538952 | tf_op jit(solution)/shard_map/ppermute | solution.py:37
  112.7 39.4 %collective-permute-start.5 = (bf16[1,64,1536]{2,1,0:T(8,128)(2,1)}, bf16[1,64,1536]{2,1,0:T(8,128)(2,1)S(1)}, u32[]{:S(2)}, u32[]{:S(2)}) collective-permute-start(bf16[1,64,1536]{2,1,0:T(8,128)(2,1)} %get-tuple-element.177), channel_id=1, source_target_pairs={{0,2},{1,3},{2,0},{3,1},{4,6},{5,7},{6,4},{7,5},{8,10},{9,11},{10,... | collective-permute-start | bytes 589832 | tf_op jit(solution)/shard_map/ppermute | solution.py:37
  114.2 42.1 %collective-permute-start.6 = (bf16[1,64,1536]{2,1,0:T(8,128)(2,1)}, bf16[1,64,1536]{2,1,0:T(8,128)(2,1)S(1)}, u32[]{:S(2)}, u32[]{:S(2)}) collective-permute-start(bf16[1,64,1536]{2,1,0:T(8,128)(2,1)} %get-tuple-element.178), channel_id=1, source_target_pairs={{0,4},{1,5},{2,6},{3,7},{4,0},{5,1},{6,2},{7,3},{8,12},{9,13},{10,... | collective-permute-start | bytes 589832 | tf_op jit(solution)/shard_map/ppermute | solution.py:37
  124.4 31.8 %collective-permute-start.12 = (bf16[1,64,1536]{2,1,0:T(8,128)(2,1)}, bf16[1,64,1536]{2,1,0:T(8,128)(2,1)S(1)}, u32[]{:S(2)}, u32[]{:S(2)}) collective-permute-start(bf16[1,64,1536]{2,1,0:T(8,128)(2,1)} %get-tuple-element.194), channel_id=1, source_target_pairs={{0,2},{1,3},{2,0},{3,1},{4,6},{5,7},{6,4},{7,5},{8,10},{9,11},{10,... | collective-permute-start | bytes 589832 | tf_op jit(solution)/shard_map/ppermute | solution.py:37
  137.3 19.0 %collective-permute-start.13 = (bf16[1,64,1536]{2,1,0:T(8,128)(2,1)}, bf16[1,64,1536]{2,1,0:T(8,128)(2,1)S(1)}, u32[]{:S(2)}, u32[]{:S(2)}) collective-permute-start(bf16[1,64,1536]{2,1,0:T(8,128)(2,1)} %get-tuple-element.195), channel_id=1, source_target_pairs={{0,4},{1,5},{2,6},{3,7},{4,0},{5,1},{6,2},{7,3},{8,12},{9,13},{10,... | collective-permute-start | bytes 589832 | tf_op jit(solution)/shard_map/ppermute | solution.py:37
  150.6 6.8 %collective-permute-start.11 = (bf16[1,64,1536]{2,1,0:T(8,128)(2,1)}, bf16[1,64,1536]{2,1,0:T(8,128)(2,1)S(1)}, u32[]{:S(2)}, u32[]{:S(2)}) collective-permute-start(bf16[1,64,1536]{2,1,0:T(8,128)(2,1)} %get-tuple-element.192), channel_id=1, source_target_pairs={{0,6},{1,7},{2,4},{3,5},{4,2},{5,3},{6,0},{7,1},{8,14},{9,15},{10,... | collective-permute-start | bytes 589832 | tf_op jit(solution)/shard_map/ppermute | solution.py:37
  152.1 7.4 %collective-permute-start.14 = (bf16[1,64,1536]{2,1,0:T(8,128)(2,1)}, bf16[1,64,1536]{2,1,0:T(8,128)(2,1)S(1)}, u32[]{:S(2)}, u32[]{:S(2)}) collective-permute-start(bf16[1,64,1536]{2,1,0:T(8,128)(2,1)} %get-tuple-element.196), channel_id=1, source_target_pairs={{0,6},{1,7},{2,4},{3,5},{4,2},{5,3},{6,0},{7,1},{8,14},{9,15},{10,... | collective-permute-start | bytes 589832 | tf_op jit(solution)/shard_map/ppermute | solution.py:37
  156.3 10.2 %copy-start.4 = (bf16[512,1536]{1,0:T(8,128)(2,1)S(1)}, bf16[512,1536]{1,0:T(8,128)(2,1)}, u32[]{:S(2)}) copy-start(bf16[512,1536]{1,0:T(8,128)(2,1)} %shard_map.209.cot_ref) | copy-start | bytes 4718596
  163.0 10.7 %collective-permute-start.16 = (bf16[2,64,1536]{2,1,0:T(8,128)(2,1)}, bf16[2,64,1536]{2,1,0:T(8,128)(2,1)S(1)}, u32[]{:S(2)}, u32[]{:S(2)}) collective-permute-start(bf16[2,64,1536]{2,1,0:T(8,128)(2,1)} %get-tuple-element.211), channel_id=1, source_target_pairs={{0,2},{1,3},{2,0},{3,1},{4,6},{5,7},{6,4},{7,5},{8,10},{9,11},{10,... | collective-permute-start | bytes 1179656 | tf_op jit(solution)/shard_map/ppermute | solution.py:37
  163.8 10.1 %collective-permute-start.17 = (bf16[2,64,1536]{2,1,0:T(8,128)(2,1)}, bf16[2,64,1536]{2,1,0:T(8,128)(2,1)S(1)}, u32[]{:S(2)}, u32[]{:S(2)}) collective-permute-start(bf16[2,64,1536]{2,1,0:T(8,128)(2,1)} %get-tuple-element.211), channel_id=1, source_target_pairs={{0,4},{1,5},{2,6},{3,7},{4,0},{5,1},{6,2},{7,3},{8,12},{9,13},{10,... | collective-permute-start | bytes 1179656 | tf_op jit(solution)/shard_map/ppermute | solution.py:37
  165.0 13.1 %collective-permute-start.18 = (bf16[2,64,1536]{2,1,0:T(8,128)(2,1)}, bf16[2,64,1536]{2,1,0:T(8,128)(2,1)S(1)}, u32[]{:S(2)}, u32[]{:S(2)}) collective-permute-start(bf16[2,64,1536]{2,1,0:T(8,128)(2,1)} %get-tuple-element.211), channel_id=1, source_target_pairs={{0,6},{1,7},{2,4},{3,5},{4,2},{5,3},{6,0},{7,1},{8,14},{9,15},{10,... | collective-permute-start | bytes 1179656 | tf_op jit(solution)/shard_map/ppermute | solution.py:37
  166.5 13.0 %collective-permute-start.15 = (bf16[512,1536]{1,0:T(8,128)(2,1)S(1)}, bf16[512,1536]{1,0:T(8,128)(2,1)S(1)}, u32[]{:S(2)}, u32[]{:S(2)}) collective-permute-start(bf16[512,1536]{1,0:T(8,128)(2,1)S(1)} %copy-done.4), channel_id=1, source_target_pairs={{0,1},{1,0},{2,3},{3,2},{4,5},{5,4},{6,7},{7,6},{8,9},{9,8},{10,11... | collective-permute-start | bytes 4718600 | tf_op jit(solution)/shard_map/ppermute | solution.py:37
  179.4 3.6 collective-permute-start.19
  207.4 182.9 %reduce-scatter.5.cloned.1.call-start = ((), (), s32[]{:S(2)}) async-start(), calls=%async_computation.9 | async-start | bytes 2949120 | tf_op jit(solution)/shard_map/reduce_scatter | solution.py:702
  208.8 3.4 collective-permute-start.20
  216.4 12.2 %collective-permute-start.21 = (bf16[2,64,1536]{2,1,0:T(8,128)(2,1)}, bf16[2,64,1536]{2,1,0:T(8,128)(2,1)S(1)}, u32[]{:S(2)}, u32[]{:S(2)}) collective-permute-start(bf16[2,64,1536]{2,1,0:T(8,128)(2,1)} %bitcast.71), channel_id=1, source_target_pairs={{0,2},{1,3},{2,0},{3,1},{4,6},{5,7},{6,4},{7,5},{8,10},{9,11},{10,... | collective-permute-start | bytes 1179656 | tf_op jit(solution)/shard_map/ppermute | solution.py:37
  218.1 19.5 %collective-permute-start.22 = (bf16[2,64,1536]{2,1,0:T(8,128)(2,1)}, bf16[2,64,1536]{2,1,0:T(8,128)(2,1)S(1)}, u32[]{:S(2)}, u32[]{:S(2)}) collective-permute-start(bf16[2,64,1536]{2,1,0:T(8,128)(2,1)} %bitcast.70), channel_id=1, source_target_pairs={{0,4},{1,5},{2,6},{3,7},{4,0},{5,1},{6,2},{7,3},{8,12},{9,13},{10,... | collective-permute-start | bytes 1179656 | tf_op jit(solution)/shard_map/ppermute | solution.py:37
  219.2 18.4 %collective-permute-start.23 = (bf16[2,64,1536]{2,1,0:T(8,128)(2,1)}, bf16[2,64,1536]{2,1,0:T(8,128)(2,1)S(1)}, u32[]{:S(2)}, u32[]{:S(2)}) collective-permute-start(bf16[2,64,1536]{2,1,0:T(8,128)(2,1)} %bitcast.69), channel_id=1, source_target_pairs={{0,6},{1,7},{2,4},{3,5},{4,2},{5,3},{6,0},{7,1},{8,14},{9,15},{10,... | collective-permute-start | bytes 1179656 | tf_op jit(solution)/shard_map/ppermute | solution.py:37
  242.1 19.6 %copy-start.32 = (bf16[2,64,1536]{2,1,0:T(8,128)(2,1)S(1)}, bf16[2,64,1536]{2,1,0:T(8,128)(2,1)}, u32[]{:S(2)}) copy-start(bf16[2,64,1536]{2,1,0:T(8,128)(2,1)} %get-tuple-element.233) | copy-start | bytes 1179652
  242.1 12.3 %collective-permute-start.24 = (bf16[2,64,1536]{2,1,0:T(8,128)(2,1)}, bf16[2,64,1536]{2,1,0:T(8,128)(2,1)S(1)}, u32[]{:S(2)}, u32[]{:S(2)}) collective-permute-start(bf16[2,64,1536]{2,1,0:T(8,128)(2,1)} %get-tuple-element.233), channel_id=1, source_target_pairs={{0,2},{1,3},{2,0},{3,1},{4,6},{5,7},{6,4},{7,5},{8,10},{9,11},{10,... | collective-permute-start | bytes 1179656 | tf_op jit(solution)/shard_map/ppermute | solution.py:37
  242.9 18.8 %collective-permute-start.25 = (bf16[2,64,1536]{2,1,0:T(8,128)(2,1)}, bf16[2,64,1536]{2,1,0:T(8,128)(2,1)S(1)}, u32[]{:S(2)}, u32[]{:S(2)}) collective-permute-start(bf16[2,64,1536]{2,1,0:T(8,128)(2,1)} %get-tuple-element.233), channel_id=1, source_target_pairs={{0,4},{1,5},{2,6},{3,7},{4,0},{5,1},{6,2},{7,3},{8,12},{9,13},{10,... | collective-permute-start | bytes 1179656 | tf_op jit(solution)/shard_map/ppermute | solution.py:37
  244.2 17.5 %collective-permute-start.26 = (bf16[2,64,1536]{2,1,0:T(8,128)(2,1)}, bf16[2,64,1536]{2,1,0:T(8,128)(2,1)S(1)}, u32[]{:S(2)}, u32[]{:S(2)}) collective-permute-start(bf16[2,64,1536]{2,1,0:T(8,128)(2,1)} %get-tuple-element.233), channel_id=1, source_target_pairs={{0,6},{1,7},{2,4},{3,5},{4,2},{5,3},{6,0},{7,1},{8,14},{9,15},{10,... | collective-permute-start | bytes 1179656 | tf_op jit(solution)/shard_map/ppermute | solution.py:37
  271.9 27.7 %collective-permute-start.27 = (bf16[1,320,1536]{2,1,0:T(8,128)(2,1)}, bf16[1,320,1536]{2,1,0:T(8,128)(2,1)S(1)}, u32[]{:S(2)}, u32[]{:S(2)}) collective-permute-start(bf16[1,320,1536]{2,1,0:T(8,128)(2,1)} %get-tuple-element.244), channel_id=1, source_target_pairs={{0,4},{1,5},{2,6},{3,7},{4,0},{5,1},{6,2},{7,3},{8,12},{9,13},{10,... | collective-permute-start | bytes 2949128 | tf_op jit(solution)/shard_map/ppermute | solution.py:37
  272.8 26.8 %collective-permute-start.28 = (bf16[1,320,1536]{2,1,0:T(8,128)(2,1)}, bf16[1,320,1536]{2,1,0:T(8,128)(2,1)}, u32[]{:S(2)}, u32[]{:S(2)}) collective-permute-start(bf16[1,320,1536]{2,1,0:T(8,128)(2,1)} %get-tuple-element.245), channel_id=1, source_target_pairs={{0,2},{1,3},{2,0},{3,1},{4,6},{5,7},{6,4},{7,5},{8,10},{9,11},{10,... | collective-permute-start | bytes 2949128 | tf_op jit(solution)/shard_map/ppermute | solution.py:37
  288.4 26.6 %collective-permute-start.29 = (bf16[1,320,1536]{2,1,0:T(8,128)(2,1)}, bf16[1,320,1536]{2,1,0:T(8,128)(2,1)S(1)}, u32[]{:S(2)}, u32[]{:S(2)}) collective-permute-start(bf16[1,320,1536]{2,1,0:T(8,128)(2,1)} %get-tuple-element.250), channel_id=1, source_target_pairs={{0,4},{1,5},{2,6},{3,7},{4,0},{5,1},{6,2},{7,3},{8,12},{9,13},{10,... | collective-permute-start | bytes 2949128 | tf_op jit(solution)/shard_map/ppermute | solution.py:37
  289.6 29.4 %collective-permute-start.30 = (bf16[1,320,1536]{2,1,0:T(8,128)(2,1)}, bf16[1,320,1536]{2,1,0:T(8,128)(2,1)S(1)}, u32[]{:S(2)}, u32[]{:S(2)}) collective-permute-start(bf16[1,320,1536]{2,1,0:T(8,128)(2,1)} %get-tuple-element.251), channel_id=1, source_target_pairs={{0,2},{1,3},{2,0},{3,1},{4,6},{5,7},{6,4},{7,5},{8,10},{9,11},{10,... | collective-permute-start | bytes 2949128 | tf_op jit(solution)/shard_map/ppermute | solution.py:37
  299.6 14.7 %copy-start.25 = (bf16[1,320,1536]{2,1,0:T(8,128)(2,1)}, bf16[1,320,1536]{2,1,0:T(8,128)(2,1)S(1)}, u32[]{:S(2)}) copy-start(bf16[1,320,1536]{2,1,0:T(8,128)(2,1)S(1)} %collective-permute-done.27.refs_1_) | copy-start | bytes 2949124
  314.3 4.7 %collective-permute-start.31 = (bf16[384,768]{1,0:T(8,128)(2,1)}, bf16[384,768]{1,0:T(8,128)(2,1)S(1)}, u32[]{:S(2)}, u32[]{:S(2)}) collective-permute-start(bf16[384,768]{1,0:T(8,128)(2,1)} %get-tuple-element.259), channel_id=1, source_target_pairs={{0,1},{1,0},{2,3},{3,2},{4,5},{5,4},{6,7},{7,6},{8,9},{9,8},{10,11... | collective-permute-start | bytes 1769480 | tf_op jit(solution)/shard_map/ppermute | solution.py:37
  314.4 4.7 %collective-permute-start.32 = (bf16[384,768]{1,0:T(8,128)(2,1)}, bf16[384,768]{1,0:T(8,128)(2,1)S(1)}, u32[]{:S(2)}, u32[]{:S(2)}) collective-permute-start(bf16[384,768]{1,0:T(8,128)(2,1)} %get-tuple-element.260), channel_id=1, source_target_pairs={{0,1},{1,0},{2,3},{3,2},{4,5},{5,4},{6,7},{7,6},{8,9},{9,8},{10,11... | collective-permute-start | bytes 1769480 | tf_op jit(solution)/shard_map/ppermute | solution.py:37
  314.9 4.2 %collective-permute-start.33 = (bf16[384,768]{1,0:T(8,128)(2,1)}, bf16[384,768]{1,0:T(8,128)(2,1)S(1)}, u32[]{:S(2)}, u32[]{:S(2)}) collective-permute-start(bf16[384,768]{1,0:T(8,128)(2,1)} %get-tuple-element.261), channel_id=1, source_target_pairs={{0,1},{1,0},{2,3},{3,2},{4,5},{5,4},{6,7},{7,6},{8,9},{9,8},{10,11... | collective-permute-start | bytes 1769480 | tf_op jit(solution)/shard_map/ppermute | solution.py:37
  315.0 4.2 %collective-permute-start.34 = (bf16[384,768]{1,0:T(8,128)(2,1)}, bf16[384,768]{1,0:T(8,128)(2,1)S(1)}, u32[]{:S(2)}, u32[]{:S(2)}) collective-permute-start(bf16[384,768]{1,0:T(8,128)(2,1)} %get-tuple-element.262), channel_id=1, source_target_pairs={{0,1},{1,0},{2,3},{3,2},{4,5},{5,4},{6,7},{7,6},{8,9},{9,8},{10,11... | collective-permute-start | bytes 1769480 | tf_op jit(solution)/shard_map/ppermute | solution.py:37
  325.6 3.7 collective-permute-start.37
  326.0 24.0 %collective-permute-start.35 = (bf16[1,320,1536]{2,1,0:T(8,128)(2,1)}, bf16[1,320,1536]{2,1,0:T(8,128)(2,1)S(1)}, u32[]{:S(2)}, u32[]{:S(2)}) collective-permute-start(bf16[1,320,1536]{2,1,0:T(8,128)(2,1)} %get-tuple-element.268), channel_id=1, source_target_pairs={{0,2},{1,3},{2,0},{3,1},{4,6},{5,7},{6,4},{7,5},{8,10},{9,11},{10,... | collective-permute-start | bytes 2949128 | tf_op jit(solution)/shard_map/ppermute | solution.py:37
  326.9 23.7 %collective-permute-start.36 = (bf16[1,320,1536]{2,1,0:T(8,128)(2,1)}, bf16[1,320,1536]{2,1,0:T(8,128)(2,1)S(1)}, u32[]{:S(2)}, u32[]{:S(2)}) collective-permute-start(bf16[1,320,1536]{2,1,0:T(8,128)(2,1)} %get-tuple-element.272), channel_id=1, source_target_pairs={{0,4},{1,5},{2,6},{3,7},{4,0},{5,1},{6,2},{7,3},{8,12},{9,13},{10,... | collective-permute-start | bytes 2949128 | tf_op jit(solution)/shard_map/ppermute | solution.py:37
  350.7 39.6 %all-to-all-start.2 = ((bf16[8,48,1536]{2,1,0:T(8,128)(2,1)}), bf16[8,48,1536]{2,1,0:T(8,128)(2,1)S(1)}, u32[]{:S(2)}, u32[]{:S(2)}) async-start(bf16[8,48,1536]{2,1,0:T(8,128)(2,1)} %bitcast.22), calls=%async_computation.4 | async-start | bytes 2359296 | tf_op jit(solution)/shard_map/all_to_all | solution.py:707
  363.3 33.9 %copy-start.12 = (f32[2,64,1536]{2,1,0:T(8,128)S(1)}, f32[2,64,1536]{2,1,0:T(8,128)}, u32[]{:S(2)}) copy-start(f32[2,64,1536]{2,1,0:T(8,128)} %get-tuple-element.197.attended_ref) | copy-start | bytes 2359300
  363.3 33.9 %copy-start.34 = (bf16[128,1536]{1,0:T(8,128)(2,1)S(1)}, bf16[128,1536]{1,0:T(8,128)(2,1)}, u32[]{:S(2)}) copy-start(bf16[128,1536]{1,0:T(8,128)(2,1)} %get-tuple-element.288) | copy-start | bytes 1179652
  363.3 1.5 collective-permute-start.38
  365.7 6.9 %collective-permute-start.41 = (f32[6,1536]{1,0:T(8,128)S(1)}, f32[6,1536]{1,0:T(8,128)S(1)}, u32[]{:S(2)}, u32[]{:S(2)}) collective-permute-start(f32[6,1536]{1,0:T(8,128)S(1)} %add.50), channel_id=1, source_target_pairs={{0,6},{1,7},{2,4},{3,5},{4,2},{5,3},{6,0},{7,1},{8,14},{9,15},{10,... | collective-permute-start | bytes 110600 | tf_op jit(solution)/shard_map/ppermute | solution.py:37
  368.5 5.2 %collective-permute-start.40 = (f32[6,1536]{1,0:T(8,128)S(1)}, f32[6,1536]{1,0:T(8,128)S(1)}, u32[]{:S(2)}, u32[]{:S(2)}) collective-permute-start(f32[6,1536]{1,0:T(8,128)S(1)} %add.50), channel_id=1, source_target_pairs={{0,4},{1,5},{2,6},{3,7},{4,0},{5,1},{6,2},{7,3},{8,12},{9,13},{10,... | collective-permute-start | bytes 110600 | tf_op jit(solution)/shard_map/ppermute | solution.py:37
  369.0 4.7 %collective-permute-start.39 = (f32[6,1536]{1,0:T(8,128)S(1)}, f32[6,1536]{1,0:T(8,128)S(1)}, u32[]{:S(2)}, u32[]{:S(2)}) collective-permute-start(f32[6,1536]{1,0:T(8,128)S(1)} %add.50), channel_id=1, source_target_pairs={{0,2},{1,3},{2,0},{3,1},{4,6},{5,7},{6,4},{7,5},{8,10},{9,11},{10,... | collective-permute-start | bytes 110600 | tf_op jit(solution)/shard_map/ppermute | solution.py:37
  369.2 14.8 %collective-permute-start.45 = (bf16[2,64,1536]{2,1,0:T(8,128)(2,1)}, bf16[2,64,1536]{2,1,0:T(8,128)(2,1)S(1)}, u32[]{:S(2)}, u32[]{:S(2)}) collective-permute-start(bf16[2,64,1536]{2,1,0:T(8,128)(2,1)} %bitcast.24), channel_id=1, source_target_pairs={{0,2},{1,3},{2,0},{3,1},{4,6},{5,7},{6,4},{7,5},{8,10},{9,11},{10,... | collective-permute-start | bytes 1179656 | tf_op jit(solution)/shard_map/ppermute | solution.py:37
  371.1 17.8 %collective-permute-start.46 = (bf16[2,64,1536]{2,1,0:T(8,128)(2,1)}, bf16[2,64,1536]{2,1,0:T(8,128)(2,1)S(1)}, u32[]{:S(2)}, u32[]{:S(2)}) collective-permute-start(bf16[2,64,1536]{2,1,0:T(8,128)(2,1)} %bitcast.25), channel_id=1, source_target_pairs={{0,4},{1,5},{2,6},{3,7},{4,0},{5,1},{6,2},{7,3},{8,12},{9,13},{10,... | collective-permute-start | bytes 1179656 | tf_op jit(solution)/shard_map/ppermute | solution.py:37
  372.5 17.7 %collective-permute-start.47 = (bf16[2,64,1536]{2,1,0:T(8,128)(2,1)}, bf16[2,64,1536]{2,1,0:T(8,128)(2,1)}, u32[]{:S(2)}, u32[]{:S(2)}) collective-permute-start(bf16[2,64,1536]{2,1,0:T(8,128)(2,1)} %bitcast.26), channel_id=1, source_target_pairs={{0,6},{1,7},{2,4},{3,5},{4,2},{5,3},{6,0},{7,1},{8,14},{9,15},{10,... | collective-permute-start | bytes 1179656 | tf_op jit(solution)/shard_map/ppermute | solution.py:37
  373.7 6.1 %collective-permute-start.44 = (f32[6,1536]{1,0:T(8,128)S(1)}, f32[6,1536]{1,0:T(8,128)S(1)}, u32[]{:S(2)}, u32[]{:S(2)}) collective-permute-start(f32[6,1536]{1,0:T(8,128)S(1)} %add_add_fusion), channel_id=1, source_target_pairs={{0,24},{8,16},{16,8},{24,0},{1,25},{9,17},{17,9},{25,1},{2,26},{10... | collective-permute-start | bytes 110600 | tf_op jit(solution)/shard_map/ppermute | solution.py:37
  376.2 5.1 %collective-permute-start.43 = (f32[6,1536]{1,0:T(8,128)S(1)}, f32[6,1536]{1,0:T(8,128)S(1)}, u32[]{:S(2)}, u32[]{:S(2)}) collective-permute-start(f32[6,1536]{1,0:T(8,128)S(1)} %add_add_fusion), channel_id=1, source_target_pairs={{0,16},{8,24},{16,0},{24,8},{1,17},{9,25},{17,1},{25,9},{2,18},{10... | collective-permute-start | bytes 110600 | tf_op jit(solution)/shard_map/ppermute | solution.py:37
  379.8 4.1 collective-permute-start.42
  390.3 13.9 %all-to-all-start.3 = ((bf16[8,48,768]{2,1,0:T(8,128)(2,1)}), bf16[8,48,768]{2,1,0:T(8,128)(2,1)S(1)}, u32[]{:S(2)}, u32[]{:S(2)}) async-start(bf16[8,48,768]{2,1,0:T(8,128)(2,1)} %bitcast.56), calls=%async_computation.5 | async-start | bytes 1179648 | tf_op jit(solution)/shard_map/all_to_all | solution.py:707
  (40 other events, 119.1 us)
Sparse Core Ops, SparseCore 0:
  31.7 49.2 all-gather.2
  82.5 88.4 all-gather.4
  207.5 84.2 reduce-scatter.2
  325.7 46.7 reduce-scatter.4
